TPU v7x, 512 devices: a whole 4x8x8 slice. The times are simulated.
512 devices in a mesh: ctx: 64 (over z_hi, y, core), head: 8 (over x, z_lo).
Axes of the slice: x: 4, y: 8, z: 8 (z_hi: 4, z_lo: 2; z = z_hi * 2 + z_lo), core: 2. Of those that a mesh axis runs over, the one named last changes fastest.
Arguments:
- queries: bfloat16 [16384, 2048], P('ctx', 'head'), may hold values from -16.25 to 16.25
- keys: bfloat16 [16384, 256], P('ctx'), may hold values from -6 to 6
- values: bfloat16 [16384, 256], P('ctx'), may hold values from -48 to 48
Outputs:
- attn_out: bfloat16 [16384, 2048], P('ctx', 'head')
- hessian: float32 [2048, 2048], P('ctx', 'head')
All inputs are finite; a program needn't handle non-finite values.
Results may differ from a plain program's by a relative error of at most 0.006.
Values may be sent and summed in bfloat16 or wider, within the bound.
No kernel may reach another device: no remote copies, remote signals or barrier semaphores. Data moves between devices by JAX's collectives and lax.ppermute only.
A program may use at most 128 MiB of HBM per device.

v0:
```python
import math

import jax
import jax.numpy as jnp
from jax import lax
from jax.sharding import PartitionSpec as P

HEADS = 16
KVG = 2
HD = 128


def from_behind(value, axis, by):
    count = lax.axis_size(axis)
    pairs = [(i, i + by) for i in range(count) if 0 <= i + by < count]
    return lax.ppermute(value, axis, pairs)


def attend_block(state, q_rows, q_pos, k_block, v_block, k_start):
    last_pos = jnp.max(q_pos)

    def update(inner):
        run_max, run_sum, run_acc = inner
        scores = jnp.einsum(
            "rd,kd->rk", q_rows, k_block, preferred_element_type=jnp.float32
        ) / math.sqrt(HD)
        k_pos = k_start + jnp.arange(k_block.shape[0], dtype=jnp.int32)
        scores = jnp.where(k_pos[None, :] <= q_pos[:, None], scores, -jnp.inf)
        new_max = jnp.maximum(run_max, jnp.max(scores, axis=1))
        factor = jnp.exp(run_max - new_max)
        weights = jnp.exp(scores - new_max[:, None])
        run_sum = run_sum * factor + jnp.sum(weights, axis=1)
        run_acc = run_acc * factor[:, None] + jnp.dot(
            weights.astype(jnp.bfloat16), v_block, preferred_element_type=jnp.float32
        )
        return (new_max, run_sum, run_acc)

    live = jnp.logical_and(k_start <= last_pos, k_start >= 0)
    return lax.cond(live, update, lambda inner: inner, state)


def attend_all(states, segments, stacked, k_start):
    return tuple(
        (
            attend_block(state, seg[0], seg[1], stacked[0], stacked[1], k_start)
            for state, seg in zip(states, segments)
        )
    )


def local(queries, keys, values):
    ctx_count = lax.axis_size("ctx")
    ctx_pos = lax.axis_index("ctx")
    head_pos = lax.axis_index("head")
    tok_here = queries.shape[0]
    heads_here = queries.shape[1] // HD
    group = head_pos * heads_here // (HEADS // KVG)
    own_keys = lax.dynamic_slice_in_dim(keys, group * HD, HD, 1)
    own_values = lax.dynamic_slice_in_dim(values, group * HD, HD, 1)
    stacked = jnp.stack([own_keys, own_values])
    grid = queries.reshape(tok_here, heads_here, HD)
    local_pos = jnp.arange(tok_here, dtype=jnp.int32)
    pieces = ((grid, ctx_pos * tok_here + local_pos),)
    segments = tuple(((rows.reshape(-1, HD), jnp.repeat(pos, heads_here)) for rows, pos in pieces))
    states = tuple(
        (
            (
                jnp.full((seg[0].shape[0],), -1e30, jnp.float32),
                jnp.zeros((seg[0].shape[0],), jnp.float32),
                jnp.zeros((seg[0].shape[0], HD), jnp.float32),
            )
            for seg in segments
        )
    )
    states = attend_all(states, segments, stacked, ctx_pos * tok_here)

    def chain_step(step, carry):
        inner, moving = carry
        moving = from_behind(moving, "ctx", 1)
        inner = attend_all(inner, segments, moving, (ctx_pos - step) * tok_here)
        return (inner, moving)

    states, moving = lax.fori_loop(1, ctx_count, chain_step, (states, stacked))
    blocks = [
        (state[2] / state[1][:, None]).astype(jnp.bfloat16).reshape(-1, heads_here * HD)
        for state in states
    ]
    attn_out = blocks[0]
    x_all = lax.all_gather(attn_out, "head", axis=1, tiled=True)
    hessian = lax.psum_scatter(
        lax.dot_general(
            x_all, attn_out, (((0,), (0,)), ((), ())), preferred_element_type=jnp.float32
        ),
        "ctx",
        scatter_dimension=0,
        tiled=True,
    )
    hessian = hessian * (2.0 / (tok_here * ctx_count))
    return (attn_out, hessian)


def solution(mesh):
    in_specs = (P("ctx", "head"), P("ctx", None), P("ctx", None))
    out_specs = (P("ctx", "head"), P("ctx", "head"))
    return jax.shard_map(local, mesh=mesh, in_specs=in_specs, out_specs=out_specs, check_vma=False)
```

profile of v0, /device:TPU:1, one launch (start us, length us, event | category | flops | bytes accessed | tf_op | source)
XLA Modules:
  0.0 1043.0 jit_solution(5286510482378696232)
XLA Ops:
  14.1 596.2 %while.22 = (s32[]{:T(128)}, f32[512]{0:T(512)}, f32[512]{0:T(512)S(1)}, f32[512,128]{1,0:T(8,128)S(1)}, bf16[2,256,128]{2,1,0:T(8,128)(2,1)S(1)}, /*index=5*/s3...) while((s32[]{:T(128)}, f32[512]{0:T(512)}, ...), condition=%wide.region_10.11_spmd.clone, body=%wide.region_5.10_spmd.clone.sunk | while | flops 68289800 | bytes 3190083 | solution.py:83
  29.9 7.3 collective-permute-start
  84.9 7.9 collective-permute-start
  102.3 8.5 collective-permute-start
  120.3 8.5 collective-permute-start
  183.4 8.2 collective-permute-start
  193.6 7.4 collective-permute-start
  202.9 10.3 collective-permute-start
  215.1 7.4 collective-permute-start
  224.4 10.3 collective-permute-start
  236.7 7.4 collective-permute-start
  246.0 10.3 collective-permute-start
  258.2 7.4 collective-permute-start
  267.6 10.3 collective-permute-start
  279.8 7.4 collective-permute-start
  289.1 7.4 collective-permute-start
  298.4 7.4 collective-permute-start
  307.8 7.4 collective-permute-start
  317.1 7.4 collective-permute-start
  326.4 7.4 collective-permute-start
  335.7 7.4 collective-permute-start
  345.1 7.4 collective-permute-start
  354.4 7.4 collective-permute-start
  363.7 7.4 collective-permute-start
  373.0 7.4 collective-permute-start
  382.4 7.4 collective-permute-start
  391.7 7.4 collective-permute-start
  401.0 7.4 collective-permute-start
  410.3 7.4 collective-permute-start
  419.7 7.4 collective-permute-start
  429.0 7.4 collective-permute-start
  438.3 7.4 collective-permute-start
  447.6 7.4 collective-permute-start
  457.0 7.4 collective-permute-start
  466.3 7.4 collective-permute-start
  475.6 7.4 collective-permute-start
  484.9 7.4 collective-permute-start
  494.3 11.1 %collective-permute-start = (bf16[2,256,128]{2,1,0:T(8,128)(2,1)S(1)}, bf16[2,256,128]{2,1,0:T(8,128)(2,1)S(1)}, u32[]{:S(2)}, u32[]{:S(2)}) collective-permute-start(bf16[2,256,128]{2,1,0:T(8,128)(2,1)S(1)} %get-tuple-element.427), channel_id=1, source_target_pairs={{0,8},{8,16},{16,24},{24,32},{32,40},{40,48},{48,56},{56,64},{64,7... | collective-permute-start | bytes 393224 | tf_op jit(solution)/shard_map/while/body/eval_jaxpr/ppermute | solution.py:16
  507.3 9.1 collective-permute-start
  518.4 12.0 %collective-permute-start = (bf16[2,256,128]{2,1,0:T(8,128)(2,1)S(1)}, bf16[2,256,128]{2,1,0:T(8,128)(2,1)S(1)}, u32[]{:S(2)}, u32[]{:S(2)}) collective-permute-start(bf16[2,256,128]{2,1,0:T(8,128)(2,1)S(1)} %get-tuple-element.427), channel_id=1, source_target_pairs={{0,8},{8,16},{16,24},{24,32},{32,40},{40,48},{48,56},{56,64},{64,7... | collective-permute-start | bytes 393224 | tf_op jit(solution)/shard_map/while/body/eval_jaxpr/ppermute | solution.py:16
  532.4 9.9 collective-permute-start
  544.2 12.7 %collective-permute-start = (bf16[2,256,128]{2,1,0:T(8,128)(2,1)S(1)}, bf16[2,256,128]{2,1,0:T(8,128)(2,1)S(1)}, u32[]{:S(2)}, u32[]{:S(2)}) collective-permute-start(bf16[2,256,128]{2,1,0:T(8,128)(2,1)S(1)} %get-tuple-element.427), channel_id=1, source_target_pairs={{0,8},{8,16},{16,24},{24,32},{32,40},{40,48},{48,56},{56,64},{64,7... | collective-permute-start | bytes 393224 | tf_op jit(solution)/shard_map/while/body/eval_jaxpr/ppermute | solution.py:16
  558.9 9.6 collective-permute-start
  570.4 12.5 %collective-permute-start = (bf16[2,256,128]{2,1,0:T(8,128)(2,1)S(1)}, bf16[2,256,128]{2,1,0:T(8,128)(2,1)S(1)}, u32[]{:S(2)}, u32[]{:S(2)}) collective-permute-start(bf16[2,256,128]{2,1,0:T(8,128)(2,1)S(1)} %get-tuple-element.427), channel_id=1, source_target_pairs={{0,8},{8,16},{16,24},{24,32},{32,40},{40,48},{48,56},{56,64},{64,7... | collective-permute-start | bytes 393224 | tf_op jit(solution)/shard_map/while/body/eval_jaxpr/ppermute | solution.py:16
  584.9 9.3 collective-permute-start
  596.2 12.2 %collective-permute-start = (bf16[2,256,128]{2,1,0:T(8,128)(2,1)S(1)}, bf16[2,256,128]{2,1,0:T(8,128)(2,1)S(1)}, u32[]{:S(2)}, u32[]{:S(2)}) collective-permute-start(bf16[2,256,128]{2,1,0:T(8,128)(2,1)S(1)} %get-tuple-element.427), channel_id=1, source_target_pairs={{0,8},{8,16},{16,24},{24,32},{32,40},{40,48},{48,56},{56,64},{64,7... | collective-permute-start | bytes 393224 | tf_op jit(solution)/shard_map/while/body/eval_jaxpr/ppermute | solution.py:16
  611.2 266.9 %all-gather.2.cloned.1.call-done = bf16[256,2048]{1,0:T(8,128)(2,1)} async-done(((bf16[256,256]{1,0:T(8,128)(2,1)}), bf16[256,2048]{1,0:T(8,128)(2,1)}) %all-gather.2.cloned.1.call-update) | async-done | bytes 1048592 | tf_op jit(solution)/shard_map/all_gather | solution.py:89
  881.3 153.5 %reduce-scatter.2.cloned.1.call-done = f32[32,256]{1,0:T(8,128)} async-done(((f32[2048,256]{1,0:T(8,128)}), f32[32,256]{1,0:T(8,128)}) %reduce-scatter.2.cloned.1.call-update) | async-done | bytes 32784 | tf_op jit(solution)/shard_map/reduce_scatter | solution.py:90
  (238 shorter events, 193.2 us)
Async XLA Ops:
  7.2 871.0 %all-gather.2.cloned.1.call-start = ((), (), s32[]{:S(2)}) async-start(), calls=%async_computation.1 | async-start | bytes 1179648 | tf_op jit(solution)/shard_map/all_gather | solution.py:89
  14.1 9.0 collective-permute-start
  29.9 9.2 collective-permute-start
  84.9 9.8 collective-permute-start
  102.3 10.4 collective-permute-start
  120.3 10.4 collective-permute-start
  183.4 10.2 collective-permute-start
  193.6 9.3 collective-permute-start
  202.9 12.2 %collective-permute-start = (bf16[2,256,128]{2,1,0:T(8,128)(2,1)S(1)}, bf16[2,256,128]{2,1,0:T(8,128)(2,1)S(1)}, u32[]{:S(2)}, u32[]{:S(2)}) collective-permute-start(bf16[2,256,128]{2,1,0:T(8,128)(2,1)S(1)} %get-tuple-element.427), channel_id=1, source_target_pairs={{0,8},{8,16},{16,24},{24,32},{32,40},{40,48},{48,56},{56,64},{64,7... | collective-permute-start | bytes 393224 | tf_op jit(solution)/shard_map/while/body/eval_jaxpr/ppermute | solution.py:16
  215.1 9.3 collective-permute-start
  224.4 12.2 %collective-permute-start = (bf16[2,256,128]{2,1,0:T(8,128)(2,1)S(1)}, bf16[2,256,128]{2,1,0:T(8,128)(2,1)S(1)}, u32[]{:S(2)}, u32[]{:S(2)}) collective-permute-start(bf16[2,256,128]{2,1,0:T(8,128)(2,1)S(1)} %get-tuple-element.427), channel_id=1, source_target_pairs={{0,8},{8,16},{16,24},{24,32},{32,40},{40,48},{48,56},{56,64},{64,7... | collective-permute-start | bytes 393224 | tf_op jit(solution)/shard_map/while/body/eval_jaxpr/ppermute | solution.py:16
  236.7 9.3 collective-permute-start
  246.0 12.2 %collective-permute-start = (bf16[2,256,128]{2,1,0:T(8,128)(2,1)S(1)}, bf16[2,256,128]{2,1,0:T(8,128)(2,1)S(1)}, u32[]{:S(2)}, u32[]{:S(2)}) collective-permute-start(bf16[2,256,128]{2,1,0:T(8,128)(2,1)S(1)} %get-tuple-element.427), channel_id=1, source_target_pairs={{0,8},{8,16},{16,24},{24,32},{32,40},{40,48},{48,56},{56,64},{64,7... | collective-permute-start | bytes 393224 | tf_op jit(solution)/shard_map/while/body/eval_jaxpr/ppermute | solution.py:16
  258.2 9.3 collective-permute-start
  267.6 12.2 %collective-permute-start = (bf16[2,256,128]{2,1,0:T(8,128)(2,1)S(1)}, bf16[2,256,128]{2,1,0:T(8,128)(2,1)S(1)}, u32[]{:S(2)}, u32[]{:S(2)}) collective-permute-start(bf16[2,256,128]{2,1,0:T(8,128)(2,1)S(1)} %get-tuple-element.427), channel_id=1, source_target_pairs={{0,8},{8,16},{16,24},{24,32},{32,40},{40,48},{48,56},{56,64},{64,7... | collective-permute-start | bytes 393224 | tf_op jit(solution)/shard_map/while/body/eval_jaxpr/ppermute | solution.py:16
  279.8 9.3 collective-permute-start
  289.1 9.3 collective-permute-start
  298.4 9.3 collective-permute-start
  307.8 9.3 collective-permute-start
  317.1 9.3 collective-permute-start
  326.4 9.3 collective-permute-start
  335.7 9.3 collective-permute-start
  345.1 9.3 collective-permute-start
  354.4 9.3 collective-permute-start
  363.7 9.3 collective-permute-start
  373.0 9.3 collective-permute-start
  382.4 9.3 collective-permute-start
  391.7 9.3 collective-permute-start
  401.0 9.3 collective-permute-start
  410.3 9.3 collective-permute-start
  419.7 9.3 collective-permute-start
  429.0 9.3 collective-permute-start
  438.3 9.3 collective-permute-start
  447.6 9.3 collective-permute-start
  457.0 9.3 collective-permute-start
  466.3 9.3 collective-permute-start
  475.6 9.3 collective-permute-start
  484.9 9.3 collective-permute-start
  494.3 13.0 %collective-permute-start = (bf16[2,256,128]{2,1,0:T(8,128)(2,1)S(1)}, bf16[2,256,128]{2,1,0:T(8,128)(2,1)S(1)}, u32[]{:S(2)}, u32[]{:S(2)}) collective-permute-start(bf16[2,256,128]{2,1,0:T(8,128)(2,1)S(1)} %get-tuple-element.427), channel_id=1, source_target_pairs={{0,8},{8,16},{16,24},{24,32},{32,40},{40,48},{48,56},{56,64},{64,7... | collective-permute-start | bytes 393224 | tf_op jit(solution)/shard_map/while/body/eval_jaxpr/ppermute | solution.py:16
  507.3 11.1 %collective-permute-start = (bf16[2,256,128]{2,1,0:T(8,128)(2,1)S(1)}, bf16[2,256,128]{2,1,0:T(8,128)(2,1)S(1)}, u32[]{:S(2)}, u32[]{:S(2)}) collective-permute-start(bf16[2,256,128]{2,1,0:T(8,128)(2,1)S(1)} %get-tuple-element.427), channel_id=1, source_target_pairs={{0,8},{8,16},{16,24},{24,32},{32,40},{40,48},{48,56},{56,64},{64,7... | collective-permute-start | bytes 393224 | tf_op jit(solution)/shard_map/while/body/eval_jaxpr/ppermute | solution.py:16
  518.4 14.0 %collective-permute-start = (bf16[2,256,128]{2,1,0:T(8,128)(2,1)S(1)}, bf16[2,256,128]{2,1,0:T(8,128)(2,1)S(1)}, u32[]{:S(2)}, u32[]{:S(2)}) collective-permute-start(bf16[2,256,128]{2,1,0:T(8,128)(2,1)S(1)} %get-tuple-element.427), channel_id=1, source_target_pairs={{0,8},{8,16},{16,24},{24,32},{32,40},{40,48},{48,56},{56,64},{64,7... | collective-permute-start | bytes 393224 | tf_op jit(solution)/shard_map/while/body/eval_jaxpr/ppermute | solution.py:16
  532.4 11.8 %collective-permute-start = (bf16[2,256,128]{2,1,0:T(8,128)(2,1)S(1)}, bf16[2,256,128]{2,1,0:T(8,128)(2,1)S(1)}, u32[]{:S(2)}, u32[]{:S(2)}) collective-permute-start(bf16[2,256,128]{2,1,0:T(8,128)(2,1)S(1)} %get-tuple-element.427), channel_id=1, source_target_pairs={{0,8},{8,16},{16,24},{24,32},{32,40},{40,48},{48,56},{56,64},{64,7... | collective-permute-start | bytes 393224 | tf_op jit(solution)/shard_map/while/body/eval_jaxpr/ppermute | solution.py:16
  544.2 14.6 %collective-permute-start = (bf16[2,256,128]{2,1,0:T(8,128)(2,1)S(1)}, bf16[2,256,128]{2,1,0:T(8,128)(2,1)S(1)}, u32[]{:S(2)}, u32[]{:S(2)}) collective-permute-start(bf16[2,256,128]{2,1,0:T(8,128)(2,1)S(1)} %get-tuple-element.427), channel_id=1, source_target_pairs={{0,8},{8,16},{16,24},{24,32},{32,40},{40,48},{48,56},{56,64},{64,7... | collective-permute-start | bytes 393224 | tf_op jit(solution)/shard_map/while/body/eval_jaxpr/ppermute | solution.py:16
  558.9 11.5 %collective-permute-start = (bf16[2,256,128]{2,1,0:T(8,128)(2,1)S(1)}, bf16[2,256,128]{2,1,0:T(8,128)(2,1)S(1)}, u32[]{:S(2)}, u32[]{:S(2)}) collective-permute-start(bf16[2,256,128]{2,1,0:T(8,128)(2,1)S(1)} %get-tuple-element.427), channel_id=1, source_target_pairs={{0,8},{8,16},{16,24},{24,32},{32,40},{40,48},{48,56},{56,64},{64,7... | collective-permute-start | bytes 393224 | tf_op jit(solution)/shard_map/while/body/eval_jaxpr/ppermute | solution.py:16
  570.4 14.5 %collective-permute-start = (bf16[2,256,128]{2,1,0:T(8,128)(2,1)S(1)}, bf16[2,256,128]{2,1,0:T(8,128)(2,1)S(1)}, u32[]{:S(2)}, u32[]{:S(2)}) collective-permute-start(bf16[2,256,128]{2,1,0:T(8,128)(2,1)S(1)} %get-tuple-element.427), channel_id=1, source_target_pairs={{0,8},{8,16},{16,24},{24,32},{32,40},{40,48},{48,56},{56,64},{64,7... | collective-permute-start | bytes 393224 | tf_op jit(solution)/shard_map/while/body/eval_jaxpr/ppermute | solution.py:16
  584.9 11.2 %collective-permute-start = (bf16[2,256,128]{2,1,0:T(8,128)(2,1)S(1)}, bf16[2,256,128]{2,1,0:T(8,128)(2,1)S(1)}, u32[]{:S(2)}, u32[]{:S(2)}) collective-permute-start(bf16[2,256,128]{2,1,0:T(8,128)(2,1)S(1)} %get-tuple-element.427), channel_id=1, source_target_pairs={{0,8},{8,16},{16,24},{24,32},{32,40},{40,48},{48,56},{56,64},{64,7... | collective-permute-start | bytes 393224 | tf_op jit(solution)/shard_map/while/body/eval_jaxpr/ppermute | solution.py:16
  596.2 14.1 %collective-permute-start = (bf16[2,256,128]{2,1,0:T(8,128)(2,1)S(1)}, bf16[2,256,128]{2,1,0:T(8,128)(2,1)S(1)}, u32[]{:S(2)}, u32[]{:S(2)}) collective-permute-start(bf16[2,256,128]{2,1,0:T(8,128)(2,1)S(1)} %get-tuple-element.427), channel_id=1, source_target_pairs={{0,8},{8,16},{16,24},{24,32},{32,40},{40,48},{48,56},{56,64},{64,7... | collective-permute-start | bytes 393224 | tf_op jit(solution)/shard_map/while/body/eval_jaxpr/ppermute | solution.py:16
  611.2 423.6 %reduce-scatter.2.cloned.1.call-start = ((), (), s32[]{:S(2)}) async-start(), calls=%async_computation.2 | async-start | bytes 2129920 | tf_op jit(solution)/shard_map/reduce_scatter | solution.py:90
  (17 other events, 116.9 us)
Sparse Core Ops, SparseCore 0:
  611.3 266.8 all-gather.1
  882.8 151.9 reduce-scatter.1
where the time goes:
time: 1050 us; the launch traced here: 1040 us
  waiting for transfers between devices  504 us (48%)
  starting transfers between devices  467 us (44%)
  loops' own time  42.4 us (4%)
  between operations  14.8 us (1%)
    ppermute x63, starting transfers between devices, from_behind(): return lax.ppermute(value, axis, pairs)  467 us
    all_gather x1, waiting for transfers between devices, local(): x_all = lax.all_gather(attn_out, 'head', axis=1, tiled=True)  267 us
    reduce_scatter x1, waiting for transfers between devices, local(): lax.psum_scatter(lax.dot_general(x_all, attn_out, (((0,), (0,)), ((), ())...  154 us
    ppermute x63, waiting for transfers between devices, from_behind(): return lax.ppermute(value, axis, pairs)  83.2 us
    another operation x1, loops' own time, local(): states, moving = lax.fori_loop(1, ctx_count, chain_step, (states, stacked))  42.3 us
  transfers between devices with their start and end apart: 65, of which 65 were waited for; matrix products, arithmetic and copies ran while one was open for 0% of the time, Pallas kernels for 0%

commit v1 on v0

v1 whole, which is shorter than its diff:
```python
import math

import jax
import jax.numpy as jnp
from jax import lax
from jax.experimental import pallas as pl
from jax.experimental.pallas import tpu as pltpu
from jax.sharding import Mesh
from jax.sharding import PartitionSpec as P

HEADS = 16
KVG = 2
HD = 128
TOKENS = 16384

CTX = ("zh", "y", "c")
HEAD = ("g", "xl", "zl")
CHIPS = ("zh", "y")
SHARE = ("xl", "zl")
NZ, NY, NC, NS = 4, 8, 2, 4
TOK = 256
CUT = TOK // NS
TILE = NY * CUT
KEYS = NZ * TILE
SCALE = math.log2(math.e) / math.sqrt(HD)
LOW = -1e30
FLOOR = -1e29
STAT = 16


def dot_nt(a, b):
    return lax.dot_general(a, b, (((1,), (1,)), ((), ())), preferred_element_type=jnp.float32)


def dot_nn(a, b):
    return lax.dot_general(a, b, (((1,), (0,)), ((), ())), preferred_element_type=jnp.float32)


def attend_kernel(pos_ref, q_ref, own_ref, oth_ref, o_ref, s_ref, mx_ref, ve_ref, acc_ref):
    zh, y, c, u = pos_ref[0], pos_ref[1], pos_ref[2], pos_ref[3]
    ones = jnp.ones((KEYS, HD), jnp.bfloat16)
    for a, kv_ref in enumerate((own_ref, oth_ref)):
        ve_ref[a, :, 0:HD] = kv_ref[:, HD : 2 * HD]
        ve_ref[a, :, HD : 2 * HD] = ones
    lane = lax.broadcasted_iota(jnp.int32, (TOK, HD), 1)

    def one_part(up, _):
        stats = jnp.zeros((TOK, HD), jnp.float32)
        for hh in range(2):
            cols = slice(hh * HD, (hh + 1) * HD)
            q = q_ref[up, :, cols]
            mx_ref[...] = jnp.full((TOK, HD), LOW, jnp.float32)
            acc_ref[...] = jnp.zeros((TOK, 2 * HD), jnp.float32)

            def scores(zt, masked):
                for a, kv_ref in enumerate((own_ref, oth_ref)):
                    s = dot_nt(q, kv_ref[zt * TILE : (zt + 1) * TILE, 0:HD])
                    if masked:
                        n = lax.broadcasted_iota(jnp.int32, (TOK, TILE), 1)
                        r = lax.broadcasted_iota(jnp.int32, (TOK, TILE), 0)
                        side = c if a == 0 else 1 - c
                        k_pos = (n // CUT) * (2 * TOK) + n % CUT + side * TOK + u * CUT
                        s = jnp.where(k_pos <= r + (y * 2 + c) * TOK, s, LOW)
                    at = (2 * zt + a) * TILE
                    s_ref[:, at : at + TILE] = s
                    m = mx_ref[...]
                    for i in range(TILE // HD):
                        m = jnp.maximum(m, s[:, i * HD : (i + 1) * HD])
                    mx_ref[...] = m

            for zt in range(NZ):
                pl.when(zt < zh)(lambda zt=zt: scores(zt, False))
                pl.when(zt == zh)(lambda zt=zt: scores(zt, True))
            top = jnp.maximum(jnp.max(mx_ref[...], axis=1, keepdims=True), FLOOR) * SCALE

            def mix(zt):
                acc = acc_ref[...]
                for a in range(2):
                    at = (2 * zt + a) * TILE
                    w = jnp.exp2(s_ref[:, at : at + TILE] * SCALE - top).astype(jnp.bfloat16)
                    acc = acc + dot_nn(w, ve_ref[a, zt * TILE : (zt + 1) * TILE, :])
                acc_ref[...] = acc

            for zt in range(NZ):
                pl.when(zt <= zh)(lambda zt=zt: mix(zt))
            total = acc_ref[:, HD : 2 * HD]
            some = total > 0.0
            safe = jnp.where(some, total, 1.0)
            o_ref[up, 0:TOK, cols] = (acc_ref[:, 0:HD] / safe).astype(jnp.bfloat16)
            lse = jnp.where(some, top + jnp.log2(safe), LOW)
            hi = lse.astype(jnp.bfloat16).astype(jnp.float32)
            mid = (lse - hi).astype(jnp.bfloat16).astype(jnp.float32)
            low = lse - hi - mid
            for i, part in enumerate((hi, mid, low)):
                stats = jnp.where(lane == hh * 3 + i, part, stats)
        o_ref[up, TOK : TOK + STAT, :] = jnp.transpose(stats)[0:STAT].astype(jnp.bfloat16)
        return 0

    lax.fori_loop(0, NS, one_part, 0)


def combine_kernel(r_ref, x_ref):
    rows = [r_ref[s, TOK : TOK + STAT, :].astype(jnp.float32) for s in range(NS)]
    rows.append(jnp.zeros((HD - NS * STAT, TOK), jnp.float32))
    stats = jnp.transpose(jnp.concatenate(rows, axis=0))
    for hh in range(2):
        cols = slice(hh * HD, (hh + 1) * HD)
        lses = []
        for s in range(NS):
            at = s * STAT + hh * 3
            lses.append(stats[:, at : at + 1] + stats[:, at + 1 : at + 2] + stats[:, at + 2 : at + 3])
        top = jnp.maximum(jnp.maximum(lses[0], lses[1]), jnp.maximum(lses[2], lses[3]))
        w = [jnp.exp2(lse - top) for lse in lses]
        inv = 1.0 / (w[0] + w[1] + w[2] + w[3])
        x = jnp.zeros((TOK, HD), jnp.float32)
        for s in range(NS):
            x = x + r_ref[s, 0:TOK, cols].astype(jnp.float32) * (w[s] * inv)
        x_ref[:, cols] = x.astype(jnp.bfloat16)


def gram_kernel(r_ref, x_ref, h_ref):
    x = x_ref[...]
    for i in range(8):
        part = lax.dot_general(
            r_ref[i], x, (((0,), (0,)), ((), ())), preferred_element_type=jnp.float32
        )
        h_ref[i * 4 : (i + 1) * 4] = part.astype(jnp.bfloat16).reshape(4, 32, 2 * HD)


def vmem(n):
    return [pl.BlockSpec(memory_space=pltpu.VMEM)] * n


def local(queries, keys, values):
    zh, y, c = (lax.axis_index(a) for a in CTX)
    g = lax.axis_index("g")
    u = lax.axis_index(SHARE)
    swap = [(0, 1), (1, 0)]
    own = jnp.concatenate(
        [lax.dynamic_slice(part, (u * CUT, g * HD), (CUT, HD)) for part in (keys, values)], axis=1
    )
    with jax.named_scope("kv_gather"):
        kv_own = lax.all_to_all(
            jnp.broadcast_to(own[None], (NZ * NY, CUT, 2 * HD)), CHIPS, 0, 0
        ).reshape(KEYS, 2 * HD)
    with jax.named_scope("q_gather"):
        q_all = lax.all_to_all(jnp.broadcast_to(queries[None], (NS, TOK, 2 * HD)), SHARE, 0, 0)
    with jax.named_scope("kv_swap"):
        kv_oth = lax.ppermute(kv_own, "c", swap)
    pos = jnp.stack([zh, y, c, u]).astype(jnp.int32)
    part = pl.pallas_call(
        attend_kernel,
        out_shape=jax.ShapeDtypeStruct((NS, TOK + STAT, 2 * HD), jnp.bfloat16),
        in_specs=[pl.BlockSpec(memory_space=pltpu.SMEM)] + vmem(3),
        out_specs=vmem(1)[0],
        scratch_shapes=[
            pltpu.VMEM((TOK, 2 * KEYS), jnp.float32),
            pltpu.VMEM((TOK, HD), jnp.float32),
            pltpu.VMEM((2, KEYS, 2 * HD), jnp.bfloat16),
            pltpu.VMEM((TOK, 2 * HD), jnp.float32),
        ],
        compiler_params=pltpu.CompilerParams(vmem_limit_bytes=32 << 20),
        name="attend",
    )(pos, q_all, kv_own, kv_oth)
    with jax.named_scope("part_exchange"):
        parts = lax.all_to_all(part, SHARE, 0, 0)
    attn_out = pl.pallas_call(
        combine_kernel,
        out_shape=jax.ShapeDtypeStruct((TOK, 2 * HD), jnp.bfloat16),
        in_specs=vmem(1),
        out_specs=vmem(1)[0],
        compiler_params=pltpu.CompilerParams(vmem_limit_bytes=32 << 20),
        name="combine",
    )(parts)
    with jax.named_scope("x_swap"):
        attn_oth = lax.ppermute(attn_out, "c", swap)
    x = jnp.concatenate([attn_out, attn_oth], axis=0)
    col = jnp.arange(HD, dtype=jnp.int32)
    picked = (col // 32) * 64 + c * 32 + col % 32
    pick = (jnp.arange(2 * HD, dtype=jnp.int32)[:, None] == picked[None, :]).astype(jnp.bfloat16)
    x_half = jnp.dot(x, pick, preferred_element_type=jnp.float32).astype(jnp.bfloat16)
    with jax.named_scope("x_gather"):
        x_all = lax.all_to_all(jnp.broadcast_to(x_half[None], (8, 2 * TOK, HD)), HEAD, 0, 0)
    gram = pl.pallas_call(
        gram_kernel,
        out_shape=jax.ShapeDtypeStruct((NZ * NY, 32, 2 * HD), jnp.bfloat16),
        in_specs=vmem(2),
        out_specs=vmem(1)[0],
        compiler_params=pltpu.CompilerParams(vmem_limit_bytes=32 << 20),
        name="gram",
    )(x_all, x)
    with jax.named_scope("h_exchange"):
        h_parts = lax.all_to_all(gram, CHIPS, 0, 0)
    hessian = jnp.sum(h_parts.astype(jnp.float32), axis=0) * (2.0 / TOKENS)
    return attn_out, hessian


def solution(mesh):
    cut = Mesh(mesh.devices.reshape(NZ, NY, NC, 2, 2, 2), CTX + HEAD)
    in_specs = (P(CTX, HEAD), P(CTX, None), P(CTX, None))
    out_specs = (P(CTX, HEAD), P(CTX, HEAD))
    return jax.shard_map(local, mesh=cut, in_specs=in_specs, out_specs=out_specs, check_vma=False)
```

time: 1050 us -> 151 us (0.14)
  the two profiles are of different devices: /device:TPU:1 before, /device:TPU:8 now
where the time goes in v1:
time: 151 us
  blocking collectives  97 us (64%)
  waiting for transfers between devices  26.3 us (17%)
  starting transfers between devices  12.1 us (8%)
  Pallas kernels  9.88 us (7%)
  local copies, waits for them, and re-layouts  2.78 us (2%)
    all_to_all x1, blocking collectives, local(): lax.all_to_all(jnp.broadcast_to(own[None], (NZ * NY, CUT, 2 * HD)), CHIPS...  47.3 us
    all_to_all x1, blocking collectives, local(): h_parts = lax.all_to_all(gram, CHIPS, 0, 0)  38.3 us
    all_to_all x1, waiting for transfers between devices, local(): lax.all_to_all(jnp.broadcast_to(x_half[None], (8, 2 * TOK, HD)), HEAD, 0, 0)  16 us
    all_to_all x1, blocking collectives, local(): parts = lax.all_to_all(part, SHARE, 0, 0)  11.5 us
    all_to_all x1, waiting for transfers between devices, local(): lax.all_to_all(jnp.broadcast_to(queries[None], (NS, TOK, 2 * HD)), SHARE,...  8.72 us
    pallas_call x1, Pallas kernels, local(): pl.pallas_call(attend_kernel, out_shape=jax.ShapeDtypeStruct((NS, TOK + S...  7.76 us
    all_to_all x1, starting transfers between devices, local(): lax.all_to_all(jnp.broadcast_to(x_half[None], (8, 2 * TOK, HD)), HEAD, 0, 0)  4.72 us
    all_to_all x1, starting transfers between devices, local(): lax.all_to_all(jnp.broadcast_to(queries[None], (NS, TOK, 2 * HD)), SHARE,...  3.6 us
  transfers between devices with their start and end apart: 4, of which 3 were waited for; matrix products, arithmetic and copies ran while one was open for 1% of the time, Pallas kernels for 0%

profile of v1, /device:TPU:8, one launch (start us, length us, event | category | flops | bytes accessed | tf_op | source)
XLA Modules:
  0.0 150.8 jit_solution(9285831325047131037)
XLA Ops:
  0.6 0.0 dynamic-slice-start
  0.7 0.0 dynamic-slice-start.1
  0.7 0.7 dynamic-slice-done
  1.4 0.0 dynamic-slice-done.1
  1.4 0.1 broadcast_in_dim.7
  1.5 0.0 copy-start.1
  1.5 47.3 %all_to_all.25 = bf16[32,64,256]{2,1,0:T(8,128)(2,1)S(1)} all-to-all(bf16[32,64,256]{2,1,0:T(8,128)(2,1)S(1)} %broadcast_in_dim.7), channel_id=1, replica_groups=mesh['zh'=4,'y'=8,'c'=2,'g'=2,'xl'=2,'zl'=2] {'zh','y'}, dimensions={0} | all-to-all | bytes 2097152 | tf_op jit(solution)/shard_map/kv_gather/all_to_all | solution.py:143
  48.8 1.9 %collective-permute-start = (bf16[2048,256]{1,0:T(8,128)(2,1)S(1)}, bf16[2048,256]{1,0:T(8,128)(2,1)S(1)}, u32[]{:S(2)}, u32[]{:S(2)}) collective-permute-start(bf16[2048,256]{1,0:T(8,128)(2,1)S(1)} %bitcast.5), channel_id=1, source_target_pairs={{0,8},{8,0},{1,9},{9,1},{2,10},{10,2},{3,11},{11,3},{4,12},{12,4},... | collective-permute-start | bytes 3145736 | tf_op jit(solution)/shard_map/kv_swap/ppermute | solution.py:149
  50.7 0.0 copy-done.1
  50.7 0.8 broadcast_in_dim.6
  51.6 3.6 %all-to-all-start = ((bf16[4,256,256]{2,1,0:T(8,128)(2,1)}), bf16[4,256,256]{2,1,0:T(8,128)(2,1)S(1)}, u32[]{:S(2)}, u32[]{:S(2)}) async-start(bf16[4,256,256]{2,1,0:T(8,128)(2,1)} %broadcast_in_dim.6), calls=%async_computation | async-start | bytes 1048576 | tf_op jit(solution)/shard_map/q_gather/all_to_all | solution.py:147
  55.2 0.1 pad_add_fusion.pos_ref
  55.2 8.7 %all-to-all-done.q_ref = bf16[4,256,256]{2,1,0:T(8,128)(2,1)S(1)} async-done(((bf16[4,256,256]{2,1,0:T(8,128)(2,1)}), bf16[4,256,256]{2,1,0:T(8,128)(2,1)S(1)}, u32[]{:S(2)}, u32[]{:S(2)}) %all-to-all-start) | async-done | bytes 524320 | tf_op jit(solution)/shard_map/q_gather/all_to_all | solution.py:147
  64.0 0.0 collective-permute-done.oth_ref
  64.0 7.8 %attend.1 = bf16[4,272,256]{2,1,0:T(8,128)(2,1)S(1)} custom-call(s32[4]{0:T(128)S(1)} %pad_add_fusion.pos_ref, bf16[4,256,256]{2,1,0:T(8,128)(2,1)S(1)} %all-to-all-done.q_ref, bf16[2048,256]{1,0:T(8,128)(2,1)S(1)} %bitcast.6, bf16[2048,256]{1,0:T(8,128)(2,1)S(1)} %collective-permute-done.oth_ref), custom_call_target="tpu_custom_call" | custom-call | tf_op jit(solution)/shard_map/attend/pallas_call | solution.py:151
  71.7 11.5 %all_to_all.26.r_ref = bf16[4,272,256]{2,1,0:T(8,128)(2,1)S(1)} all-to-all(bf16[4,272,256]{2,1,0:T(8,128)(2,1)S(1)} %attend.1), channel_id=1, replica_groups=mesh['zh'=4,'y'=8,'c'=2,'g'=2,'xl'=2,'zl'=2] {'xl','zl'}, dimensions={0} | all-to-all | bytes 1114112 | tf_op jit(solution)/shard_map/part_exchange/all_to_all | solution.py:166
  83.2 1.6 %combine.1 = bf16[256,256]{1,0:T(8,128)(2,1)} custom-call(bf16[4,272,256]{2,1,0:T(8,128)(2,1)S(1)} %all_to_all.26.r_ref), custom_call_target="tpu_custom_call" | custom-call | tf_op jit(solution)/shard_map/combine/pallas_call | solution.py:167
  84.8 1.9 %collective-permute-start.1 = (bf16[256,256]{1,0:T(8,128)(2,1)}, bf16[256,256]{1,0:T(8,128)(2,1)S(1)}, u32[]{:S(2)}, u32[]{:S(2)}) collective-permute-start(bf16[256,256]{1,0:T(8,128)(2,1)} %combine.1), channel_id=1, source_target_pairs={{0,8},{8,0},{1,9},{9,1},{2,10},{10,2},{3,11},{11,3},{4,12},{12,4},... | collective-permute-start | bytes 393224 | tf_op jit(solution)/shard_map/x_swap/ppermute | solution.py:176
  86.8 1.5 %collective-permute-done.1 = bf16[256,256]{1,0:T(8,128)(2,1)S(1)} collective-permute-done((bf16[256,256]{1,0:T(8,128)(2,1)}, bf16[256,256]{1,0:T(8,128)(2,1)S(1)}, u32[]{:S(2)}, u32[]{:S(2)}) %collective-permute-start.1) | collective-permute-done | bytes 131104 | tf_op jit(solution)/shard_map/x_swap/ppermute | solution.py:176
  88.3 1.1 convolution_convert_fusion
  89.4 1.1 broadcast_in_dim.8
  90.5 0.0 copy-start
  90.5 4.7 %all-to-all-start.3 = ((bf16[8,512,128]{2,1,0:T(8,128)(2,1)}), bf16[8,512,128]{2,1,0:T(8,128)(2,1)S(1)}, u32[]{:S(2)}, u32[]{:S(2)}) async-start(bf16[8,512,128]{2,1,0:T(8,128)(2,1)} %broadcast_in_dim.8), calls=%async_computation.3 | async-start | bytes 2097152 | tf_op jit(solution)/shard_map/x_gather/all_to_all | solution.py:183
  95.2 0.0 copy-done
  95.3 16.0 %all-to-all-done.3.r_ref = bf16[8,512,128]{2,1,0:T(8,128)(2,1)S(1)} async-done(((bf16[8,512,128]{2,1,0:T(8,128)(2,1)}), bf16[8,512,128]{2,1,0:T(8,128)(2,1)S(1)}, u32[]{:S(2)}, u32[]{:S(2)}) %all-to-all-start.3) | async-done | bytes 1048608 | tf_op jit(solution)/shard_map/x_gather/all_to_all | solution.py:183
  111.3 0.5 gram.1
  111.8 38.3 %all_to_all.27 = bf16[32,32,256]{2,1,0:T(8,128)(2,1)S(1)} all-to-all(bf16[32,32,256]{2,1,0:T(8,128)(2,1)S(1)} %gram.1), channel_id=1, replica_groups=mesh['zh'=4,'y'=8,'c'=2,'g'=2,'xl'=2,'zl'=2] {'zh','y'}, dimensions={0} | all-to-all | bytes 1048576 | tf_op jit(solution)/shard_map/h_exchange/all_to_all | solution.py:193
  150.1 0.1 convert_reduce_fusion
  150.2 0.6 broadcast_multiply_fusion
  (3 shorter events, 0.0 us)
Async XLA Ops:
  0.6 0.7 dynamic-slice-start
  0.7 0.7 dynamic-slice-start.1
  1.5 49.2 %copy-start.1 = (bf16[256,256]{1,0:T(8,128)(2,1)S(1)}, bf16[256,256]{1,0:T(8,128)(2,1)}, u32[]{:S(2)}) copy-start(bf16[256,256]{1,0:T(8,128)(2,1)} %param.3) | copy-start | bytes 393220
  48.8 15.2 %collective-permute-start = (bf16[2048,256]{1,0:T(8,128)(2,1)S(1)}, bf16[2048,256]{1,0:T(8,128)(2,1)S(1)}, u32[]{:S(2)}, u32[]{:S(2)}) collective-permute-start(bf16[2048,256]{1,0:T(8,128)(2,1)S(1)} %bitcast.5), channel_id=1, source_target_pairs={{0,8},{8,0},{1,9},{9,1},{2,10},{10,2},{3,11},{11,3},{4,12},{12,4},... | collective-permute-start | bytes 3145736 | tf_op jit(solution)/shard_map/kv_swap/ppermute | solution.py:149
  51.6 12.4 %all-to-all-start = ((bf16[4,256,256]{2,1,0:T(8,128)(2,1)}), bf16[4,256,256]{2,1,0:T(8,128)(2,1)S(1)}, u32[]{:S(2)}, u32[]{:S(2)}) async-start(bf16[4,256,256]{2,1,0:T(8,128)(2,1)} %broadcast_in_dim.6), calls=%async_computation | async-start | bytes 1048576 | tf_op jit(solution)/shard_map/q_gather/all_to_all | solution.py:147
  84.8 3.4 %collective-permute-start.1 = (bf16[256,256]{1,0:T(8,128)(2,1)}, bf16[256,256]{1,0:T(8,128)(2,1)S(1)}, u32[]{:S(2)}, u32[]{:S(2)}) collective-permute-start(bf16[256,256]{1,0:T(8,128)(2,1)} %combine.1), channel_id=1, source_target_pairs={{0,8},{8,0},{1,9},{9,1},{2,10},{10,2},{3,11},{11,3},{4,12},{12,4},... | collective-permute-start | bytes 393224 | tf_op jit(solution)/shard_map/x_swap/ppermute | solution.py:176
  90.5 4.7 %copy-start = (bf16[256,256]{1,0:T(8,128)(2,1)S(1)}, bf16[256,256]{1,0:T(8,128)(2,1)}, u32[]{:S(2)}) copy-start(bf16[256,256]{1,0:T(8,128)(2,1)} %combine.1) | copy-start | bytes 393220
  90.5 20.8 %all-to-all-start.3 = ((bf16[8,512,128]{2,1,0:T(8,128)(2,1)}), bf16[8,512,128]{2,1,0:T(8,128)(2,1)S(1)}, u32[]{:S(2)}, u32[]{:S(2)}) async-start(bf16[8,512,128]{2,1,0:T(8,128)(2,1)} %broadcast_in_dim.8), calls=%async_computation.3 | async-start | bytes 2097152 | tf_op jit(solution)/shard_map/x_gather/all_to_all | solution.py:183

commit v2 on v0

v2 whole, which is shorter than its diff:
```python
import math

import jax
import jax.numpy as jnp
from jax import lax
from jax.experimental import pallas as pl
from jax.experimental.pallas import tpu as pltpu
from jax.sharding import Mesh
from jax.sharding import PartitionSpec as P

HEADS = 16
KVG = 2
HD = 128
TOKENS = 16384

CTX = ("zh", "y", "c")
HEAD = ("g", "xl", "zl")
CHIPS = ("zh", "y")
SHARE = ("xl", "zl")
NZ, NY, NC, NS = 4, 8, 2, 4
TOK = 256
CUT = TOK // NS
TILE = NY * CUT
WIDE = NC * TILE
KEYS = NZ * TILE
ROWS = NS * TOK
PIECE = 256
SCALE = math.log2(math.e) / math.sqrt(HD)
LOW = -1e30
FLOOR = -1e29
STAT = 16
ABC = (((1,), (0,)), ((), ()))
ATB = (((0,), (0,)), ((), ()))


def dot(a, b, dims=ABC):
    return lax.dot_general(a, b, dims, preferred_element_type=jnp.float32)


def iota(shape, dim):
    return lax.broadcasted_iota(jnp.int32, shape, dim)


def column(side, at):
    return (at // 32) * 64 + side * 32 + at % 32


def prep_kernel(pos_ref, k_ref, v_ref, o_ref):
    u, g = pos_ref[3], pos_ref[4]
    rows = pl.ds(pl.multiple_of(u * CUT, CUT), CUT)
    k = jnp.where(g == 0, k_ref[rows, 0:HD], k_ref[rows, HD : 2 * HD])
    v = jnp.where(g == 0, v_ref[rows, 0:HD], v_ref[rows, HD : 2 * HD])
    to = iota((HD, HD), 1)
    order = iota((HD, HD), 0) == column(to // 64, to % 64)
    v = dot(v, order.astype(jnp.bfloat16)).astype(jnp.bfloat16)
    for i in range(NZ * NY):
        o_ref[i, :, 0:HD] = k
        o_ref[i, :, HD : 2 * HD] = v


def attend_kernel(
    pos_ref, q0_ref, q1_ref, q2_ref, own_ref, oth_ref, o_ref, q_s, k_s, ve_s, s_s, mx_s, acc_s, st_s, o0_s
):
    zh, y, c, u = pos_ref[0], pos_ref[1], pos_ref[2], pos_ref[3]
    for zt in range(NZ):
        for a, kv_ref in enumerate((own_ref, oth_ref)):
            src = slice(zt * TILE, (zt + 1) * TILE)
            dst = slice(a * TILE, (a + 1) * TILE)
            k_s[zt, :, dst] = jnp.transpose(kv_ref[src, 0:HD])
            ve_s[zt, dst, 0:HD] = kv_ref[src, HD : 2 * HD]
            ve_s[zt, dst, HD : 2 * HD] = jnp.ones((TILE, HD), jnp.bfloat16)
    for hh in range(2):
        cols = slice(hh * HD, (hh + 1) * HD)
        for i, q in enumerate((q0_ref[:, cols], q1_ref[:, cols], q2_ref[0, :, cols], q2_ref[1, :, cols])):
            q_s[hh, i * TOK : (i + 1) * TOK, :] = q

    def body(zt, masked, new, old, top):
        if new is not None:
            q = q_s[new]
            m = mx_s[...]
        if old is not None:
            acc = acc_s[...]
        for p in range(WIDE // PIECE):
            at = slice(p * PIECE, (p + 1) * PIECE)
            if old is not None:
                w = jnp.exp2(s_s[zt, :, at] * SCALE - top).astype(jnp.bfloat16)
                acc = acc + dot(w, ve_s[zt, at, :])
            if new is not None:
                s = dot(q, k_s[zt, :, at])
                if masked:
                    n = iota((ROWS, PIECE), 1) + p * PIECE % TILE
                    r = iota((ROWS, PIECE), 0) % TOK
                    side = c if p * PIECE < TILE else 1 - c
                    k_pos = (n // CUT) * (2 * TOK) + n % CUT + side * TOK + u * CUT
                    s = jnp.where(k_pos <= r + (y * 2 + c) * TOK, s, LOW)
                s_s[zt, :, at] = s
                for i in range(PIECE // HD):
                    m = jnp.maximum(m, s[:, i * HD : (i + 1) * HD])
        if new is not None:
            mx_s[...] = m
        if old is not None:
            acc_s[...] = acc

    def sweep(new, old, top):
        if new is not None:
            mx_s[...] = jnp.full((ROWS, HD), LOW, jnp.float32)
        if old is not None:
            acc_s[...] = jnp.zeros((ROWS, 2 * HD), jnp.float32)

        def step(zt, _):
            body(zt, False, new, old, top)
            return 0

        lax.fori_loop(0, zh, step, 0)
        body(zh, True, new, old, top)

    def tops():
        return jnp.maximum(jnp.max(mx_s[...], axis=1, keepdims=True), FLOOR) * SCALE

    def finish(hh, top):
        total = acc_s[:, HD : 2 * HD]
        some = total > 0.0
        safe = jnp.where(some, total, 1.0)
        lse = jnp.where(some, top + jnp.log2(safe), LOW)
        hi = lse.astype(jnp.bfloat16).astype(jnp.float32)
        mid = (lse - hi).astype(jnp.bfloat16).astype(jnp.float32)
        lane = iota((ROWS, HD), 1) - 3 * hh
        parts = jnp.where(lane == 0, hi, jnp.where(lane == 1, mid, lse - hi - mid))
        return acc_s[:, 0:HD] / safe, parts

    sweep(0, None, None)
    top0 = tops()
    sweep(1, 0, top0)
    o0_s[...], st_s[...] = finish(0, top0)
    top1 = tops()
    sweep(None, 1, top1)
    o1, st1 = finish(1, top1)
    o0 = o0_s[...]
    lane = iota((ROWS, HD), 1)
    stats = jnp.where(lane < 3, st_s[...], st1)
    left = lane < HD // 2
    sides = (
        jnp.where(left, o0, pltpu.roll(o1, HD // 2, 1)).astype(jnp.bfloat16),
        jnp.where(left, pltpu.roll(o0, HD // 2, 1), o1).astype(jnp.bfloat16),
    )
    for i in range(NS):
        up = u + (1 - 2 * (u // 2)) * 2 * (i % 2) + (1 - 2 * (u % 2)) * (i // 2)
        rows = slice(i * TOK, (i + 1) * TOK)
        turned = jnp.transpose(stats[rows])
        tail = jnp.concatenate([turned[0:8, 0:HD], turned[0:8, HD : 2 * HD]], axis=0)
        for side in range(NC):
            o_ref[side * NS + up, 0:TOK, :] = sides[side][rows]
            o_ref[side * NS + up, TOK : TOK + STAT, :] = tail.astype(jnp.bfloat16)


def combine_kernel(r_ref, x_ref, many_ref):
    left = iota((HD, HD), 1) < HD // 2
    for half in range(2):
        shares = []
        for c in range(NC):
            for hh in range(2):
                lses = []
                for s in range(c * NS, (c + 1) * NS):
                    t = r_ref[s, TOK : TOK + STAT, :].astype(jnp.float32)
                    at = half * 8 + hh * 3
                    lses.append(t[at : at + 1] + t[at + 1 : at + 2] + t[at + 2 : at + 3])
                top = jnp.maximum(jnp.maximum(lses[0], lses[1]), jnp.maximum(lses[2], lses[3]))
                w = [jnp.exp2(lse - top) for lse in lses]
                inv = 1.0 / (w[0] + w[1] + w[2] + w[3])
                shares += [part * inv for part in w]
        shares.append(jnp.zeros((HD - len(shares), HD), jnp.float32))
        turned = jnp.transpose(jnp.concatenate(shares, axis=0))
        for c in range(NC):
            x = jnp.zeros((HD, HD), jnp.float32)
            for s in range(NS):
                at = c * 2 * NS + s
                w = jnp.where(left, turned[:, at : at + 1], turned[:, at + NS : at + NS + 1])
                x = x + r_ref[c * NS + s, half * HD : (half + 1) * HD, :].astype(jnp.float32) * w
            x = x.astype(jnp.bfloat16)
            rows = slice(c * TOK + half * HD, c * TOK + (half + 1) * HD)
            x_ref[rows, :] = x
            for i in range(8):
                many_ref[i, rows, :] = x


def assemble_kernel(pos_ref, own_ref, oth_ref, x_ref, out_ref):
    c = pos_ref[2]
    at, to = iota((HD, 2 * HD), 0), iota((HD, 2 * HD), 1)
    x = jnp.zeros((NC * TOK, 2 * HD), jnp.float32)
    for part_ref, side in ((own_ref, c), (oth_ref, 1 - c)):
        x = x + dot(part_ref[...], (to == column(side, at)).astype(jnp.bfloat16))
    x_ref[...] = x.astype(jnp.bfloat16)
    out_ref[...] = x_ref[pl.ds(pl.multiple_of(c * TOK, TOK), TOK), :]


def gram_kernel(r_ref, x_ref, h_ref):
    x = x_ref[...]
    for i in range(8):
        part = dot(r_ref[i], x, ATB)
        h_ref[i * 4 : (i + 1) * 4] = part.astype(jnp.bfloat16).reshape(4, 32, 2 * HD)


def call(kernel, name, outs, args, scratch=(), flops=0, moved=0):
    spaces = [pltpu.SMEM if a.dtype == jnp.int32 else pltpu.VMEM for a in args]
    shapes = [jax.ShapeDtypeStruct(s, jnp.bfloat16) for s in outs]
    return pl.pallas_call(
        kernel,
        out_shape=shapes,
        in_specs=[pl.BlockSpec(memory_space=s) for s in spaces],
        out_specs=[pl.BlockSpec(memory_space=pltpu.VMEM)] * len(outs),
        scratch_shapes=list(scratch),
        compiler_params=pltpu.CompilerParams(vmem_limit_bytes=40 << 20),
        cost_estimate=pl.CostEstimate(flops=flops, bytes_accessed=moved, transcendentals=0),
        name=name,
    )(*args)


def local(queries, keys, values):
    spots = [lax.axis_index(a) for a in CTX] + [lax.axis_index(SHARE), lax.axis_index("g")]
    pos = jnp.stack(spots).astype(jnp.int32)
    swap = [(0, 1), (1, 0)]
    (own,) = call(prep_kernel, "prep", [(NZ * NY, CUT, 2 * HD)], (pos, keys, values))
    with jax.named_scope("kv_gather"):
        kv_own = lax.all_to_all(own, CHIPS, 0, 0).reshape(KEYS, 2 * HD)
    with jax.named_scope("q_gather"):
        q1 = lax.ppermute(queries, "xl", swap)
        q2 = lax.ppermute(jnp.stack([queries, q1]), "zl", swap)
    with jax.named_scope("kv_swap"):
        kv_oth = lax.ppermute(kv_own, "c", swap)
    f32, bf16 = jnp.float32, jnp.bfloat16
    scratch = (
        pltpu.VMEM((2, ROWS, HD), bf16),
        pltpu.VMEM((NZ, HD, WIDE), bf16),
        pltpu.VMEM((NZ, WIDE, 2 * HD), bf16),
        pltpu.VMEM((NZ, ROWS, WIDE), f32),
        pltpu.VMEM((ROWS, HD), f32),
        pltpu.VMEM((ROWS, 2 * HD), f32),
        pltpu.VMEM((ROWS, HD), f32),
        pltpu.VMEM((ROWS, HD), f32),
    )
    (part,) = call(
        attend_kernel,
        "attend",
        [(NC * NS, TOK + STAT, HD)],
        (pos, queries, q1, q2, kv_own, kv_oth),
        scratch,
        flops=1 << 33,
    )
    with jax.named_scope("part_exchange"):
        parts = lax.all_to_all(part, ("c",) + SHARE, 0, 0)
    x_own, x_many = call(
        combine_kernel, "combine", [(NC * TOK, HD), (8, NC * TOK, HD)], (parts,)
    )
    with jax.named_scope("x_swap"):
        x_oth = lax.ppermute(x_own, "c", swap)
    with jax.named_scope("x_gather"):
        x_all = lax.all_to_all(x_many, HEAD, 0, 0)
    x, attn_out = call(
        assemble_kernel,
        "assemble",
        [(NC * TOK, 2 * HD), (TOK, 2 * HD)],
        (pos, x_own, x_oth),
        flops=1 << 27,
        moved=1 << 20,
    )
    (gram,) = call(gram_kernel, "gram", [(NZ * NY, 32, 2 * HD)], (x_all, x))
    with jax.named_scope("h_exchange"):
        h_parts = lax.all_to_all(gram, CHIPS, 0, 0)
    hessian = jnp.sum(h_parts.astype(jnp.float32), axis=0) * (2.0 / TOKENS)
    return attn_out, hessian


def solution(mesh):
    cut = Mesh(mesh.devices.reshape(NZ, NY, NC, 2, 2, 2), CTX + HEAD)
    in_specs = (P(CTX, HEAD), P(CTX, None), P(CTX, None))
    out_specs = (P(CTX, HEAD), P(CTX, HEAD))
    return jax.shard_map(local, mesh=cut, in_specs=in_specs, out_specs=out_specs, check_vma=False)
```

time: 1050 us -> 144 us (0.14)
  the two profiles are of different devices: /device:TPU:1 before, /device:TPU:8 now
where the time goes in v2:
time: 144 us; the launch traced here: 143 us
  blocking collectives  92.6 us (64%)
  waiting for transfers between devices  23.5 us (16%)
  starting transfers between devices  14.5 us (10%)
  Pallas kernels  9.26 us (6%)
  local copies, waits for them, and re-layouts  1.9 us (1%)
    all_to_all x1, blocking collectives, local(): kv_own = lax.all_to_all(own, CHIPS, 0, 0).reshape(KEYS, 2 * HD)  47.3 us
    all_to_all x1, blocking collectives, local(): h_parts = lax.all_to_all(gram, CHIPS, 0, 0)  31.8 us
    all_to_all x1, blocking collectives, local(): parts = lax.all_to_all(part, ('c',) + SHARE, 0, 0)  13.5 us
    all_to_all x1, waiting for transfers between devices, local(): x_all = lax.all_to_all(x_many, HEAD, 0, 0)  11.3 us
    pallas_call x5, Pallas kernels, call(): pl.pallas_call(kernel, out_shape=shapes, in_specs=[pl.BlockSpec(memory_sp...  9.26 us
    ppermute x1, waiting for transfers between devices, local(): q2 = lax.ppermute(jnp.stack([queries, q1]), 'zl', swap)  6.5 us
    ppermute x1, waiting for transfers between devices, local(): q1 = lax.ppermute(queries, 'xl', swap)  4.39 us
    all_to_all x1, starting transfers between devices, local(): x_all = lax.all_to_all(x_many, HEAD, 0, 0)  4.01 us
  transfers between devices with their start and end apart: 5, of which 4 were waited for; matrix products, arithmetic and copies ran while one was open for 0% of the time, Pallas kernels for 1%

profile of v2, /device:TPU:8, one launch (start us, length us, event | category | flops | bytes accessed | tf_op | source)
XLA Modules:
  0.0 143.2 jit_solution(2128707719306921310)
XLA Ops:
  0.6 0.1 stack.32.pos_ref
  0.7 0.0 copy-start
  0.7 0.9 copy-done
  1.6 0.0 copy-start.1
  1.6 0.9 copy-done.1
  2.5 0.9 prep.1
  3.4 0.0 copy-start.2
  3.4 47.3 %all_to_all.20 = bf16[32,64,256]{2,1,0:T(8,128)(2,1)S(1)} all-to-all(bf16[32,64,256]{2,1,0:T(8,128)(2,1)S(1)} %prep.1), channel_id=1, replica_groups=mesh['zh'=4,'y'=8,'c'=2,'g'=2,'xl'=2,'zl'=2] {'zh','y'}, dimensions={0} | all-to-all | bytes 2097152 | tf_op jit(solution)/shard_map/kv_gather/all_to_all | solution.py:224
  50.7 1.9 %collective-permute-start.2 = (bf16[2048,256]{1,0:T(8,128)(2,1)S(1)}, bf16[2048,256]{1,0:T(8,128)(2,1)S(1)}, u32[]{:S(2)}, u32[]{:S(2)}) collective-permute-start(bf16[2048,256]{1,0:T(8,128)(2,1)S(1)} %bitcast.8), channel_id=1, source_target_pairs={{0,8},{8,0},{1,9},{9,1},{2,10},{10,2},{3,11},{11,3},{4,12},{12,4},... | collective-permute-start | bytes 3145736 | tf_op jit(solution)/shard_map/kv_swap/ppermute | solution.py:229
  52.6 0.0 copy-done.2
  52.6 3.4 %collective-permute-start = (bf16[256,256]{1,0:T(8,128)(2,1)S(1)}, bf16[256,256]{1,0:T(8,128)(2,1)S(1)}, u32[]{:S(2)}, u32[]{:S(2)}) collective-permute-start(bf16[256,256]{1,0:T(8,128)(2,1)S(1)} %copy-done.2), channel_id=1, source_target_pairs={{0,2},{2,0},{1,3},{3,1},{4,6},{6,4},{5,7},{7,5},{8,10},{10,8},{9,1... | collective-permute-start | bytes 393224 | tf_op jit(solution)/shard_map/q_gather/ppermute | solution.py:226
  56.0 4.4 %collective-permute-done.q1_ref = bf16[256,256]{1,0:T(8,128)(2,1)S(1)} collective-permute-done((bf16[256,256]{1,0:T(8,128)(2,1)S(1)}, bf16[256,256]{1,0:T(8,128)(2,1)S(1)}, u32[]{:S(2)}, u32[]{:S(2)}) %collective-permute-start) | collective-permute-done | bytes 131104 | tf_op jit(solution)/shard_map/q_gather/ppermute | solution.py:226
  60.5 3.3 %collective-permute-start.1 = (bf16[2,256,256]{2,1,0:T(8,128)(2,1)S(1)}, bf16[2,256,256]{2,1,0:T(8,128)(2,1)S(1)}, u32[]{:S(2)}, u32[]{:S(2)}) collective-permute-start(bf16[2,256,256]{2,1,0:T(8,128)(2,1)S(1)} %pad_maximum_fusion), channel_id=1, source_target_pairs={{0,1},{1,0},{2,3},{3,2},{4,5},{5,4},{6,7},{7,6},{8,9},{9,8},{10,11... | collective-permute-start | bytes 786440 | tf_op jit(solution)/shard_map/q_gather/ppermute | solution.py:227
  63.8 6.5 %collective-permute-done.1.q2_ref = bf16[2,256,256]{2,1,0:T(8,128)(2,1)S(1)} collective-permute-done((bf16[2,256,256]{2,1,0:T(8,128)(2,1)S(1)}, bf16[2,256,256]{2,1,0:T(8,128)(2,1)S(1)}, u32[]{:S(2)}, u32[]{:S(2)}) %collective-permute-start.1) | collective-permute-done | bytes 262176 | tf_op jit(solution)/shard_map/q_gather/ppermute | solution.py:227
  70.3 0.0 collective-permute-done.2.oth_ref
  70.3 4.7 %attend.1 = bf16[8,272,128]{2,1,0:T(8,128)(2,1)S(1)} custom-call(s32[5]{0:T(128)S(1)} %stack.32.pos_ref, bf16[256,256]{1,0:T(8,128)(2,1)S(1)} %copy-done.2, bf16[256,256]{1,0:T(8,128)(2,1)S(1)} %collective-permute-done.q1_ref, bf16[2,256,256]{2,1,0:T(8,128)(2,1)S(1)} %collective-permute-done.1.q2_ref, bf16[2048,256]{1,0:T(8,128)(2,1)S(1)} %bitcast.9, ...), custom_call_target="tpu_custom_call" | custom-call | flops 8589934592 | tf_op jit(solution)/shard_map/attend/pallas_call | solution.py:206
  74.9 13.5 %all_to_all.21.r_ref = bf16[8,272,128]{2,1,0:T(8,128)(2,1)S(1)} all-to-all(bf16[8,272,128]{2,1,0:T(8,128)(2,1)S(1)} %attend.1), channel_id=1, replica_groups=mesh['zh'=4,'y'=8,'c'=2,'g'=2,'xl'=2,'zl'=2] {'c','xl','zl'}, dimensions={0} | all-to-all | bytes 1114112 | tf_op jit(solution)/shard_map/part_exchange/all_to_all | solution.py:250
  88.4 1.8 %combine.1 = (bf16[512,128]{1,0:T(8,128)(2,1)S(1)}, bf16[8,512,128]{2,1,0:T(8,128)(2,1)}) custom-call(bf16[8,272,128]{2,1,0:T(8,128)(2,1)S(1)} %all_to_all.21.r_ref), custom_call_target="tpu_custom_call" | custom-call | tf_op jit(solution)/shard_map/combine/pallas_call | solution.py:206
  90.1 4.0 %all-to-all-start.2 = ((bf16[8,512,128]{2,1,0:T(8,128)(2,1)}), bf16[8,512,128]{2,1,0:T(8,128)(2,1)S(1)}, u32[]{:S(2)}, u32[]{:S(2)}) async-start(bf16[8,512,128]{2,1,0:T(8,128)(2,1)} %get-tuple-element.8), calls=%async_computation.2 | async-start | bytes 2097152 | tf_op jit(solution)/shard_map/x_gather/all_to_all | solution.py:257
  94.2 1.9 %collective-permute-start.3 = (bf16[512,128]{1,0:T(8,128)(2,1)S(1)}, bf16[512,128]{1,0:T(8,128)(2,1)S(1)}, u32[]{:S(2)}, u32[]{:S(2)}) collective-permute-start(bf16[512,128]{1,0:T(8,128)(2,1)S(1)} %get-tuple-element.6.own_ref), channel_id=1, source_target_pairs={{0,8},{8,0},{1,9},{9,1},{2,10},{10,2},{3,11},{11,3},{4,12},{12,4},... | collective-permute-start | bytes 393224 | tf_op jit(solution)/shard_map/x_swap/ppermute | solution.py:255
  96.1 1.3 collective-permute-done.3.oth_ref
  97.4 1.5 %assemble.1 = (bf16[512,256]{1,0:T(8,128)(2,1)S(1)}, bf16[256,256]{1,0:T(8,128)(2,1)}) custom-call(s32[5]{0:T(128)S(1)} %stack.32.pos_ref, bf16[512,128]{1,0:T(8,128)(2,1)S(1)} %get-tuple-element.6.own_ref, bf16[512,128]{1,0:T(8,128)(2,1)S(1)} %collective-permute-done.3.oth_ref), custom_call_target="tpu_custom_call" | custom-call | flops 134217728 | bytes 1048576 | tf_op jit(solution)/shard_map/assemble/pallas_call | solution.py:206
  98.9 11.3 %all-to-all-done.2.r_ref = bf16[8,512,128]{2,1,0:T(8,128)(2,1)S(1)} async-done(((bf16[8,512,128]{2,1,0:T(8,128)(2,1)}), bf16[8,512,128]{2,1,0:T(8,128)(2,1)S(1)}, u32[]{:S(2)}, u32[]{:S(2)}) %all-to-all-start.2) | async-done | bytes 1048608 | tf_op jit(solution)/shard_map/x_gather/all_to_all | solution.py:257
  110.2 0.5 gram.1
  110.7 31.8 %all_to_all.22 = bf16[32,32,256]{2,1,0:T(8,128)(2,1)S(1)} all-to-all(bf16[32,32,256]{2,1,0:T(8,128)(2,1)S(1)} %gram.1), channel_id=1, replica_groups=mesh['zh'=4,'y'=8,'c'=2,'g'=2,'xl'=2,'zl'=2] {'zh','y'}, dimensions={0} | all-to-all | bytes 1048576 | tf_op jit(solution)/shard_map/h_exchange/all_to_all | solution.py:268
  142.5 0.1 convert_reduce_fusion
  142.6 0.6 broadcast_multiply_fusion
  (1 shorter events, 0.0 us)
Async XLA Ops:
  0.7 0.9 copy-start
  1.6 0.9 copy-start.1
  3.4 49.2 %copy-start.2 = (bf16[256,256]{1,0:T(8,128)(2,1)S(1)}, bf16[256,256]{1,0:T(8,128)(2,1)}, u32[]{:S(2)}) copy-start(bf16[256,256]{1,0:T(8,128)(2,1)} %q0_ref.1) | copy-start | bytes 393220
  50.7 19.6 %collective-permute-start.2 = (bf16[2048,256]{1,0:T(8,128)(2,1)S(1)}, bf16[2048,256]{1,0:T(8,128)(2,1)S(1)}, u32[]{:S(2)}, u32[]{:S(2)}) collective-permute-start(bf16[2048,256]{1,0:T(8,128)(2,1)S(1)} %bitcast.8), channel_id=1, source_target_pairs={{0,8},{8,0},{1,9},{9,1},{2,10},{10,2},{3,11},{11,3},{4,12},{12,4},... | collective-permute-start | bytes 3145736 | tf_op jit(solution)/shard_map/kv_swap/ppermute | solution.py:229
  52.6 7.8 %collective-permute-start = (bf16[256,256]{1,0:T(8,128)(2,1)S(1)}, bf16[256,256]{1,0:T(8,128)(2,1)S(1)}, u32[]{:S(2)}, u32[]{:S(2)}) collective-permute-start(bf16[256,256]{1,0:T(8,128)(2,1)S(1)} %copy-done.2), channel_id=1, source_target_pairs={{0,2},{2,0},{1,3},{3,1},{4,6},{6,4},{5,7},{7,5},{8,10},{10,8},{9,1... | collective-permute-start | bytes 393224 | tf_op jit(solution)/shard_map/q_gather/ppermute | solution.py:226
  60.5 9.8 %collective-permute-start.1 = (bf16[2,256,256]{2,1,0:T(8,128)(2,1)S(1)}, bf16[2,256,256]{2,1,0:T(8,128)(2,1)S(1)}, u32[]{:S(2)}, u32[]{:S(2)}) collective-permute-start(bf16[2,256,256]{2,1,0:T(8,128)(2,1)S(1)} %pad_maximum_fusion), channel_id=1, source_target_pairs={{0,1},{1,0},{2,3},{3,2},{4,5},{5,4},{6,7},{7,6},{8,9},{9,8},{10,11... | collective-permute-start | bytes 786440 | tf_op jit(solution)/shard_map/q_gather/ppermute | solution.py:227
  90.1 20.0 %all-to-all-start.2 = ((bf16[8,512,128]{2,1,0:T(8,128)(2,1)}), bf16[8,512,128]{2,1,0:T(8,128)(2,1)S(1)}, u32[]{:S(2)}, u32[]{:S(2)}) async-start(bf16[8,512,128]{2,1,0:T(8,128)(2,1)} %get-tuple-element.8), calls=%async_computation.2 | async-start | bytes 2097152 | tf_op jit(solution)/shard_map/x_gather/all_to_all | solution.py:257
  94.2 3.2 %collective-permute-start.3 = (bf16[512,128]{1,0:T(8,128)(2,1)S(1)}, bf16[512,128]{1,0:T(8,128)(2,1)S(1)}, u32[]{:S(2)}, u32[]{:S(2)}) collective-permute-start(bf16[512,128]{1,0:T(8,128)(2,1)S(1)} %get-tuple-element.6.own_ref), channel_id=1, source_target_pairs={{0,8},{8,0},{1,9},{9,1},{2,10},{10,2},{3,11},{11,3},{4,12},{12,4},... | collective-permute-start | bytes 393224 | tf_op jit(solution)/shard_map/x_swap/ppermute | solution.py:255

commit v3 on v2

v3 whole, which is shorter than its diff:
```python
import math

import jax
import jax.numpy as jnp
from jax import lax
from jax.experimental import pallas as pl
from jax.experimental.pallas import tpu as pltpu
from jax.sharding import Mesh
from jax.sharding import PartitionSpec as P

HEADS = 16
KVG = 2
HD = 128
TOKENS = 16384

CTX = ("zh", "yh", "b", "c")
HEAD = ("g", "xl", "zl")
CHIPS = ("zh", "yh", "b")
PAIRS = ("zh", "yh")
QUAD = ("b", "c")
SHARE = ("xl", "zl")
NZ, NY, NC, NS = 4, 8, 2, 4
NQ = 4
GRP = HD // NQ
TOK = 256
CUT = TOK // NS
TILE = NY * CUT
WIDE = NC * TILE
KEYS = NZ * TILE
ROWS = NS * TOK
PIECE = 256
SCALE = math.log2(math.e) / math.sqrt(HD)
LOW = -1e30
FLOOR = -1e29
STAT = 16
ABC = (((1,), (0,)), ((), ()))
ATB = (((0,), (0,)), ((), ()))


def dot(a, b, dims=ABC):
    return lax.dot_general(a, b, dims, preferred_element_type=jnp.float32)


def iota(shape, dim):
    return lax.broadcasted_iota(jnp.int32, shape, dim)


def spot(axes):
    return lax.axis_index(axes)


def prep_kernel(k_ref, v_ref, o_ref, kv_s, sems):
    rows = pl.ds(pl.multiple_of(spot(SHARE) * CUT, CUT), CUT)
    cols = pl.ds(pl.multiple_of(spot("g") * HD, HD), HD)
    copies = [
        pltpu.make_async_copy(ref.at[rows, cols], kv_s.at[i], sems.at[i])
        for i, ref in enumerate((k_ref, v_ref))
    ]
    for copy in copies:
        copy.start()
    for copy in copies:
        copy.wait()
    for i in range(NZ * NY):
        for a in range(2):
            o_ref[i, :, a * HD : (a + 1) * HD] = kv_s[a]


def attend_kernel(
    q0_ref, q1_ref, q2_ref, own_ref, oth_ref, o_ref, q_s, k_s, ve_s, s_s, mx_s, acc_s, st_s, o0_s
):
    zh, y, c, u = spot("zh"), spot(("yh", "b")), spot("c"), spot(SHARE)
    for zt in range(NZ):
        for a, kv_ref in enumerate((own_ref, oth_ref)):
            src = slice(zt * TILE, (zt + 1) * TILE)
            dst = slice(a * TILE, (a + 1) * TILE)
            k_s[zt, :, dst] = jnp.transpose(kv_ref[src, 0:HD])
            ve_s[zt, dst, 0:HD] = kv_ref[src, HD : 2 * HD]
            ve_s[zt, dst, HD : 2 * HD] = jnp.ones((TILE, HD), jnp.bfloat16)
    for hh in range(2):
        cols = slice(hh * HD, (hh + 1) * HD)
        for i, q in enumerate((q0_ref[:, cols], q1_ref[:, cols], q2_ref[0, :, cols], q2_ref[1, :, cols])):
            q_s[hh, i * TOK : (i + 1) * TOK, :] = q

    def body(zt, masked, new, old, top):
        if new is not None:
            q = q_s[new]
            m = mx_s[...]
        if old is not None:
            acc = acc_s[...]
        for p in range(WIDE // PIECE):
            at = slice(p * PIECE, (p + 1) * PIECE)
            if old is not None:
                w = jnp.exp2(s_s[zt, :, at] * SCALE - top).astype(jnp.bfloat16)
                acc = acc + dot(w, ve_s[zt, at, :])
            if new is not None:
                s = dot(q, k_s[zt, :, at])
                if masked:
                    n = iota((ROWS, PIECE), 1) + p * PIECE % TILE
                    r = iota((ROWS, PIECE), 0) % TOK
                    side = c if p * PIECE < TILE else 1 - c
                    k_pos = (n // CUT) * (2 * TOK) + n % CUT + side * TOK + u * CUT
                    s = jnp.where(k_pos <= r + (y * 2 + c) * TOK, s, LOW)
                s_s[zt, :, at] = s
                for i in range(PIECE // HD):
                    m = jnp.maximum(m, s[:, i * HD : (i + 1) * HD])
        if new is not None:
            mx_s[...] = m
        if old is not None:
            acc_s[...] = acc

    def sweep(new, old, top):
        if new is not None:
            mx_s[...] = jnp.full((ROWS, HD), LOW, jnp.float32)
        if old is not None:
            acc_s[...] = jnp.zeros((ROWS, 2 * HD), jnp.float32)

        def step(zt, _):
            body(zt, False, new, old, top)
            return 0

        lax.fori_loop(0, zh, step, 0)
        body(zh, True, new, old, top)

    def tops():
        return jnp.maximum(jnp.max(mx_s[...], axis=1, keepdims=True), FLOOR) * SCALE

    def finish(hh, top):
        total = acc_s[:, HD : 2 * HD]
        some = total > 0.0
        safe = jnp.where(some, total, 1.0)
        lse = jnp.where(some, top + jnp.log2(safe), LOW)
        hi = lse.astype(jnp.bfloat16).astype(jnp.float32)
        mid = (lse - hi).astype(jnp.bfloat16).astype(jnp.float32)
        lane = iota((ROWS, HD), 1) - 3 * hh
        parts = jnp.where(lane == 0, hi, jnp.where(lane == 1, mid, lse - hi - mid))
        return acc_s[:, 0:HD] / safe, parts

    sweep(0, None, None)
    top0 = tops()
    sweep(1, 0, top0)
    o0_s[...], st_s[...] = finish(0, top0)
    top1 = tops()
    sweep(None, 1, top1)
    o1, st1 = finish(1, top1)
    stats = jnp.where(iota((ROWS, HD), 1) < 3, st_s[...], st1)
    place = iota((TOK // 2, HD), 1) // GRP

    def swap(a, b, by):
        even = place // (by // GRP) % 2 == 0
        return (
            jnp.where(even, a, pltpu.roll(b, by, 1)),
            jnp.where(even, pltpu.roll(a, HD - by, 1), b),
        )

    for i in range(NS):
        up = u + (1 - 2 * (u // 2)) * 2 * (i % 2) + (1 - 2 * (u % 2)) * (i // 2)
        at = i * TOK
        mid, end = at + TOK // 2, at + TOK
        low0, low1 = swap(o0_s[at:mid], o1[at:mid], GRP)
        high0, high1 = swap(o0_s[mid:end], o1[mid:end], GRP)
        slots = [None] * NQ
        slots[0], slots[2] = swap(low0, high0, 2 * GRP)
        slots[1], slots[3] = swap(low1, high1, 2 * GRP)
        turned = jnp.transpose(stats[at:end])
        tail = jnp.concatenate([turned[0:8, 0:HD], turned[0:8, HD : 2 * HD]], axis=0)
        for k in range(NQ):
            o_ref[k * NS + up, 0:HD, :] = slots[k].astype(jnp.bfloat16)
            o_ref[k * NS + up, HD : HD + STAT, :] = tail.astype(jnp.bfloat16)


def combine_kernel(r_ref, x_ref, many_ref):
    place = iota((HD, HD), 1) // GRP
    turned = []
    for half in range(2):
        shares = []
        for k in range(NQ):
            for hh in range(2):
                lses = []
                for s in range(k * NS, (k + 1) * NS):
                    t = r_ref[s, HD : HD + STAT, :].astype(jnp.float32)
                    at = half * 8 + hh * 3
                    lses.append(t[at : at + 1] + t[at + 1 : at + 2] + t[at + 2 : at + 3])
                top = jnp.maximum(jnp.maximum(lses[0], lses[1]), jnp.maximum(lses[2], lses[3]))
                w = [jnp.exp2(lse - top) for lse in lses]
                inv = 1.0 / (w[0] + w[1] + w[2] + w[3])
                shares += [part * inv for part in w]
        shares.append(jnp.zeros((HD - len(shares), HD), jnp.float32))
        turned.append(jnp.transpose(jnp.concatenate(shares, axis=0)))
    for k in range(NQ):
        x = jnp.zeros((HD, HD), jnp.float32)
        for s in range(NS):
            at = k * 2 * NS + s
            w = [turned[i // 2][:, at + i % 2 * NS : at + i % 2 * NS + 1] for i in range(NQ)]
            w = jnp.where(place < 2, jnp.where(place == 0, w[0], w[1]), jnp.where(place == 2, w[2], w[3]))
            x = x + r_ref[k * NS + s, 0:HD, :].astype(jnp.float32) * w
        x = x.astype(jnp.bfloat16)
        rows = slice(k * HD, (k + 1) * HD)
        x_ref[rows, :] = x
        for i in range(8):
            many_ref[i, rows, :] = x


def assemble_kernel(x0_ref, x1_ref, x2_ref, x_ref, out_ref):
    b, c = spot("b"), spot("c")
    at, to = iota((HD, 2 * HD), 0), iota((HD, 2 * HD), 1)
    parts = ((x0_ref[...], b, c), (x1_ref[...], 1 - b, c), (x2_ref[0], b, 1 - c), (x2_ref[1], 1 - b, 1 - c))
    for half in range(2):
        x = jnp.zeros((NQ * HD, 2 * HD), jnp.float32)
        for part, pb, pc in parts:
            place = at - half * (HD // 2)
            col = place // GRP * HD + (pb * 2 + pc) * GRP + place % GRP
            pick = jnp.logical_and(at // (HD // 2) == half, to == col)
            x = x + dot(part, pick.astype(jnp.bfloat16))
        x_ref[half] = x.astype(jnp.bfloat16)
        mine = pl.ds(pl.multiple_of((b * 2 + c) * HD, HD), HD)
        out_ref[half * HD : (half + 1) * HD, :] = x_ref[half, mine, :]


def gram_kernel(r_ref, x_ref, h_ref):
    for i in range(8):
        part = dot(r_ref[i], x_ref[0], ATB)[0 : HD // 2] + dot(r_ref[i], x_ref[1], ATB)[HD // 2 : HD]
        h_ref[i * 2 : (i + 1) * 2] = part.astype(jnp.bfloat16).reshape(2, GRP, 2 * HD)


def call(kernel, name, outs, args, scratch=(), flops=0, moved=0, space=pltpu.VMEM, limit=40):
    return pl.pallas_call(
        kernel,
        out_shape=[jax.ShapeDtypeStruct(s, jnp.bfloat16) for s in outs],
        in_specs=[pl.BlockSpec(memory_space=space)] * len(args),
        out_specs=[pl.BlockSpec(memory_space=pltpu.VMEM)] * len(outs),
        scratch_shapes=list(scratch),
        compiler_params=pltpu.CompilerParams(vmem_limit_bytes=limit << 20),
        cost_estimate=pl.CostEstimate(flops=flops, bytes_accessed=moved, transcendentals=0),
        name=name,
    )(*args)


def local(queries, keys, values):
    swap = [(0, 1), (1, 0)]
    (own,) = call(
        prep_kernel,
        "prep",
        [(NZ * NY, CUT, 2 * HD)],
        (keys, values),
        (pltpu.VMEM((2, CUT, HD), jnp.bfloat16), pltpu.SemaphoreType.DMA((2,))),
        moved=1 << 20,
        space=pl.ANY,
        limit=60,
    )
    with jax.named_scope("q_gather"):
        q1 = lax.ppermute(queries, "xl", swap)
        q2 = lax.ppermute(jnp.stack([queries, q1]), "zl", swap)
    with jax.named_scope("kv_gather"):
        kv_own = lax.all_to_all(own, CHIPS, 0, 0)
        kv_own, q2 = lax.optimization_barrier((kv_own, q2))
        kv_own = kv_own.reshape(KEYS, 2 * HD)
    with jax.named_scope("kv_swap"):
        kv_oth = lax.ppermute(kv_own, "c", swap)
    f32, bf16 = jnp.float32, jnp.bfloat16
    scratch = (
        pltpu.VMEM((2, ROWS, HD), bf16),
        pltpu.VMEM((NZ, HD, WIDE), bf16),
        pltpu.VMEM((NZ, WIDE, 2 * HD), bf16),
        pltpu.VMEM((NZ, ROWS, WIDE), f32),
        pltpu.VMEM((ROWS, HD), f32),
        pltpu.VMEM((ROWS, 2 * HD), f32),
        pltpu.VMEM((ROWS, HD), f32),
        pltpu.VMEM((ROWS, HD), f32),
    )
    (part,) = call(
        attend_kernel,
        "attend",
        [(NQ * NS, HD + STAT, HD)],
        (queries, q1, q2, kv_own, kv_oth),
        scratch,
        flops=1 << 33,
    )
    with jax.named_scope("part_exchange"):
        parts = lax.all_to_all(part, QUAD + SHARE, 0, 0)
    x0, x_many = call(combine_kernel, "combine", [(NQ * HD, HD), (8, NQ * HD, HD)], (parts,))
    with jax.named_scope("x_swap"):
        x1 = lax.ppermute(x0, "b", swap)
        x2 = lax.ppermute(jnp.stack([x0, x1]), "c", swap)
    with jax.named_scope("x_gather"):
        x_all = lax.all_to_all(x_many, HEAD, 0, 0)
    x, attn_out = call(
        assemble_kernel,
        "assemble",
        [(2, NQ * HD, 2 * HD), (TOK, 2 * HD)],
        (x0, x1, x2),
        flops=1 << 28,
        moved=1 << 20,
    )
    (gram,) = call(gram_kernel, "gram", [(NZ * NY // 2, GRP, 2 * HD)], (x_all, x))
    with jax.named_scope("h_exchange"):
        h_parts = lax.all_to_all(gram, PAIRS, 0, 0)
    hessian = jnp.sum(h_parts.astype(jnp.float32), axis=0) * (2.0 / TOKENS)
    return attn_out, hessian


def solution(mesh):
    cut = Mesh(mesh.devices.reshape(NZ, NY // 2, 2, NC, 2, 2, 2), CTX + HEAD)
    in_specs = (P(CTX, HEAD), P(CTX, None), P(CTX, None))
    out_specs = (P(CTX, HEAD), P(CTX, HEAD))
    return jax.shard_map(local, mesh=cut, in_specs=in_specs, out_specs=out_specs, check_vma=False)
```

time: 144 us -> 128 us (0.89)
  the two profiles are of different devices: /device:TPU:8 before, /device:TPU:1 now
where the time goes in v3:
time: 128 us
  blocking collectives  44.9 us (35%)
  waiting for transfers between devices  36 us (28%)
  starting transfers between devices  34.7 us (27%)
  Pallas kernels  10.7 us (8%)
    all_to_all x1, blocking collectives, local(): h_parts = lax.all_to_all(gram, PAIRS, 0, 0)  29.4 us
    ppermute x1, waiting for transfers between devices, local(): q2 = lax.ppermute(jnp.stack([queries, q1]), 'zl', swap)  22.8 us
    all_to_all x1, starting transfers between devices, local(): kv_own = lax.all_to_all(own, CHIPS, 0, 0)  16.7 us
    all_to_all x1, blocking collectives, local(): parts = lax.all_to_all(part, QUAD + SHARE, 0, 0)  15.5 us
    pallas_call x5, Pallas kernels, call(): pl.pallas_call(kernel, out_shape=[jax.ShapeDtypeStruct(s, jnp.bfloat16) f...  10.7 us
    ppermute x1, waiting for transfers between devices, local(): x1 = lax.ppermute(x0, 'b', swap)  4.02 us
    all_to_all x1, starting transfers between devices, local(): x_all = lax.all_to_all(x_many, HEAD, 0, 0)  3.73 us
    ppermute x1, starting transfers between devices, local(): x2 = lax.ppermute(jnp.stack([x0, x1]), 'c', swap)  3.46 us
  transfers between devices with their start and end apart: 7, of which 6 were waited for; matrix products, arithmetic and copies ran while one was open for 0% of the time, Pallas kernels for 1%

profile of v3, /device:TPU:1, one launch (start us, length us, event | category | flops | bytes accessed | tf_op | source)
XLA Modules:
  0.0 127.7 jit_solution(4893809292155410749)
XLA Ops:
  0.6 1.9 %prep.1 = bf16[32,64,256]{2,1,0:T(8,128)(2,1)} custom-call(bf16[256,256]{1,0:T(8,128)(2,1)} %k_ref.1, bf16[256,256]{1,0:T(8,128)(2,1)} %v_ref.1), custom_call_target="tpu_custom_call" | custom-call | bytes 1048576 | tf_op jit(solution)/shard_map/prep/pallas_call | solution.py:226
  2.5 0.0 copy-start
  2.5 16.7 %all-to-all-start = ((bf16[32,64,256]{2,1,0:T(8,128)(2,1)}), bf16[32,64,256]{2,1,0:T(8,128)(2,1)S(1)}, u32[]{:S(2)}, u32[]{:S(2)}) async-start(bf16[32,64,256]{2,1,0:T(8,128)(2,1)} %prep.1), calls=%async_computation | async-start | bytes 2097152 | tf_op jit(solution)/shard_map/kv_gather/all_to_all | solution.py:254
  19.2 0.0 copy-done
  19.2 3.1 %collective-permute-start = (bf16[256,256]{1,0:T(8,128)(2,1)S(1)}, bf16[256,256]{1,0:T(8,128)(2,1)S(1)}, u32[]{:S(2)}, u32[]{:S(2)}) collective-permute-start(bf16[256,256]{1,0:T(8,128)(2,1)S(1)} %copy-done), channel_id=1, source_target_pairs={{0,2},{2,0},{1,3},{3,1},{4,6},{6,4},{5,7},{7,5},{8,10},{10,8},{9,1... | collective-permute-start | bytes 393224 | tf_op jit(solution)/shard_map/q_gather/ppermute | solution.py:251
  22.3 2.9 %collective-permute-done.q1_ref = bf16[256,256]{1,0:T(8,128)(2,1)S(1)} collective-permute-done((bf16[256,256]{1,0:T(8,128)(2,1)S(1)}, bf16[256,256]{1,0:T(8,128)(2,1)S(1)}, u32[]{:S(2)}, u32[]{:S(2)}) %collective-permute-start) | collective-permute-done | bytes 131104 | tf_op jit(solution)/shard_map/q_gather/ppermute | solution.py:251
  25.2 3.1 %collective-permute-start.1 = (bf16[2,256,256]{2,1,0:T(8,128)(2,1)S(1)}, bf16[2,256,256]{2,1,0:T(8,128)(2,1)S(1)}, u32[]{:S(2)}, u32[]{:S(2)}) collective-permute-start(bf16[2,256,256]{2,1,0:T(8,128)(2,1)S(1)} %pad_maximum_fusion), channel_id=1, source_target_pairs={{0,1},{1,0},{2,3},{3,2},{4,5},{5,4},{6,7},{7,6},{8,9},{9,8},{10,11... | collective-permute-start | bytes 786440 | tf_op jit(solution)/shard_map/q_gather/ppermute | solution.py:252
  28.3 22.8 %collective-permute-done.1.q2_ref = bf16[2,256,256]{2,1,0:T(8,128)(2,1)S(1)} collective-permute-done((bf16[2,256,256]{2,1,0:T(8,128)(2,1)S(1)}, bf16[2,256,256]{2,1,0:T(8,128)(2,1)S(1)}, u32[]{:S(2)}, u32[]{:S(2)}) %collective-permute-start.1) | collective-permute-done | bytes 262176 | tf_op jit(solution)/shard_map/q_gather/ppermute | solution.py:252
  51.1 0.0 all-to-all-done
  51.1 2.4 %collective-permute-start.2 = (bf16[2048,256]{1,0:T(8,128)(2,1)S(1)}, bf16[2048,256]{1,0:T(8,128)(2,1)S(1)}, u32[]{:S(2)}, u32[]{:S(2)}) collective-permute-start(bf16[2048,256]{1,0:T(8,128)(2,1)S(1)} %bitcast.5), channel_id=1, source_target_pairs={{0,8},{8,0},{1,9},{9,1},{2,10},{10,2},{3,11},{11,3},{4,12},{12,4},... | collective-permute-start | bytes 3145736 | tf_op jit(solution)/shard_map/kv_swap/ppermute | solution.py:258
  53.5 2.3 %collective-permute-done.2.oth_ref = bf16[2048,256]{1,0:T(8,128)(2,1)S(1)} collective-permute-done((bf16[2048,256]{1,0:T(8,128)(2,1)S(1)}, bf16[2048,256]{1,0:T(8,128)(2,1)S(1)}, u32[]{:S(2)}, u32[]{:S(2)}) %collective-permute-start.2) | collective-permute-done | bytes 1048608 | tf_op jit(solution)/shard_map/kv_swap/ppermute | solution.py:258
  55.8 4.3 %attend.1 = bf16[16,144,128]{2,1,0:T(8,128)(2,1)S(1)} custom-call(bf16[256,256]{1,0:T(8,128)(2,1)S(1)} %copy-done, bf16[256,256]{1,0:T(8,128)(2,1)S(1)} %collective-permute-done.q1_ref, bf16[2,256,256]{2,1,0:T(8,128)(2,1)S(1)} %collective-permute-done.1.q2_ref, bf16[2048,256]{1,0:T(8,128)(2,1)S(1)} %bitcast.6, ...), custom_call_target="tpu_custom_call" | custom-call | flops 8589934592 | tf_op jit(solution)/shard_map/attend/pallas_call | solution.py:226
  60.1 15.5 %all_to_all.20.r_ref = bf16[16,144,128]{2,1,0:T(8,128)(2,1)S(1)} all-to-all(bf16[16,144,128]{2,1,0:T(8,128)(2,1)S(1)} %attend.1), channel_id=1, replica_groups=mesh['zh'=4,'yh'=4,'b'=2,'c'=2,'g'=2,'xl'=2,'zl'=2] {'b','c','xl','zl'}, dimensions={0} | all-to-all | bytes 1179648 | tf_op jit(solution)/shard_map/part_exchange/all_to_all | solution.py:279
  75.7 2.4 %combine.1 = (bf16[512,128]{1,0:T(8,128)(2,1)S(1)}, bf16[8,512,128]{2,1,0:T(8,128)(2,1)}) custom-call(bf16[16,144,128]{2,1,0:T(8,128)(2,1)S(1)} %all_to_all.20.r_ref), custom_call_target="tpu_custom_call" | custom-call | tf_op jit(solution)/shard_map/combine/pallas_call | solution.py:226
  78.1 3.7 %all-to-all-start.2 = ((bf16[8,512,128]{2,1,0:T(8,128)(2,1)}), bf16[8,512,128]{2,1,0:T(8,128)(2,1)S(1)}, u32[]{:S(2)}, u32[]{:S(2)}) async-start(bf16[8,512,128]{2,1,0:T(8,128)(2,1)} %get-tuple-element.12), calls=%async_computation.2 | async-start | bytes 2097152 | tf_op jit(solution)/shard_map/x_gather/all_to_all | solution.py:285
  81.8 2.2 %collective-permute-start.3 = (bf16[512,128]{1,0:T(8,128)(2,1)S(1)}, bf16[512,128]{1,0:T(8,128)(2,1)S(1)}, u32[]{:S(2)}, u32[]{:S(2)}) collective-permute-start(bf16[512,128]{1,0:T(8,128)(2,1)S(1)} %get-tuple-element.10.x0_ref), channel_id=1, source_target_pairs={{0,16},{16,0},{1,17},{17,1},{2,18},{18,2},{3,19},{19,3},{4,20},{20... | collective-permute-start | bytes 393224 | tf_op jit(solution)/shard_map/x_swap/ppermute | solution.py:282
  84.0 4.0 %collective-permute-done.3.x1_ref = bf16[512,128]{1,0:T(8,128)(2,1)S(1)} collective-permute-done((bf16[512,128]{1,0:T(8,128)(2,1)S(1)}, bf16[512,128]{1,0:T(8,128)(2,1)S(1)}, u32[]{:S(2)}, u32[]{:S(2)}) %collective-permute-start.3) | collective-permute-done | bytes 131104 | tf_op jit(solution)/shard_map/x_swap/ppermute | solution.py:282
  88.1 3.5 %collective-permute-start.4 = (bf16[2,512,128]{2,1,0:T(8,128)(2,1)S(1)}, bf16[2,512,128]{2,1,0:T(8,128)(2,1)S(1)}, u32[]{:S(2)}, u32[]{:S(2)}) collective-permute-start(bf16[2,512,128]{2,1,0:T(8,128)(2,1)S(1)} %pad_maximum_fusion.1), channel_id=1, source_target_pairs={{0,8},{8,0},{1,9},{9,1},{2,10},{10,2},{3,11},{11,3},{4,12},{12,4},... | collective-permute-start | bytes 786440 | tf_op jit(solution)/shard_map/x_swap/ppermute | solution.py:283
  91.5 1.1 collective-permute-done.4.x2_ref
  92.7 1.4 %assemble.1 = (bf16[2,512,256]{2,1,0:T(8,128)(2,1)S(1)}, bf16[256,256]{1,0:T(8,128)(2,1)}) custom-call(bf16[512,128]{1,0:T(8,128)(2,1)S(1)} %get-tuple-element.10.x0_ref, bf16[512,128]{1,0:T(8,128)(2,1)S(1)} %collective-permute-done.3.x1_ref, bf16[2,512,128]{2,1,0:T(8,128)(2,1)S(1)} %collective-permute-done.4.x2_ref), custom_call_target="tpu_custom_call" | custom-call | flops 268435456 | bytes 1048576 | tf_op jit(solution)/shard_map/assemble/pallas_call | solution.py:226
  94.1 2.9 %all-to-all-done.2.r_ref = bf16[8,512,128]{2,1,0:T(8,128)(2,1)S(1)} async-done(((bf16[8,512,128]{2,1,0:T(8,128)(2,1)}), bf16[8,512,128]{2,1,0:T(8,128)(2,1)S(1)}, u32[]{:S(2)}, u32[]{:S(2)}) %all-to-all-start.2) | async-done | bytes 1048608 | tf_op jit(solution)/shard_map/x_gather/all_to_all | solution.py:285
  97.0 0.8 gram.1
  97.7 29.4 %all_to_all.21 = bf16[16,32,256]{2,1,0:T(8,128)(2,1)S(1)} all-to-all(bf16[16,32,256]{2,1,0:T(8,128)(2,1)S(1)} %gram.1), channel_id=1, replica_groups=mesh['zh'=4,'yh'=4,'b'=2,'c'=2,'g'=2,'xl'=2,'zl'=2] {'zh','yh'}, dimensions={0} | all-to-all | bytes 524288 | tf_op jit(solution)/shard_map/h_exchange/all_to_all | solution.py:296
  127.1 0.6 broadcast_multiply_fusion
  (3 shorter events, 0.1 us)
Async XLA Ops:
  2.5 16.7 %copy-start = (bf16[256,256]{1,0:T(8,128)(2,1)S(1)}, bf16[256,256]{1,0:T(8,128)(2,1)}, u32[]{:S(2)}) copy-start(bf16[256,256]{1,0:T(8,128)(2,1)} %q0_ref.1) | copy-start | bytes 393220
  2.5 48.6 %all-to-all-start = ((bf16[32,64,256]{2,1,0:T(8,128)(2,1)}), bf16[32,64,256]{2,1,0:T(8,128)(2,1)S(1)}, u32[]{:S(2)}, u32[]{:S(2)}) async-start(bf16[32,64,256]{2,1,0:T(8,128)(2,1)} %prep.1), calls=%async_computation | async-start | bytes 2097152 | tf_op jit(solution)/shard_map/kv_gather/all_to_all | solution.py:254
  19.2 6.0 %collective-permute-start = (bf16[256,256]{1,0:T(8,128)(2,1)S(1)}, bf16[256,256]{1,0:T(8,128)(2,1)S(1)}, u32[]{:S(2)}, u32[]{:S(2)}) collective-permute-start(bf16[256,256]{1,0:T(8,128)(2,1)S(1)} %copy-done), channel_id=1, source_target_pairs={{0,2},{2,0},{1,3},{3,1},{4,6},{6,4},{5,7},{7,5},{8,10},{10,8},{9,1... | collective-permute-start | bytes 393224 | tf_op jit(solution)/shard_map/q_gather/ppermute | solution.py:251
  25.2 25.9 %collective-permute-start.1 = (bf16[2,256,256]{2,1,0:T(8,128)(2,1)S(1)}, bf16[2,256,256]{2,1,0:T(8,128)(2,1)S(1)}, u32[]{:S(2)}, u32[]{:S(2)}) collective-permute-start(bf16[2,256,256]{2,1,0:T(8,128)(2,1)S(1)} %pad_maximum_fusion), channel_id=1, source_target_pairs={{0,1},{1,0},{2,3},{3,2},{4,5},{5,4},{6,7},{7,6},{8,9},{9,8},{10,11... | collective-permute-start | bytes 786440 | tf_op jit(solution)/shard_map/q_gather/ppermute | solution.py:252
  51.1 4.7 %collective-permute-start.2 = (bf16[2048,256]{1,0:T(8,128)(2,1)S(1)}, bf16[2048,256]{1,0:T(8,128)(2,1)S(1)}, u32[]{:S(2)}, u32[]{:S(2)}) collective-permute-start(bf16[2048,256]{1,0:T(8,128)(2,1)S(1)} %bitcast.5), channel_id=1, source_target_pairs={{0,8},{8,0},{1,9},{9,1},{2,10},{10,2},{3,11},{11,3},{4,12},{12,4},... | collective-permute-start | bytes 3145736 | tf_op jit(solution)/shard_map/kv_swap/ppermute | solution.py:258
  78.1 18.9 %all-to-all-start.2 = ((bf16[8,512,128]{2,1,0:T(8,128)(2,1)}), bf16[8,512,128]{2,1,0:T(8,128)(2,1)S(1)}, u32[]{:S(2)}, u32[]{:S(2)}) async-start(bf16[8,512,128]{2,1,0:T(8,128)(2,1)} %get-tuple-element.12), calls=%async_computation.2 | async-start | bytes 2097152 | tf_op jit(solution)/shard_map/x_gather/all_to_all | solution.py:285
  81.8 6.2 %collective-permute-start.3 = (bf16[512,128]{1,0:T(8,128)(2,1)S(1)}, bf16[512,128]{1,0:T(8,128)(2,1)S(1)}, u32[]{:S(2)}, u32[]{:S(2)}) collective-permute-start(bf16[512,128]{1,0:T(8,128)(2,1)S(1)} %get-tuple-element.10.x0_ref), channel_id=1, source_target_pairs={{0,16},{16,0},{1,17},{17,1},{2,18},{18,2},{3,19},{19,3},{4,20},{20... | collective-permute-start | bytes 393224 | tf_op jit(solution)/shard_map/x_swap/ppermute | solution.py:282
  88.1 4.6 %collective-permute-start.4 = (bf16[2,512,128]{2,1,0:T(8,128)(2,1)S(1)}, bf16[2,512,128]{2,1,0:T(8,128)(2,1)S(1)}, u32[]{:S(2)}, u32[]{:S(2)}) collective-permute-start(bf16[2,512,128]{2,1,0:T(8,128)(2,1)S(1)} %pad_maximum_fusion.1), channel_id=1, source_target_pairs={{0,8},{8,0},{1,9},{9,1},{2,10},{10,2},{3,11},{11,3},{4,12},{12,4},... | collective-permute-start | bytes 786440 | tf_op jit(solution)/shard_map/x_swap/ppermute | solution.py:283

commit v4 on v3

--- a/solution.py
+++ b/solution.py
@@ -169,29 +169,28 @@
 
 
 def combine_kernel(r_ref, x_ref, many_ref):
-    place = iota((HD, HD), 1) // GRP
-    turned = []
-    for half in range(2):
-        shares = []
-        for k in range(NQ):
-            for hh in range(2):
-                lses = []
-                for s in range(k * NS, (k + 1) * NS):
-                    t = r_ref[s, HD : HD + STAT, :].astype(jnp.float32)
-                    at = half * 8 + hh * 3
-                    lses.append(t[at : at + 1] + t[at + 1 : at + 2] + t[at + 2 : at + 3])
-                top = jnp.maximum(jnp.maximum(lses[0], lses[1]), jnp.maximum(lses[2], lses[3]))
-                w = [jnp.exp2(lse - top) for lse in lses]
-                inv = 1.0 / (w[0] + w[1] + w[2] + w[3])
-                shares += [part * inv for part in w]
-        shares.append(jnp.zeros((HD - len(shares), HD), jnp.float32))
-        turned.append(jnp.transpose(jnp.concatenate(shares, axis=0)))
+    row = iota((STAT, HD), 0)
+    lanes = jnp.logical_and(row % NQ == iota((STAT, HD), 1) // GRP, row < 3 * NQ).astype(jnp.bfloat16)
     for k in range(NQ):
+        shares = [[] for _ in range(NS)]
+        for place in range(NQ):
+            lses = []
+            for s in range(k * NS, (k + 1) * NS):
+                at = HD + place // 2 * 8 + place % 2 * 3
+                t = r_ref[s, HD : HD + STAT, :].astype(jnp.float32)[at - HD : at - HD + 3]
+                lses.append(t[0:1] + t[1:2] + t[2:3])
+            top = jnp.maximum(jnp.maximum(lses[0], lses[1]), jnp.maximum(lses[2], lses[3]))
+            w = [jnp.exp2(lse - top) for lse in lses]
+            inv = 1.0 / (w[0] + w[1] + w[2] + w[3])
+            for s in range(NS):
+                shares[s].append(w[s] * inv)
         x = jnp.zeros((HD, HD), jnp.float32)
         for s in range(NS):
-            at = k * 2 * NS + s
-            w = [turned[i // 2][:, at + i % 2 * NS : at + i % 2 * NS + 1] for i in range(NQ)]
-            w = jnp.where(place < 2, jnp.where(place == 0, w[0], w[1]), jnp.where(place == 2, w[2], w[3]))
+            w = jnp.concatenate(shares[s], axis=0)
+            hi = w.astype(jnp.bfloat16).astype(jnp.float32)
+            mid = (w - hi).astype(jnp.bfloat16).astype(jnp.float32)
+            lever = jnp.concatenate([hi, mid, w - hi - mid, jnp.zeros_like(w)], axis=0)
+            w = dot(lever.astype(jnp.bfloat16), lanes, ATB)
             x = x + r_ref[k * NS + s, 0:HD, :].astype(jnp.float32) * w
         x = x.astype(jnp.bfloat16)
         rows = slice(k * HD, (k + 1) * HD)

time: 128 us -> 127 us (level)
  no operation moved by 1% of the time
where the time goes in v4:
time: 127 us
  blocking collectives  44.9 us (35%)
  waiting for transfers between devices  36 us (28%)
  starting transfers between devices  34.7 us (27%)
  Pallas kernels  9.68 us (8%)
    all_to_all x1, blocking collectives, local(): h_parts = lax.all_to_all(gram, PAIRS, 0, 0)  29.4 us
    ppermute x1, waiting for transfers between devices, local(): q2 = lax.ppermute(jnp.stack([queries, q1]), 'zl', swap)  22.8 us
    all_to_all x1, starting transfers between devices, local(): kv_own = lax.all_to_all(own, CHIPS, 0, 0)  16.7 us
    all_to_all x1, blocking collectives, local(): parts = lax.all_to_all(part, QUAD + SHARE, 0, 0)  15.5 us
    pallas_call x5, Pallas kernels, call(): pl.pallas_call(kernel, out_shape=[jax.ShapeDtypeStruct(s, jnp.bfloat16) f...  9.68 us
    ppermute x1, waiting for transfers between devices, local(): x1 = lax.ppermute(x0, 'b', swap)  4.02 us
    all_to_all x1, starting transfers between devices, local(): x_all = lax.all_to_all(x_many, HEAD, 0, 0)  3.73 us
    ppermute x1, starting transfers between devices, local(): x2 = lax.ppermute(jnp.stack([x0, x1]), 'c', swap)  3.46 us
  transfers between devices with their start and end apart: 7, of which 6 were waited for; matrix products, arithmetic and copies ran while one was open for 0% of the time, Pallas kernels for 1%

profile of v4, /device:TPU:1, one launch (start us, length us, event | category | flops | bytes accessed | tf_op | source)
XLA Modules:
  0.0 126.7 jit_solution(4610933447894780030)
XLA Ops:
  0.6 1.9 %prep.1 = bf16[32,64,256]{2,1,0:T(8,128)(2,1)} custom-call(bf16[256,256]{1,0:T(8,128)(2,1)} %k_ref.1, bf16[256,256]{1,0:T(8,128)(2,1)} %v_ref.1), custom_call_target="tpu_custom_call" | custom-call | bytes 1048576 | tf_op jit(solution)/shard_map/prep/pallas_call | solution.py:225
  2.5 0.0 copy-start
  2.5 16.7 %all-to-all-start = ((bf16[32,64,256]{2,1,0:T(8,128)(2,1)}), bf16[32,64,256]{2,1,0:T(8,128)(2,1)S(1)}, u32[]{:S(2)}, u32[]{:S(2)}) async-start(bf16[32,64,256]{2,1,0:T(8,128)(2,1)} %prep.1), calls=%async_computation | async-start | bytes 2097152 | tf_op jit(solution)/shard_map/kv_gather/all_to_all | solution.py:253
  19.2 0.0 copy-done
  19.2 3.1 %collective-permute-start = (bf16[256,256]{1,0:T(8,128)(2,1)S(1)}, bf16[256,256]{1,0:T(8,128)(2,1)S(1)}, u32[]{:S(2)}, u32[]{:S(2)}) collective-permute-start(bf16[256,256]{1,0:T(8,128)(2,1)S(1)} %copy-done), channel_id=1, source_target_pairs={{0,2},{2,0},{1,3},{3,1},{4,6},{6,4},{5,7},{7,5},{8,10},{10,8},{9,1... | collective-permute-start | bytes 393224 | tf_op jit(solution)/shard_map/q_gather/ppermute | solution.py:250
  22.3 2.9 %collective-permute-done.q1_ref = bf16[256,256]{1,0:T(8,128)(2,1)S(1)} collective-permute-done((bf16[256,256]{1,0:T(8,128)(2,1)S(1)}, bf16[256,256]{1,0:T(8,128)(2,1)S(1)}, u32[]{:S(2)}, u32[]{:S(2)}) %collective-permute-start) | collective-permute-done | bytes 131104 | tf_op jit(solution)/shard_map/q_gather/ppermute | solution.py:250
  25.2 3.1 %collective-permute-start.1 = (bf16[2,256,256]{2,1,0:T(8,128)(2,1)S(1)}, bf16[2,256,256]{2,1,0:T(8,128)(2,1)S(1)}, u32[]{:S(2)}, u32[]{:S(2)}) collective-permute-start(bf16[2,256,256]{2,1,0:T(8,128)(2,1)S(1)} %pad_maximum_fusion), channel_id=1, source_target_pairs={{0,1},{1,0},{2,3},{3,2},{4,5},{5,4},{6,7},{7,6},{8,9},{9,8},{10,11... | collective-permute-start | bytes 786440 | tf_op jit(solution)/shard_map/q_gather/ppermute | solution.py:251
  28.3 22.8 %collective-permute-done.1.q2_ref = bf16[2,256,256]{2,1,0:T(8,128)(2,1)S(1)} collective-permute-done((bf16[2,256,256]{2,1,0:T(8,128)(2,1)S(1)}, bf16[2,256,256]{2,1,0:T(8,128)(2,1)S(1)}, u32[]{:S(2)}, u32[]{:S(2)}) %collective-permute-start.1) | collective-permute-done | bytes 262176 | tf_op jit(solution)/shard_map/q_gather/ppermute | solution.py:251
  51.1 0.0 all-to-all-done
  51.1 2.4 %collective-permute-start.2 = (bf16[2048,256]{1,0:T(8,128)(2,1)S(1)}, bf16[2048,256]{1,0:T(8,128)(2,1)S(1)}, u32[]{:S(2)}, u32[]{:S(2)}) collective-permute-start(bf16[2048,256]{1,0:T(8,128)(2,1)S(1)} %bitcast.5), channel_id=1, source_target_pairs={{0,8},{8,0},{1,9},{9,1},{2,10},{10,2},{3,11},{11,3},{4,12},{12,4},... | collective-permute-start | bytes 3145736 | tf_op jit(solution)/shard_map/kv_swap/ppermute | solution.py:257
  53.5 2.3 %collective-permute-done.2.oth_ref = bf16[2048,256]{1,0:T(8,128)(2,1)S(1)} collective-permute-done((bf16[2048,256]{1,0:T(8,128)(2,1)S(1)}, bf16[2048,256]{1,0:T(8,128)(2,1)S(1)}, u32[]{:S(2)}, u32[]{:S(2)}) %collective-permute-start.2) | collective-permute-done | bytes 1048608 | tf_op jit(solution)/shard_map/kv_swap/ppermute | solution.py:257
  55.8 4.3 %attend.1 = bf16[16,144,128]{2,1,0:T(8,128)(2,1)S(1)} custom-call(bf16[256,256]{1,0:T(8,128)(2,1)S(1)} %copy-done, bf16[256,256]{1,0:T(8,128)(2,1)S(1)} %collective-permute-done.q1_ref, bf16[2,256,256]{2,1,0:T(8,128)(2,1)S(1)} %collective-permute-done.1.q2_ref, bf16[2048,256]{1,0:T(8,128)(2,1)S(1)} %bitcast.6, ...), custom_call_target="tpu_custom_call" | custom-call | flops 8589934592 | tf_op jit(solution)/shard_map/attend/pallas_call | solution.py:225
  60.1 15.5 %all_to_all.20.r_ref = bf16[16,144,128]{2,1,0:T(8,128)(2,1)S(1)} all-to-all(bf16[16,144,128]{2,1,0:T(8,128)(2,1)S(1)} %attend.1), channel_id=1, replica_groups=mesh['zh'=4,'yh'=4,'b'=2,'c'=2,'g'=2,'xl'=2,'zl'=2] {'b','c','xl','zl'}, dimensions={0} | all-to-all | bytes 1179648 | tf_op jit(solution)/shard_map/part_exchange/all_to_all | solution.py:278
  75.7 1.4 %combine.1 = (bf16[512,128]{1,0:T(8,128)(2,1)S(1)}, bf16[8,512,128]{2,1,0:T(8,128)(2,1)}) custom-call(bf16[16,144,128]{2,1,0:T(8,128)(2,1)S(1)} %all_to_all.20.r_ref), custom_call_target="tpu_custom_call" | custom-call | tf_op jit(solution)/shard_map/combine/pallas_call | solution.py:225
  77.0 3.7 %all-to-all-start.2 = ((bf16[8,512,128]{2,1,0:T(8,128)(2,1)}), bf16[8,512,128]{2,1,0:T(8,128)(2,1)S(1)}, u32[]{:S(2)}, u32[]{:S(2)}) async-start(bf16[8,512,128]{2,1,0:T(8,128)(2,1)} %get-tuple-element.12), calls=%async_computation.2 | async-start | bytes 2097152 | tf_op jit(solution)/shard_map/x_gather/all_to_all | solution.py:284
  80.8 2.2 %collective-permute-start.3 = (bf16[512,128]{1,0:T(8,128)(2,1)S(1)}, bf16[512,128]{1,0:T(8,128)(2,1)S(1)}, u32[]{:S(2)}, u32[]{:S(2)}) collective-permute-start(bf16[512,128]{1,0:T(8,128)(2,1)S(1)} %get-tuple-element.10.x0_ref), channel_id=1, source_target_pairs={{0,16},{16,0},{1,17},{17,1},{2,18},{18,2},{3,19},{19,3},{4,20},{20... | collective-permute-start | bytes 393224 | tf_op jit(solution)/shard_map/x_swap/ppermute | solution.py:281
  83.0 4.0 %collective-permute-done.3.x1_ref = bf16[512,128]{1,0:T(8,128)(2,1)S(1)} collective-permute-done((bf16[512,128]{1,0:T(8,128)(2,1)S(1)}, bf16[512,128]{1,0:T(8,128)(2,1)S(1)}, u32[]{:S(2)}, u32[]{:S(2)}) %collective-permute-start.3) | collective-permute-done | bytes 131104 | tf_op jit(solution)/shard_map/x_swap/ppermute | solution.py:281
  87.0 3.5 %collective-permute-start.4 = (bf16[2,512,128]{2,1,0:T(8,128)(2,1)S(1)}, bf16[2,512,128]{2,1,0:T(8,128)(2,1)S(1)}, u32[]{:S(2)}, u32[]{:S(2)}) collective-permute-start(bf16[2,512,128]{2,1,0:T(8,128)(2,1)S(1)} %pad_maximum_fusion.1), channel_id=1, source_target_pairs={{0,8},{8,0},{1,9},{9,1},{2,10},{10,2},{3,11},{11,3},{4,12},{12,4},... | collective-permute-start | bytes 786440 | tf_op jit(solution)/shard_map/x_swap/ppermute | solution.py:282
  90.5 1.1 collective-permute-done.4.x2_ref
  91.6 1.4 %assemble.1 = (bf16[2,512,256]{2,1,0:T(8,128)(2,1)S(1)}, bf16[256,256]{1,0:T(8,128)(2,1)}) custom-call(bf16[512,128]{1,0:T(8,128)(2,1)S(1)} %get-tuple-element.10.x0_ref, bf16[512,128]{1,0:T(8,128)(2,1)S(1)} %collective-permute-done.3.x1_ref, bf16[2,512,128]{2,1,0:T(8,128)(2,1)S(1)} %collective-permute-done.4.x2_ref), custom_call_target="tpu_custom_call" | custom-call | flops 268435456 | bytes 1048576 | tf_op jit(solution)/shard_map/assemble/pallas_call | solution.py:225
  93.0 2.9 %all-to-all-done.2.r_ref = bf16[8,512,128]{2,1,0:T(8,128)(2,1)S(1)} async-done(((bf16[8,512,128]{2,1,0:T(8,128)(2,1)}), bf16[8,512,128]{2,1,0:T(8,128)(2,1)S(1)}, u32[]{:S(2)}, u32[]{:S(2)}) %all-to-all-start.2) | async-done | bytes 1048608 | tf_op jit(solution)/shard_map/x_gather/all_to_all | solution.py:284
  95.9 0.8 gram.1
  96.7 29.4 %all_to_all.21 = bf16[16,32,256]{2,1,0:T(8,128)(2,1)S(1)} all-to-all(bf16[16,32,256]{2,1,0:T(8,128)(2,1)S(1)} %gram.1), channel_id=1, replica_groups=mesh['zh'=4,'yh'=4,'b'=2,'c'=2,'g'=2,'xl'=2,'zl'=2] {'zh','yh'}, dimensions={0} | all-to-all | bytes 524288 | tf_op jit(solution)/shard_map/h_exchange/all_to_all | solution.py:295
  126.1 0.6 broadcast_multiply_fusion
  (3 shorter events, 0.1 us)
Async XLA Ops:
  2.5 16.7 %copy-start = (bf16[256,256]{1,0:T(8,128)(2,1)S(1)}, bf16[256,256]{1,0:T(8,128)(2,1)}, u32[]{:S(2)}) copy-start(bf16[256,256]{1,0:T(8,128)(2,1)} %q0_ref.1) | copy-start | bytes 393220
  2.5 48.6 %all-to-all-start = ((bf16[32,64,256]{2,1,0:T(8,128)(2,1)}), bf16[32,64,256]{2,1,0:T(8,128)(2,1)S(1)}, u32[]{:S(2)}, u32[]{:S(2)}) async-start(bf16[32,64,256]{2,1,0:T(8,128)(2,1)} %prep.1), calls=%async_computation | async-start | bytes 2097152 | tf_op jit(solution)/shard_map/kv_gather/all_to_all | solution.py:253
  19.2 6.0 %collective-permute-start = (bf16[256,256]{1,0:T(8,128)(2,1)S(1)}, bf16[256,256]{1,0:T(8,128)(2,1)S(1)}, u32[]{:S(2)}, u32[]{:S(2)}) collective-permute-start(bf16[256,256]{1,0:T(8,128)(2,1)S(1)} %copy-done), channel_id=1, source_target_pairs={{0,2},{2,0},{1,3},{3,1},{4,6},{6,4},{5,7},{7,5},{8,10},{10,8},{9,1... | collective-permute-start | bytes 393224 | tf_op jit(solution)/shard_map/q_gather/ppermute | solution.py:250
  25.2 25.9 %collective-permute-start.1 = (bf16[2,256,256]{2,1,0:T(8,128)(2,1)S(1)}, bf16[2,256,256]{2,1,0:T(8,128)(2,1)S(1)}, u32[]{:S(2)}, u32[]{:S(2)}) collective-permute-start(bf16[2,256,256]{2,1,0:T(8,128)(2,1)S(1)} %pad_maximum_fusion), channel_id=1, source_target_pairs={{0,1},{1,0},{2,3},{3,2},{4,5},{5,4},{6,7},{7,6},{8,9},{9,8},{10,11... | collective-permute-start | bytes 786440 | tf_op jit(solution)/shard_map/q_gather/ppermute | solution.py:251
  51.1 4.7 %collective-permute-start.2 = (bf16[2048,256]{1,0:T(8,128)(2,1)S(1)}, bf16[2048,256]{1,0:T(8,128)(2,1)S(1)}, u32[]{:S(2)}, u32[]{:S(2)}) collective-permute-start(bf16[2048,256]{1,0:T(8,128)(2,1)S(1)} %bitcast.5), channel_id=1, source_target_pairs={{0,8},{8,0},{1,9},{9,1},{2,10},{10,2},{3,11},{11,3},{4,12},{12,4},... | collective-permute-start | bytes 3145736 | tf_op jit(solution)/shard_map/kv_swap/ppermute | solution.py:257
  77.0 18.9 %all-to-all-start.2 = ((bf16[8,512,128]{2,1,0:T(8,128)(2,1)}), bf16[8,512,128]{2,1,0:T(8,128)(2,1)S(1)}, u32[]{:S(2)}, u32[]{:S(2)}) async-start(bf16[8,512,128]{2,1,0:T(8,128)(2,1)} %get-tuple-element.12), calls=%async_computation.2 | async-start | bytes 2097152 | tf_op jit(solution)/shard_map/x_gather/all_to_all | solution.py:284
  80.8 6.2 %collective-permute-start.3 = (bf16[512,128]{1,0:T(8,128)(2,1)S(1)}, bf16[512,128]{1,0:T(8,128)(2,1)S(1)}, u32[]{:S(2)}, u32[]{:S(2)}) collective-permute-start(bf16[512,128]{1,0:T(8,128)(2,1)S(1)} %get-tuple-element.10.x0_ref), channel_id=1, source_target_pairs={{0,16},{16,0},{1,17},{17,1},{2,18},{18,2},{3,19},{19,3},{4,20},{20... | collective-permute-start | bytes 393224 | tf_op jit(solution)/shard_map/x_swap/ppermute | solution.py:281
  87.0 4.6 %collective-permute-start.4 = (bf16[2,512,128]{2,1,0:T(8,128)(2,1)S(1)}, bf16[2,512,128]{2,1,0:T(8,128)(2,1)S(1)}, u32[]{:S(2)}, u32[]{:S(2)}) collective-permute-start(bf16[2,512,128]{2,1,0:T(8,128)(2,1)S(1)} %pad_maximum_fusion.1), channel_id=1, source_target_pairs={{0,8},{8,0},{1,9},{9,1},{2,10},{10,2},{3,11},{11,3},{4,12},{12,4},... | collective-permute-start | bytes 786440 | tf_op jit(solution)/shard_map/x_swap/ppermute | solution.py:282

commit v5 on v4

--- a/solution.py
+++ b/solution.py
@@ -18,7 +18,7 @@
 CHIPS = ("zh", "yh", "b")
 PAIRS = ("zh", "yh")
 QUAD = ("b", "c")
-SHARE = ("xl", "zl")
+SHARE = ("b", "xl")
 NZ, NY, NC, NS = 4, 8, 2, 4
 NQ = 4
 GRP = HD // NQ
@@ -50,25 +50,25 @@
 
 
 def prep_kernel(k_ref, v_ref, o_ref, kv_s, sems):
-    rows = pl.ds(pl.multiple_of(spot(SHARE) * CUT, CUT), CUT)
     cols = pl.ds(pl.multiple_of(spot("g") * HD, HD), HD)
-    copies = [
-        pltpu.make_async_copy(ref.at[rows, cols], kv_s.at[i], sems.at[i])
-        for i, ref in enumerate((k_ref, v_ref))
-    ]
+    copies = []
+    for b in range(2):
+        rows = pl.ds(pl.multiple_of((b * 2 + spot("xl")) * CUT, CUT), CUT)
+        for i, ref in enumerate((k_ref, v_ref)):
+            copies.append(pltpu.make_async_copy(ref.at[rows, cols], kv_s.at[b, i], sems.at[b, i]))
     for copy in copies:
         copy.start()
     for copy in copies:
         copy.wait()
     for i in range(NZ * NY):
         for a in range(2):
-            o_ref[i, :, a * HD : (a + 1) * HD] = kv_s[a]
+            o_ref[i, :, a * HD : (a + 1) * HD] = kv_s[i % 2, a]
 
 
 def attend_kernel(
     q0_ref, q1_ref, q2_ref, own_ref, oth_ref, o_ref, q_s, k_s, ve_s, s_s, mx_s, acc_s, st_s, o0_s
 ):
-    zh, y, c, u = spot("zh"), spot(("yh", "b")), spot("c"), spot(SHARE)
+    zh, yh, b, c, u, xl = spot("zh"), spot("yh"), spot("b"), spot("c"), spot(SHARE), spot("xl")
     for zt in range(NZ):
         for a, kv_ref in enumerate((own_ref, oth_ref)):
             src = slice(zt * TILE, (zt + 1) * TILE)
@@ -96,10 +96,11 @@
                 s = dot(q, k_s[zt, :, at])
                 if masked:
                     n = iota((ROWS, PIECE), 1) + p * PIECE % TILE
-                    r = iota((ROWS, PIECE), 0) % TOK
+                    r = iota((ROWS, PIECE), 0)
+                    r = r % TOK + jnp.where(r // (2 * TOK) == 0, b, 1 - b) * (NC * TOK)
                     side = c if p * PIECE < TILE else 1 - c
                     k_pos = (n // CUT) * (2 * TOK) + n % CUT + side * TOK + u * CUT
-                    s = jnp.where(k_pos <= r + (y * 2 + c) * TOK, s, LOW)
+                    s = jnp.where(k_pos <= r + (yh * 2 * NC + c) * TOK, s, LOW)
                 s_s[zt, :, at] = s
                 for i in range(PIECE // HD):
                     m = jnp.maximum(m, s[:, i * HD : (i + 1) * HD])
@@ -153,7 +154,10 @@
         )
 
     for i in range(NS):
-        up = u + (1 - 2 * (u // 2)) * 2 * (i % 2) + (1 - 2 * (u % 2)) * (i // 2)
+        to_x = xl + (1 - 2 * xl) * (i % 2)
+        to_b = b + (1 - 2 * b) * (i // 2)
+        rows = pl.ds(pl.multiple_of(to_b * HD, HD), HD)
+        tails = pl.ds(pl.multiple_of(2 * HD + to_b * STAT, STAT), STAT)
         at = i * TOK
         mid, end = at + TOK // 2, at + TOK
         low0, low1 = swap(o0_s[at:mid], o1[at:mid], GRP)
@@ -164,20 +168,22 @@
         turned = jnp.transpose(stats[at:end])
         tail = jnp.concatenate([turned[0:8, 0:HD], turned[0:8, HD : 2 * HD]], axis=0)
         for k in range(NQ):
-            o_ref[k * NS + up, 0:HD, :] = slots[k].astype(jnp.bfloat16)
-            o_ref[k * NS + up, HD : HD + STAT, :] = tail.astype(jnp.bfloat16)
+            o_ref[k * 2 + to_x, rows, :] = slots[k].astype(jnp.bfloat16)
+            o_ref[k * 2 + to_x, tails, :] = tail.astype(jnp.bfloat16)
 
 
 def combine_kernel(r_ref, x_ref, many_ref):
     row = iota((STAT, HD), 0)
     lanes = jnp.logical_and(row % NQ == iota((STAT, HD), 1) // GRP, row < 3 * NQ).astype(jnp.bfloat16)
     for k in range(NQ):
+        sources = [(s // 2 * NC + k % NC) * 2 + s % 2 for s in range(NS)]
+        first, stat = k // NC * HD, 2 * HD + k // NC * STAT
         shares = [[] for _ in range(NS)]
         for place in range(NQ):
             lses = []
-            for s in range(k * NS, (k + 1) * NS):
-                at = HD + place // 2 * 8 + place % 2 * 3
-                t = r_ref[s, HD : HD + STAT, :].astype(jnp.float32)[at - HD : at - HD + 3]
+            for s in sources:
+                at = place // 2 * 8 + place % 2 * 3
+                t = r_ref[s, stat : stat + STAT, :].astype(jnp.float32)[at : at + 3]
                 lses.append(t[0:1] + t[1:2] + t[2:3])
             top = jnp.maximum(jnp.maximum(lses[0], lses[1]), jnp.maximum(lses[2], lses[3]))
             w = [jnp.exp2(lse - top) for lse in lses]
@@ -191,7 +197,7 @@
             mid = (w - hi).astype(jnp.bfloat16).astype(jnp.float32)
             lever = jnp.concatenate([hi, mid, w - hi - mid, jnp.zeros_like(w)], axis=0)
             w = dot(lever.astype(jnp.bfloat16), lanes, ATB)
-            x = x + r_ref[k * NS + s, 0:HD, :].astype(jnp.float32) * w
+            x = x + r_ref[sources[s], first : first + HD, :].astype(jnp.float32) * w
         x = x.astype(jnp.bfloat16)
         rows = slice(k * HD, (k + 1) * HD)
         x_ref[rows, :] = x
@@ -241,14 +247,14 @@
         "prep",
         [(NZ * NY, CUT, 2 * HD)],
         (keys, values),
-        (pltpu.VMEM((2, CUT, HD), jnp.bfloat16), pltpu.SemaphoreType.DMA((2,))),
+        (pltpu.VMEM((2, 2, CUT, HD), jnp.bfloat16), pltpu.SemaphoreType.DMA((2, 2))),
         moved=1 << 20,
         space=pl.ANY,
         limit=60,
     )
     with jax.named_scope("q_gather"):
         q1 = lax.ppermute(queries, "xl", swap)
-        q2 = lax.ppermute(jnp.stack([queries, q1]), "zl", swap)
+        q2 = lax.ppermute(jnp.stack([queries, q1]), "b", swap)
     with jax.named_scope("kv_gather"):
         kv_own = lax.all_to_all(own, CHIPS, 0, 0)
         kv_own, q2 = lax.optimization_barrier((kv_own, q2))
@@ -269,13 +275,13 @@
     (part,) = call(
         attend_kernel,
         "attend",
-        [(NQ * NS, HD + STAT, HD)],
+        [(NQ * 2, 2 * (HD + STAT), HD)],
         (queries, q1, q2, kv_own, kv_oth),
         scratch,
         flops=1 << 33,
     )
     with jax.named_scope("part_exchange"):
-        parts = lax.all_to_all(part, QUAD + SHARE, 0, 0)
+        parts = lax.all_to_all(part, QUAD + ("xl",), 0, 0)
     x0, x_many = call(combine_kernel, "combine", [(NQ * HD, HD), (8, NQ * HD, HD)], (parts,))
     with jax.named_scope("x_swap"):
         x1 = lax.ppermute(x0, "b", swap)

time: 127 us -> 125 us (0.984)
  starting transfers between devices: 34.7 us -> 37.2 us
  waiting for transfers between devices: 36 us -> 33.6 us
  blocking collectives: 44.9 us -> 42.9 us
    ppermute x1, waiting for transfers between devices: 22.8 us -> 20.5 us  [local(): q2 = lax.ppermute(jnp.stack([queries, q1]), 'b', swap)]
    ppermute x1, starting transfers between devices: 2.39 us -> 3.74 us  [local(): kv_oth = lax.ppermute(kv_own, 'c', swap)]
    all_to_all x1, blocking collectives: 15.5 us -> 14.2 us  [local(): parts = lax.all_to_all(part, QUAD + ('xl',), 0, 0)]
where the time goes in v5:
time: 125 us
  blocking collectives  42.9 us (34%)
  starting transfers between devices  37.2 us (30%)
  waiting for transfers between devices  33.6 us (27%)
  Pallas kernels  9.66 us (8%)
    all_to_all x1, blocking collectives, local(): h_parts = lax.all_to_all(gram, PAIRS, 0, 0)  28.7 us
    ppermute x1, waiting for transfers between devices, local(): q2 = lax.ppermute(jnp.stack([queries, q1]), 'b', swap)  20.5 us
    all_to_all x1, starting transfers between devices, local(): kv_own = lax.all_to_all(own, CHIPS, 0, 0)  16.7 us
    all_to_all x1, blocking collectives, local(): parts = lax.all_to_all(part, QUAD + ('xl',), 0, 0)  14.2 us
    pallas_call x5, Pallas kernels, call(): pl.pallas_call(kernel, out_shape=[jax.ShapeDtypeStruct(s, jnp.bfloat16) f...  9.66 us
    all_to_all x1, starting transfers between devices, local(): x_all = lax.all_to_all(x_many, HEAD, 0, 0)  4.82 us
    ppermute x1, waiting for transfers between devices, local(): x1 = lax.ppermute(x0, 'b', swap)  3.97 us
    ppermute x1, starting transfers between devices, local(): kv_oth = lax.ppermute(kv_own, 'c', swap)  3.74 us
  transfers between devices with their start and end apart: 7, of which 6 were waited for; matrix products, arithmetic and copies ran while one was open for 0% of the time, Pallas kernels for 1%

profile of v5, /device:TPU:1, one launch (start us, length us, event | category | flops | bytes accessed | tf_op | source)
XLA Modules:
  0.0 124.8 jit_solution(2478074752157035584)
XLA Ops:
  0.6 1.9 %prep.1 = bf16[32,64,256]{2,1,0:T(8,128)(2,1)} custom-call(bf16[256,256]{1,0:T(8,128)(2,1)} %k_ref.1, bf16[256,256]{1,0:T(8,128)(2,1)} %v_ref.1), custom_call_target="tpu_custom_call" | custom-call | bytes 1048576 | tf_op jit(solution)/shard_map/prep/pallas_call | solution.py:231
  2.6 0.0 copy-start
  2.6 16.7 %all-to-all-start = ((bf16[32,64,256]{2,1,0:T(8,128)(2,1)}), bf16[32,64,256]{2,1,0:T(8,128)(2,1)S(1)}, u32[]{:S(2)}, u32[]{:S(2)}) async-start(bf16[32,64,256]{2,1,0:T(8,128)(2,1)} %prep.1), calls=%async_computation | async-start | bytes 2097152 | tf_op jit(solution)/shard_map/kv_gather/all_to_all | solution.py:259
  19.2 0.0 copy-done
  19.2 3.1 %collective-permute-start = (bf16[256,256]{1,0:T(8,128)(2,1)S(1)}, bf16[256,256]{1,0:T(8,128)(2,1)S(1)}, u32[]{:S(2)}, u32[]{:S(2)}) collective-permute-start(bf16[256,256]{1,0:T(8,128)(2,1)S(1)} %copy-done), channel_id=1, source_target_pairs={{0,2},{2,0},{1,3},{3,1},{4,6},{6,4},{5,7},{7,5},{8,10},{10,8},{9,1... | collective-permute-start | bytes 393224 | tf_op jit(solution)/shard_map/q_gather/ppermute | solution.py:256
  22.4 2.9 %collective-permute-done.q1_ref = bf16[256,256]{1,0:T(8,128)(2,1)S(1)} collective-permute-done((bf16[256,256]{1,0:T(8,128)(2,1)S(1)}, bf16[256,256]{1,0:T(8,128)(2,1)S(1)}, u32[]{:S(2)}, u32[]{:S(2)}) %collective-permute-start) | collective-permute-done | bytes 131104 | tf_op jit(solution)/shard_map/q_gather/ppermute | solution.py:256
  25.3 3.1 %collective-permute-start.1 = (bf16[2,256,256]{2,1,0:T(8,128)(2,1)S(1)}, bf16[2,256,256]{2,1,0:T(8,128)(2,1)S(1)}, u32[]{:S(2)}, u32[]{:S(2)}) collective-permute-start(bf16[2,256,256]{2,1,0:T(8,128)(2,1)S(1)} %pad_maximum_fusion), channel_id=1, source_target_pairs={{0,16},{16,0},{1,17},{17,1},{2,18},{18,2},{3,19},{19,3},{4,20},{20... | collective-permute-start | bytes 786440 | tf_op jit(solution)/shard_map/q_gather/ppermute | solution.py:257
  28.4 20.5 %collective-permute-done.1.q2_ref = bf16[2,256,256]{2,1,0:T(8,128)(2,1)S(1)} collective-permute-done((bf16[2,256,256]{2,1,0:T(8,128)(2,1)S(1)}, bf16[2,256,256]{2,1,0:T(8,128)(2,1)S(1)}, u32[]{:S(2)}, u32[]{:S(2)}) %collective-permute-start.1) | collective-permute-done | bytes 262176 | tf_op jit(solution)/shard_map/q_gather/ppermute | solution.py:257
  48.9 0.0 all-to-all-done
  48.9 3.7 %collective-permute-start.2 = (bf16[2048,256]{1,0:T(8,128)(2,1)S(1)}, bf16[2048,256]{1,0:T(8,128)(2,1)S(1)}, u32[]{:S(2)}, u32[]{:S(2)}) collective-permute-start(bf16[2048,256]{1,0:T(8,128)(2,1)S(1)} %bitcast.5), channel_id=1, source_target_pairs={{0,8},{8,0},{1,9},{9,1},{2,10},{10,2},{3,11},{11,3},{4,12},{12,4},... | collective-permute-start | bytes 3145736 | tf_op jit(solution)/shard_map/kv_swap/ppermute | solution.py:263
  52.6 2.3 %collective-permute-done.2.oth_ref = bf16[2048,256]{1,0:T(8,128)(2,1)S(1)} collective-permute-done((bf16[2048,256]{1,0:T(8,128)(2,1)S(1)}, bf16[2048,256]{1,0:T(8,128)(2,1)S(1)}, u32[]{:S(2)}, u32[]{:S(2)}) %collective-permute-start.2) | collective-permute-done | bytes 1048608 | tf_op jit(solution)/shard_map/kv_swap/ppermute | solution.py:263
  54.9 4.2 %attend.1 = bf16[8,288,128]{2,1,0:T(8,128)(2,1)S(1)} custom-call(bf16[256,256]{1,0:T(8,128)(2,1)S(1)} %copy-done, bf16[256,256]{1,0:T(8,128)(2,1)S(1)} %collective-permute-done.q1_ref, bf16[2,256,256]{2,1,0:T(8,128)(2,1)S(1)} %collective-permute-done.1.q2_ref, bf16[2048,256]{1,0:T(8,128)(2,1)S(1)} %bitcast.6, ...), custom_call_target="tpu_custom_call" | custom-call | flops 8589934592 | tf_op jit(solution)/shard_map/attend/pallas_call | solution.py:231
  59.1 14.2 %all_to_all.20.r_ref = bf16[8,288,128]{2,1,0:T(8,128)(2,1)S(1)} all-to-all(bf16[8,288,128]{2,1,0:T(8,128)(2,1)S(1)} %attend.1), channel_id=1, replica_groups=mesh['zh'=4,'yh'=4,'b'=2,'c'=2,'g'=2,'xl'=2,'zl'=2] {'b','c','xl'}, dimensions={0} | all-to-all | bytes 1179648 | tf_op jit(solution)/shard_map/part_exchange/all_to_all | solution.py:284
  73.3 1.4 %combine.1 = (bf16[512,128]{1,0:T(8,128)(2,1)S(1)}, bf16[8,512,128]{2,1,0:T(8,128)(2,1)}) custom-call(bf16[8,288,128]{2,1,0:T(8,128)(2,1)S(1)} %all_to_all.20.r_ref), custom_call_target="tpu_custom_call" | custom-call | tf_op jit(solution)/shard_map/combine/pallas_call | solution.py:231
  74.7 4.8 %all-to-all-start.2 = ((bf16[8,512,128]{2,1,0:T(8,128)(2,1)}), bf16[8,512,128]{2,1,0:T(8,128)(2,1)S(1)}, u32[]{:S(2)}, u32[]{:S(2)}) async-start(bf16[8,512,128]{2,1,0:T(8,128)(2,1)} %get-tuple-element.12), calls=%async_computation.2 | async-start | bytes 2097152 | tf_op jit(solution)/shard_map/x_gather/all_to_all | solution.py:290
  79.5 2.3 %collective-permute-start.3 = (bf16[512,128]{1,0:T(8,128)(2,1)S(1)}, bf16[512,128]{1,0:T(8,128)(2,1)S(1)}, u32[]{:S(2)}, u32[]{:S(2)}) collective-permute-start(bf16[512,128]{1,0:T(8,128)(2,1)S(1)} %get-tuple-element.10.x0_ref), channel_id=1, source_target_pairs={{0,16},{16,0},{1,17},{17,1},{2,18},{18,2},{3,19},{19,3},{4,20},{20... | collective-permute-start | bytes 393224 | tf_op jit(solution)/shard_map/x_swap/ppermute | solution.py:287
  81.8 4.0 %collective-permute-done.3.x1_ref = bf16[512,128]{1,0:T(8,128)(2,1)S(1)} collective-permute-done((bf16[512,128]{1,0:T(8,128)(2,1)S(1)}, bf16[512,128]{1,0:T(8,128)(2,1)S(1)}, u32[]{:S(2)}, u32[]{:S(2)}) %collective-permute-start.3) | collective-permute-done | bytes 131104 | tf_op jit(solution)/shard_map/x_swap/ppermute | solution.py:287
  85.8 3.5 %collective-permute-start.4 = (bf16[2,512,128]{2,1,0:T(8,128)(2,1)S(1)}, bf16[2,512,128]{2,1,0:T(8,128)(2,1)S(1)}, u32[]{:S(2)}, u32[]{:S(2)}) collective-permute-start(bf16[2,512,128]{2,1,0:T(8,128)(2,1)S(1)} %pad_maximum_fusion.1), channel_id=1, source_target_pairs={{0,8},{8,0},{1,9},{9,1},{2,10},{10,2},{3,11},{11,3},{4,12},{12,4},... | collective-permute-start | bytes 786440 | tf_op jit(solution)/shard_map/x_swap/ppermute | solution.py:288
  89.3 1.1 collective-permute-done.4.x2_ref
  90.4 1.4 %assemble.1 = (bf16[2,512,256]{2,1,0:T(8,128)(2,1)S(1)}, bf16[256,256]{1,0:T(8,128)(2,1)}) custom-call(bf16[512,128]{1,0:T(8,128)(2,1)S(1)} %get-tuple-element.10.x0_ref, bf16[512,128]{1,0:T(8,128)(2,1)S(1)} %collective-permute-done.3.x1_ref, bf16[2,512,128]{2,1,0:T(8,128)(2,1)S(1)} %collective-permute-done.4.x2_ref), custom_call_target="tpu_custom_call" | custom-call | flops 268435456 | bytes 1048576 | tf_op jit(solution)/shard_map/assemble/pallas_call | solution.py:231
  91.8 2.9 %all-to-all-done.2.r_ref = bf16[8,512,128]{2,1,0:T(8,128)(2,1)S(1)} async-done(((bf16[8,512,128]{2,1,0:T(8,128)(2,1)}), bf16[8,512,128]{2,1,0:T(8,128)(2,1)S(1)}, u32[]{:S(2)}, u32[]{:S(2)}) %all-to-all-start.2) | async-done | bytes 1048608 | tf_op jit(solution)/shard_map/x_gather/all_to_all | solution.py:290
  94.7 0.8 gram.1
  95.4 28.7 %all_to_all.21 = bf16[16,32,256]{2,1,0:T(8,128)(2,1)S(1)} all-to-all(bf16[16,32,256]{2,1,0:T(8,128)(2,1)S(1)} %gram.1), channel_id=1, replica_groups=mesh['zh'=4,'yh'=4,'b'=2,'c'=2,'g'=2,'xl'=2,'zl'=2] {'zh','yh'}, dimensions={0} | all-to-all | bytes 524288 | tf_op jit(solution)/shard_map/h_exchange/all_to_all | solution.py:301
  124.2 0.6 broadcast_multiply_fusion
  (3 shorter events, 0.1 us)
Async XLA Ops:
  2.6 16.7 %copy-start = (bf16[256,256]{1,0:T(8,128)(2,1)S(1)}, bf16[256,256]{1,0:T(8,128)(2,1)}, u32[]{:S(2)}) copy-start(bf16[256,256]{1,0:T(8,128)(2,1)} %q0_ref.1) | copy-start | bytes 393220
  2.6 46.3 %all-to-all-start = ((bf16[32,64,256]{2,1,0:T(8,128)(2,1)}), bf16[32,64,256]{2,1,0:T(8,128)(2,1)S(1)}, u32[]{:S(2)}, u32[]{:S(2)}) async-start(bf16[32,64,256]{2,1,0:T(8,128)(2,1)} %prep.1), calls=%async_computation | async-start | bytes 2097152 | tf_op jit(solution)/shard_map/kv_gather/all_to_all | solution.py:259
  19.2 6.0 %collective-permute-start = (bf16[256,256]{1,0:T(8,128)(2,1)S(1)}, bf16[256,256]{1,0:T(8,128)(2,1)S(1)}, u32[]{:S(2)}, u32[]{:S(2)}) collective-permute-start(bf16[256,256]{1,0:T(8,128)(2,1)S(1)} %copy-done), channel_id=1, source_target_pairs={{0,2},{2,0},{1,3},{3,1},{4,6},{6,4},{5,7},{7,5},{8,10},{10,8},{9,1... | collective-permute-start | bytes 393224 | tf_op jit(solution)/shard_map/q_gather/ppermute | solution.py:256
  25.3 23.6 %collective-permute-start.1 = (bf16[2,256,256]{2,1,0:T(8,128)(2,1)S(1)}, bf16[2,256,256]{2,1,0:T(8,128)(2,1)S(1)}, u32[]{:S(2)}, u32[]{:S(2)}) collective-permute-start(bf16[2,256,256]{2,1,0:T(8,128)(2,1)S(1)} %pad_maximum_fusion), channel_id=1, source_target_pairs={{0,16},{16,0},{1,17},{17,1},{2,18},{18,2},{3,19},{19,3},{4,20},{20... | collective-permute-start | bytes 786440 | tf_op jit(solution)/shard_map/q_gather/ppermute | solution.py:257
  48.9 6.0 %collective-permute-start.2 = (bf16[2048,256]{1,0:T(8,128)(2,1)S(1)}, bf16[2048,256]{1,0:T(8,128)(2,1)S(1)}, u32[]{:S(2)}, u32[]{:S(2)}) collective-permute-start(bf16[2048,256]{1,0:T(8,128)(2,1)S(1)} %bitcast.5), channel_id=1, source_target_pairs={{0,8},{8,0},{1,9},{9,1},{2,10},{10,2},{3,11},{11,3},{4,12},{12,4},... | collective-permute-start | bytes 3145736 | tf_op jit(solution)/shard_map/kv_swap/ppermute | solution.py:263
  74.7 20.0 %all-to-all-start.2 = ((bf16[8,512,128]{2,1,0:T(8,128)(2,1)}), bf16[8,512,128]{2,1,0:T(8,128)(2,1)S(1)}, u32[]{:S(2)}, u32[]{:S(2)}) async-start(bf16[8,512,128]{2,1,0:T(8,128)(2,1)} %get-tuple-element.12), calls=%async_computation.2 | async-start | bytes 2097152 | tf_op jit(solution)/shard_map/x_gather/all_to_all | solution.py:290
  79.5 6.2 %collective-permute-start.3 = (bf16[512,128]{1,0:T(8,128)(2,1)S(1)}, bf16[512,128]{1,0:T(8,128)(2,1)S(1)}, u32[]{:S(2)}, u32[]{:S(2)}) collective-permute-start(bf16[512,128]{1,0:T(8,128)(2,1)S(1)} %get-tuple-element.10.x0_ref), channel_id=1, source_target_pairs={{0,16},{16,0},{1,17},{17,1},{2,18},{18,2},{3,19},{19,3},{4,20},{20... | collective-permute-start | bytes 393224 | tf_op jit(solution)/shard_map/x_swap/ppermute | solution.py:287
  85.8 4.6 %collective-permute-start.4 = (bf16[2,512,128]{2,1,0:T(8,128)(2,1)S(1)}, bf16[2,512,128]{2,1,0:T(8,128)(2,1)S(1)}, u32[]{:S(2)}, u32[]{:S(2)}) collective-permute-start(bf16[2,512,128]{2,1,0:T(8,128)(2,1)S(1)} %pad_maximum_fusion.1), channel_id=1, source_target_pairs={{0,8},{8,0},{1,9},{9,1},{2,10},{10,2},{3,11},{11,3},{4,12},{12,4},... | collective-permute-start | bytes 786440 | tf_op jit(solution)/shard_map/x_swap/ppermute | solution.py:288

commit v6 on v5

--- a/solution.py
+++ b/solution.py
@@ -25,10 +25,10 @@
 TOK = 256
 CUT = TOK // NS
 TILE = NY * CUT
-WIDE = NC * TILE
 KEYS = NZ * TILE
 ROWS = NS * TOK
 PIECE = 256
+PIECES = TILE // PIECE
 SCALE = math.log2(math.e) / math.sqrt(HD)
 LOW = -1e30
 FLOOR = -1e29
@@ -65,45 +65,77 @@
             o_ref[i, :, a * HD : (a + 1) * HD] = kv_s[i % 2, a]
 
 
+def lay_keys(kv_ref, k_ref, ve_ref):
+    for zt in range(NZ):
+        src = slice(zt * TILE, (zt + 1) * TILE)
+        k_ref[zt] = jnp.transpose(kv_ref[src, 0:HD])
+        ve_ref[zt, :, 0:HD] = kv_ref[src, HD : 2 * HD]
+        ve_ref[zt, :, HD : 2 * HD] = jnp.ones((TILE, HD), jnp.bfloat16)
+
+
+def score(q, k_ref, zt, p, side, masked):
+    s = dot(q, k_ref[zt, :, p * PIECE : (p + 1) * PIECE])
+    if masked:
+        b, c = spot("b"), spot("c")
+        n = iota((ROWS, PIECE), 1) + p * PIECE
+        r = iota((ROWS, PIECE), 0)
+        r = r % TOK + jnp.where(r // (2 * TOK) == 0, b, 1 - b) * (NC * TOK)
+        k_pos = (n // CUT) * (2 * TOK) + n % CUT + side * TOK + spot(SHARE) * CUT
+        s = jnp.where(k_pos <= r + (spot("yh") * 2 * NC + c) * TOK, s, LOW)
+    return s
+
+
+def highest(m, s):
+    for i in range(PIECE // HD):
+        m = jnp.maximum(m, s[:, i * HD : (i + 1) * HD])
+    return m
+
+
+def begin_kernel(near_ref, far_ref, kv_ref, q_ref, k_ref, ve_ref, s_ref, mx_ref):
+    lay_keys(kv_ref, k_ref, ve_ref)
+    for hh in range(2):
+        for i in range(NS):
+            part_ref = (near_ref, far_ref)[i // 2]
+            q_ref[hh, i * TOK : (i + 1) * TOK, :] = part_ref[i % 2, :, hh * HD : (hh + 1) * HD]
+    mx_ref[...] = jnp.full((ROWS, HD), LOW, jnp.float32)
+
+    def body(zt, masked):
+        q = q_ref[0]
+        m = mx_ref[...]
+        for p in range(PIECES):
+            s = score(q, k_ref, zt, p, spot("c"), masked)
+            s_ref[zt, :, p * PIECE : (p + 1) * PIECE] = s
+            m = highest(m, s)
+        mx_ref[...] = m
+
+    lax.fori_loop(0, spot("zh"), lambda zt, _: (body(zt, False), 0)[1], 0)
+    body(spot("zh"), True)
+
+
 def attend_kernel(
-    q0_ref, q1_ref, q2_ref, own_ref, oth_ref, o_ref, q_s, k_s, ve_s, s_s, mx_s, acc_s, st_s, o0_s
+    q_ref, k0_ref, ve0_ref, s0_ref, mx0_ref, oth_ref, o_ref, k1_s, ve1_s, s_s, mx_s, acc_s, st_s, o0_s
 ):
-    zh, yh, b, c, u, xl = spot("zh"), spot("yh"), spot("b"), spot("c"), spot(SHARE), spot("xl")
-    for zt in range(NZ):
-        for a, kv_ref in enumerate((own_ref, oth_ref)):
-            src = slice(zt * TILE, (zt + 1) * TILE)
-            dst = slice(a * TILE, (a + 1) * TILE)
-            k_s[zt, :, dst] = jnp.transpose(kv_ref[src, 0:HD])
-            ve_s[zt, dst, 0:HD] = kv_ref[src, HD : 2 * HD]
-            ve_s[zt, dst, HD : 2 * HD] = jnp.ones((TILE, HD), jnp.bfloat16)
-    for hh in range(2):
-        cols = slice(hh * HD, (hh + 1) * HD)
-        for i, q in enumerate((q0_ref[:, cols], q1_ref[:, cols], q2_ref[0, :, cols], q2_ref[1, :, cols])):
-            q_s[hh, i * TOK : (i + 1) * TOK, :] = q
+    zh, b, c, xl = spot("zh"), spot("b"), spot("c"), spot("xl")
+    lay_keys(oth_ref, k1_s, ve1_s)
+    sides = ((k0_ref, ve0_ref, c), (k1_s, ve1_s, 1 - c))
 
     def body(zt, masked, new, old, top):
         if new is not None:
-            q = q_s[new]
+            q = q_ref[new]
             m = mx_s[...]
         if old is not None:
             acc = acc_s[...]
-        for p in range(WIDE // PIECE):
-            at = slice(p * PIECE, (p + 1) * PIECE)
-            if old is not None:
-                w = jnp.exp2(s_s[zt, :, at] * SCALE - top).astype(jnp.bfloat16)
-                acc = acc + dot(w, ve_s[zt, at, :])
-            if new is not None:
-                s = dot(q, k_s[zt, :, at])
-                if masked:
-                    n = iota((ROWS, PIECE), 1) + p * PIECE % TILE
-                    r = iota((ROWS, PIECE), 0)
-                    r = r % TOK + jnp.where(r // (2 * TOK) == 0, b, 1 - b) * (NC * TOK)
-                    side = c if p * PIECE < TILE else 1 - c
-                    k_pos = (n // CUT) * (2 * TOK) + n % CUT + side * TOK + u * CUT
-                    s = jnp.where(k_pos <= r + (yh * 2 * NC + c) * TOK, s, LOW)
-                s_s[zt, :, at] = s
-                for i in range(PIECE // HD):
-                    m = jnp.maximum(m, s[:, i * HD : (i + 1) * HD])
+        for a, (k_ref, ve_ref, side) in enumerate(sides):
+            for p in range(PIECES):
+                at = slice(p * PIECE, (p + 1) * PIECE)
+                if old is not None:
+                    s_ref = s0_ref if old == 0 and a == 0 else s_s.at[a]
+                    w = jnp.exp2(s_ref[zt, :, at] * SCALE - top).astype(jnp.bfloat16)
+                    acc = acc + dot(w, ve_ref[zt, at, :])
+                if new == 1 or new == 0 and a == 1:
+                    s = score(q, k_ref, zt, p, side, masked)
+                    s_s[a, zt, :, at] = s
+                    m = highest(m, s)
         if new is not None:
             mx_s[...] = m
         if old is not None:
@@ -111,7 +143,7 @@
 
     def sweep(new, old, top):
         if new is not None:
-            mx_s[...] = jnp.full((ROWS, HD), LOW, jnp.float32)
+            mx_s[...] = jnp.full((ROWS, HD), LOW, jnp.float32) if new else mx0_ref[...]
         if old is not None:
             acc_s[...] = jnp.zeros((ROWS, 2 * HD), jnp.float32)
 
@@ -227,10 +259,10 @@
         h_ref[i * 2 : (i + 1) * 2] = part.astype(jnp.bfloat16).reshape(2, GRP, 2 * HD)
 
 
-def call(kernel, name, outs, args, scratch=(), flops=0, moved=0, space=pltpu.VMEM, limit=40):
+def call(kernel, name, outs, args, scratch=(), flops=0, moved=0, space=pltpu.VMEM, limit=40, kinds=()):
     return pl.pallas_call(
         kernel,
-        out_shape=[jax.ShapeDtypeStruct(s, jnp.bfloat16) for s in outs],
+        out_shape=[jax.ShapeDtypeStruct(s, kind) for s, kind in zip(outs, kinds or [jnp.bfloat16] * len(outs))],
         in_specs=[pl.BlockSpec(memory_space=space)] * len(args),
         out_specs=[pl.BlockSpec(memory_space=pltpu.VMEM)] * len(outs),
         scratch_shapes=list(scratch),
@@ -253,32 +285,40 @@
         limit=60,
     )
     with jax.named_scope("q_gather"):
-        q1 = lax.ppermute(queries, "xl", swap)
-        q2 = lax.ppermute(jnp.stack([queries, q1]), "b", swap)
+        near = jnp.stack([queries, lax.ppermute(queries, "xl", swap)])
+        far = lax.ppermute(near, "b", swap)
     with jax.named_scope("kv_gather"):
         kv_own = lax.all_to_all(own, CHIPS, 0, 0)
-        kv_own, q2 = lax.optimization_barrier((kv_own, q2))
+        kv_own, far = lax.optimization_barrier((kv_own, far))
         kv_own = kv_own.reshape(KEYS, 2 * HD)
     with jax.named_scope("kv_swap"):
         kv_oth = lax.ppermute(kv_own, "c", swap)
     f32, bf16 = jnp.float32, jnp.bfloat16
-    scratch = (
-        pltpu.VMEM((2, ROWS, HD), bf16),
-        pltpu.VMEM((NZ, HD, WIDE), bf16),
-        pltpu.VMEM((NZ, WIDE, 2 * HD), bf16),
-        pltpu.VMEM((NZ, ROWS, WIDE), f32),
-        pltpu.VMEM((ROWS, HD), f32),
-        pltpu.VMEM((ROWS, 2 * HD), f32),
-        pltpu.VMEM((ROWS, HD), f32),
-        pltpu.VMEM((ROWS, HD), f32),
+    begun = call(
+        begin_kernel,
+        "attend_begin",
+        [(2, ROWS, HD), (NZ, HD, TILE), (NZ, TILE, 2 * HD), (NZ, ROWS, TILE), (ROWS, HD)],
+        (near, far, kv_own),
+        flops=1 << 31,
+        limit=24,
+        kinds=(bf16, bf16, bf16, f32, f32),
     )
     (part,) = call(
         attend_kernel,
         "attend",
         [(NQ * 2, 2 * (HD + STAT), HD)],
-        (queries, q1, q2, kv_own, kv_oth),
-        scratch,
+        (*begun, kv_oth),
+        (
+            pltpu.VMEM((NZ, HD, TILE), bf16),
+            pltpu.VMEM((NZ, TILE, 2 * HD), bf16),
+            pltpu.VMEM((NC, NZ, ROWS, TILE), f32),
+            pltpu.VMEM((ROWS, HD), f32),
+            pltpu.VMEM((ROWS, 2 * HD), f32),
+            pltpu.VMEM((ROWS, HD), f32),
+            pltpu.VMEM((ROWS, HD), f32),
+        ),
         flops=1 << 33,
+        limit=32,
     )
     with jax.named_scope("part_exchange"):
         parts = lax.all_to_all(part, QUAD + ("xl",), 0, 0)

time: 125 us -> 124 us (level)
  waiting for transfers between devices: 33.6 us -> 31.9 us
    pallas_call x5 -> x6, Pallas kernels: 9.66 us -> 9.84 us  [call(): pl.pallas_call(kernel, out_shape=[jax.ShapeDtypeStruct(s, kind) for s, ki...]
  transfers between devices with their start and end apart: 7 -> 7, of which waited for: 6 -> 6; matrix products, arithmetic and copies ran while one was open for 0% -> 1% of each run, Pallas kernels for 1% -> 2%
where the time goes in v6:
time: 124 us; the launch traced here: 123 us
  blocking collectives  42.1 us (34%)
  starting transfers between devices  37.1 us (30%)
  waiting for transfers between devices  31.9 us (26%)
  Pallas kernels  9.84 us (8%)
  other arithmetic  1.62 us (1%)
    all_to_all x1, blocking collectives, local(): h_parts = lax.all_to_all(gram, PAIRS, 0, 0)  27.9 us
    ppermute x1, waiting for transfers between devices, local(): far = lax.ppermute(near, 'b', swap)  19.4 us
    all_to_all x1, starting transfers between devices, local(): kv_own = lax.all_to_all(own, CHIPS, 0, 0)  16.5 us
    all_to_all x1, blocking collectives, local(): parts = lax.all_to_all(part, QUAD + ('xl',), 0, 0)  14.2 us
    pallas_call x6, Pallas kernels, call(): pl.pallas_call(kernel, out_shape=[jax.ShapeDtypeStruct(s, kind) for s, ki...  9.84 us
    all_to_all x1, starting transfers between devices, local(): x_all = lax.all_to_all(x_many, HEAD, 0, 0)  4.81 us
    ppermute x1, waiting for transfers between devices, local(): x1 = lax.ppermute(x0, 'b', swap)  3.97 us
    ppermute x1, starting transfers between devices, local(): kv_oth = lax.ppermute(kv_own, 'c', swap)  3.74 us
  transfers between devices with their start and end apart: 7, of which 6 were waited for; matrix products, arithmetic and copies ran while one was open for 1% of the time, Pallas kernels for 2%

profile of v6, /device:TPU:1, one launch (start us, length us, event | category | flops | bytes accessed | tf_op | source)
XLA Modules:
  0.0 123.2 jit_solution(15227665671503273117)
XLA Ops:
  0.6 1.9 %prep.1 = bf16[32,64,256]{2,1,0:T(8,128)(2,1)} custom-call(bf16[256,256]{1,0:T(8,128)(2,1)} %k_ref.1, bf16[256,256]{1,0:T(8,128)(2,1)} %v_ref.1), custom_call_target="tpu_custom_call" | custom-call | bytes 1048576 | tf_op jit(solution)/shard_map/prep/pallas_call | solution.py:263
  2.6 16.5 %all-to-all-start = ((bf16[32,64,256]{2,1,0:T(8,128)(2,1)}), bf16[32,64,256]{2,1,0:T(8,128)(2,1)S(1)}, u32[]{:S(2)}, u32[]{:S(2)}) async-start(bf16[32,64,256]{2,1,0:T(8,128)(2,1)} %prep.1), calls=%async_computation | async-start | bytes 2097152 | tf_op jit(solution)/shard_map/kv_gather/all_to_all | solution.py:291
  19.1 3.1 %collective-permute-start = (bf16[256,256]{1,0:T(8,128)(2,1)}, bf16[256,256]{1,0:T(8,128)(2,1)S(1)}, u32[]{:S(2)}, u32[]{:S(2)}) collective-permute-start(bf16[256,256]{1,0:T(8,128)(2,1)} %param.3), channel_id=1, source_target_pairs={{0,2},{2,0},{1,3},{3,1},{4,6},{6,4},{5,7},{7,5},{8,10},{10,8},{9,1... | collective-permute-start | bytes 393224 | tf_op jit(solution)/shard_map/q_gather/ppermute | solution.py:288
  22.2 3.1 %collective-permute-done = bf16[256,256]{1,0:T(8,128)(2,1)S(1)} collective-permute-done((bf16[256,256]{1,0:T(8,128)(2,1)}, bf16[256,256]{1,0:T(8,128)(2,1)S(1)}, u32[]{:S(2)}, u32[]{:S(2)}) %collective-permute-start) | collective-permute-done | bytes 131104 | tf_op jit(solution)/shard_map/q_gather/ppermute | solution.py:288
  25.3 0.9 pad_maximum_fusion.near_ref
  26.2 3.1 %collective-permute-start.1 = (bf16[2,256,256]{2,1,0:T(8,128)(2,1)S(1)}, bf16[2,256,256]{2,1,0:T(8,128)(2,1)S(1)}, u32[]{:S(2)}, u32[]{:S(2)}) collective-permute-start(bf16[2,256,256]{2,1,0:T(8,128)(2,1)S(1)} %pad_maximum_fusion.near_ref), channel_id=1, source_target_pairs={{0,16},{16,0},{1,17},{17,1},{2,18},{18,2},{3,19},{19,3},{4,20},{20... | collective-permute-start | bytes 786440 | tf_op jit(solution)/shard_map/q_gather/ppermute | solution.py:289
  29.4 19.4 %collective-permute-done.1.far_ref = bf16[2,256,256]{2,1,0:T(8,128)(2,1)S(1)} collective-permute-done((bf16[2,256,256]{2,1,0:T(8,128)(2,1)S(1)}, bf16[2,256,256]{2,1,0:T(8,128)(2,1)S(1)}, u32[]{:S(2)}, u32[]{:S(2)}) %collective-permute-start.1) | collective-permute-done | bytes 262176 | tf_op jit(solution)/shard_map/q_gather/ppermute | solution.py:289
  48.7 0.0 all-to-all-done
  48.7 3.7 %collective-permute-start.2 = (bf16[2048,256]{1,0:T(8,128)(2,1)S(1)}, bf16[2048,256]{1,0:T(8,128)(2,1)S(1)}, u32[]{:S(2)}, u32[]{:S(2)}) collective-permute-start(bf16[2048,256]{1,0:T(8,128)(2,1)S(1)} %bitcast.5), channel_id=1, source_target_pairs={{0,8},{8,0},{1,9},{9,1},{2,10},{10,2},{3,11},{11,3},{4,12},{12,4},... | collective-permute-start | bytes 3145736 | tf_op jit(solution)/shard_map/kv_swap/ppermute | solution.py:295
  52.5 0.8 attend_begin.1
  53.3 1.4 %collective-permute-done.2.oth_ref = bf16[2048,256]{1,0:T(8,128)(2,1)S(1)} collective-permute-done((bf16[2048,256]{1,0:T(8,128)(2,1)S(1)}, bf16[2048,256]{1,0:T(8,128)(2,1)S(1)}, u32[]{:S(2)}, u32[]{:S(2)}) %collective-permute-start.2) | collective-permute-done | bytes 1048608 | tf_op jit(solution)/shard_map/kv_swap/ppermute | solution.py:295
  54.7 3.6 %attend.1 = bf16[8,288,128]{2,1,0:T(8,128)(2,1)S(1)} custom-call(bf16[2,1024,128]{2,1,0:T(8,128)(2,1)S(1)} %get-tuple-element.15.q_ref, bf16[4,128,512]{2,1,0:T(8,128)(2,1)S(1)} %get-tuple-element.16.k0_ref, bf16[4,512,256]{2,1,0:T(8,128)(2,1)S(1)} %get-tuple-element.17.ve0_ref, f32[4,1024,512]{2,1,0:T(8,128)S(1)} %get-tuple-element.18.s0_ref, ...), custom_call_target="tpu_custom_call" | custom-call | flops 8589934592 | tf_op jit(solution)/shard_map/attend/pallas_call | solution.py:263
  58.4 14.2 %all_to_all.20.r_ref = bf16[8,288,128]{2,1,0:T(8,128)(2,1)S(1)} all-to-all(bf16[8,288,128]{2,1,0:T(8,128)(2,1)S(1)} %attend.1), channel_id=1, replica_groups=mesh['zh'=4,'yh'=4,'b'=2,'c'=2,'g'=2,'xl'=2,'zl'=2] {'b','c','xl'}, dimensions={0} | all-to-all | bytes 1179648 | tf_op jit(solution)/shard_map/part_exchange/all_to_all | solution.py:324
  72.6 1.4 %combine.1 = (bf16[512,128]{1,0:T(8,128)(2,1)S(1)}, bf16[8,512,128]{2,1,0:T(8,128)(2,1)}) custom-call(bf16[8,288,128]{2,1,0:T(8,128)(2,1)S(1)} %all_to_all.20.r_ref), custom_call_target="tpu_custom_call" | custom-call | tf_op jit(solution)/shard_map/combine/pallas_call | solution.py:263
  73.9 4.8 %all-to-all-start.2 = ((bf16[8,512,128]{2,1,0:T(8,128)(2,1)}), bf16[8,512,128]{2,1,0:T(8,128)(2,1)S(1)}, u32[]{:S(2)}, u32[]{:S(2)}) async-start(bf16[8,512,128]{2,1,0:T(8,128)(2,1)} %get-tuple-element.22), calls=%async_computation.2 | async-start | bytes 2097152 | tf_op jit(solution)/shard_map/x_gather/all_to_all | solution.py:330
  78.7 2.3 %collective-permute-start.3 = (bf16[512,128]{1,0:T(8,128)(2,1)S(1)}, bf16[512,128]{1,0:T(8,128)(2,1)S(1)}, u32[]{:S(2)}, u32[]{:S(2)}) collective-permute-start(bf16[512,128]{1,0:T(8,128)(2,1)S(1)} %get-tuple-element.20.x0_ref), channel_id=1, source_target_pairs={{0,16},{16,0},{1,17},{17,1},{2,18},{18,2},{3,19},{19,3},{4,20},{20... | collective-permute-start | bytes 393224 | tf_op jit(solution)/shard_map/x_swap/ppermute | solution.py:327
  81.0 4.0 %collective-permute-done.3.x1_ref = bf16[512,128]{1,0:T(8,128)(2,1)S(1)} collective-permute-done((bf16[512,128]{1,0:T(8,128)(2,1)S(1)}, bf16[512,128]{1,0:T(8,128)(2,1)S(1)}, u32[]{:S(2)}, u32[]{:S(2)}) %collective-permute-start.3) | collective-permute-done | bytes 131104 | tf_op jit(solution)/shard_map/x_swap/ppermute | solution.py:327
  85.0 3.5 %collective-permute-start.4 = (bf16[2,512,128]{2,1,0:T(8,128)(2,1)S(1)}, bf16[2,512,128]{2,1,0:T(8,128)(2,1)S(1)}, u32[]{:S(2)}, u32[]{:S(2)}) collective-permute-start(bf16[2,512,128]{2,1,0:T(8,128)(2,1)S(1)} %pad_maximum_fusion.1), channel_id=1, source_target_pairs={{0,8},{8,0},{1,9},{9,1},{2,10},{10,2},{3,11},{11,3},{4,12},{12,4},... | collective-permute-start | bytes 786440 | tf_op jit(solution)/shard_map/x_swap/ppermute | solution.py:328
  88.5 1.1 collective-permute-done.4.x2_ref
  89.6 1.4 %assemble.1 = (bf16[2,512,256]{2,1,0:T(8,128)(2,1)S(1)}, bf16[256,256]{1,0:T(8,128)(2,1)}) custom-call(bf16[512,128]{1,0:T(8,128)(2,1)S(1)} %get-tuple-element.20.x0_ref, bf16[512,128]{1,0:T(8,128)(2,1)S(1)} %collective-permute-done.3.x1_ref, bf16[2,512,128]{2,1,0:T(8,128)(2,1)S(1)} %collective-permute-done.4.x2_ref), custom_call_target="tpu_custom_call" | custom-call | flops 268435456 | bytes 1048576 | tf_op jit(solution)/shard_map/assemble/pallas_call | solution.py:263
  91.0 2.9 %all-to-all-done.2.r_ref = bf16[8,512,128]{2,1,0:T(8,128)(2,1)S(1)} async-done(((bf16[8,512,128]{2,1,0:T(8,128)(2,1)}), bf16[8,512,128]{2,1,0:T(8,128)(2,1)S(1)}, u32[]{:S(2)}, u32[]{:S(2)}) %all-to-all-start.2) | async-done | bytes 1048608 | tf_op jit(solution)/shard_map/x_gather/all_to_all | solution.py:330
  93.9 0.8 gram.1
  94.7 27.9 %all_to_all.21 = bf16[16,32,256]{2,1,0:T(8,128)(2,1)S(1)} all-to-all(bf16[16,32,256]{2,1,0:T(8,128)(2,1)S(1)} %gram.1), channel_id=1, replica_groups=mesh['zh'=4,'yh'=4,'b'=2,'c'=2,'g'=2,'xl'=2,'zl'=2] {'zh','yh'}, dimensions={0} | all-to-all | bytes 524288 | tf_op jit(solution)/shard_map/h_exchange/all_to_all | solution.py:341
  122.6 0.6 broadcast_multiply_fusion
  (2 shorter events, 0.1 us)
Async XLA Ops:
  2.6 46.2 %all-to-all-start = ((bf16[32,64,256]{2,1,0:T(8,128)(2,1)}), bf16[32,64,256]{2,1,0:T(8,128)(2,1)S(1)}, u32[]{:S(2)}, u32[]{:S(2)}) async-start(bf16[32,64,256]{2,1,0:T(8,128)(2,1)} %prep.1), calls=%async_computation | async-start | bytes 2097152 | tf_op jit(solution)/shard_map/kv_gather/all_to_all | solution.py:291
  19.1 6.2 %collective-permute-start = (bf16[256,256]{1,0:T(8,128)(2,1)}, bf16[256,256]{1,0:T(8,128)(2,1)S(1)}, u32[]{:S(2)}, u32[]{:S(2)}) collective-permute-start(bf16[256,256]{1,0:T(8,128)(2,1)} %param.3), channel_id=1, source_target_pairs={{0,2},{2,0},{1,3},{3,1},{4,6},{6,4},{5,7},{7,5},{8,10},{10,8},{9,1... | collective-permute-start | bytes 393224 | tf_op jit(solution)/shard_map/q_gather/ppermute | solution.py:288
  26.2 22.5 %collective-permute-start.1 = (bf16[2,256,256]{2,1,0:T(8,128)(2,1)S(1)}, bf16[2,256,256]{2,1,0:T(8,128)(2,1)S(1)}, u32[]{:S(2)}, u32[]{:S(2)}) collective-permute-start(bf16[2,256,256]{2,1,0:T(8,128)(2,1)S(1)} %pad_maximum_fusion.near_ref), channel_id=1, source_target_pairs={{0,16},{16,0},{1,17},{17,1},{2,18},{18,2},{3,19},{19,3},{4,20},{20... | collective-permute-start | bytes 786440 | tf_op jit(solution)/shard_map/q_gather/ppermute | solution.py:289
  48.7 6.0 %collective-permute-start.2 = (bf16[2048,256]{1,0:T(8,128)(2,1)S(1)}, bf16[2048,256]{1,0:T(8,128)(2,1)S(1)}, u32[]{:S(2)}, u32[]{:S(2)}) collective-permute-start(bf16[2048,256]{1,0:T(8,128)(2,1)S(1)} %bitcast.5), channel_id=1, source_target_pairs={{0,8},{8,0},{1,9},{9,1},{2,10},{10,2},{3,11},{11,3},{4,12},{12,4},... | collective-permute-start | bytes 3145736 | tf_op jit(solution)/shard_map/kv_swap/ppermute | solution.py:295
  73.9 20.0 %all-to-all-start.2 = ((bf16[8,512,128]{2,1,0:T(8,128)(2,1)}), bf16[8,512,128]{2,1,0:T(8,128)(2,1)S(1)}, u32[]{:S(2)}, u32[]{:S(2)}) async-start(bf16[8,512,128]{2,1,0:T(8,128)(2,1)} %get-tuple-element.22), calls=%async_computation.2 | async-start | bytes 2097152 | tf_op jit(solution)/shard_map/x_gather/all_to_all | solution.py:330
  78.7 6.2 %collective-permute-start.3 = (bf16[512,128]{1,0:T(8,128)(2,1)S(1)}, bf16[512,128]{1,0:T(8,128)(2,1)S(1)}, u32[]{:S(2)}, u32[]{:S(2)}) collective-permute-start(bf16[512,128]{1,0:T(8,128)(2,1)S(1)} %get-tuple-element.20.x0_ref), channel_id=1, source_target_pairs={{0,16},{16,0},{1,17},{17,1},{2,18},{18,2},{3,19},{19,3},{4,20},{20... | collective-permute-start | bytes 393224 | tf_op jit(solution)/shard_map/x_swap/ppermute | solution.py:327
  85.0 4.6 %collective-permute-start.4 = (bf16[2,512,128]{2,1,0:T(8,128)(2,1)S(1)}, bf16[2,512,128]{2,1,0:T(8,128)(2,1)S(1)}, u32[]{:S(2)}, u32[]{:S(2)}) collective-permute-start(bf16[2,512,128]{2,1,0:T(8,128)(2,1)S(1)} %pad_maximum_fusion.1), channel_id=1, source_target_pairs={{0,8},{8,0},{1,9},{9,1},{2,10},{10,2},{3,11},{11,3},{4,12},{12,4},... | collective-permute-start | bytes 786440 | tf_op jit(solution)/shard_map/x_swap/ppermute | solution.py:328

commit v7 on v6

--- a/solution.py
+++ b/solution.py
@@ -15,8 +15,8 @@
 
 CTX = ("zh", "yh", "b", "c")
 HEAD = ("g", "xl", "zl")
-CHIPS = ("zh", "yh", "b")
-PAIRS = ("zh", "yh")
+CHIPS = ("yh", "b", "zh")
+PAIRS = ("yh", "zh")
 QUAD = ("b", "c")
 SHARE = ("b", "xl")
 NZ, NY, NC, NS = 4, 8, 2, 4
@@ -25,7 +25,6 @@
 TOK = 256
 CUT = TOK // NS
 TILE = NY * CUT
-KEYS = NZ * TILE
 ROWS = NS * TOK
 PIECE = 256
 PIECES = TILE // PIECE
@@ -62,14 +61,14 @@
         copy.wait()
     for i in range(NZ * NY):
         for a in range(2):
-            o_ref[i, :, a * HD : (a + 1) * HD] = kv_s[i % 2, a]
+            o_ref[i, :, a * HD : (a + 1) * HD] = kv_s[i // NZ % 2, a]
 
 
 def lay_keys(kv_ref, k_ref, ve_ref):
     for zt in range(NZ):
-        src = slice(zt * TILE, (zt + 1) * TILE)
-        k_ref[zt] = jnp.transpose(kv_ref[src, 0:HD])
-        ve_ref[zt, :, 0:HD] = kv_ref[src, HD : 2 * HD]
+        kv = kv_ref[:, zt].reshape(TILE, 2 * HD)
+        k_ref[zt] = jnp.transpose(kv[:, 0:HD])
+        ve_ref[zt, :, 0:HD] = kv[:, HD : 2 * HD]
         ve_ref[zt, :, HD : 2 * HD] = jnp.ones((TILE, HD), jnp.bfloat16)
 
 
@@ -91,29 +90,30 @@
     return m
 
 
-def begin_kernel(near_ref, far_ref, kv_ref, q_ref, k_ref, ve_ref, s_ref, mx_ref):
+def begin_kernel(near_ref, far_ref, kv_ref, q_ref, k_ref, ve_ref, s0_ref, s1_ref, mx_ref):
     lay_keys(kv_ref, k_ref, ve_ref)
     for hh in range(2):
         for i in range(NS):
             part_ref = (near_ref, far_ref)[i // 2]
             q_ref[hh, i * TOK : (i + 1) * TOK, :] = part_ref[i % 2, :, hh * HD : (hh + 1) * HD]
-    mx_ref[...] = jnp.full((ROWS, HD), LOW, jnp.float32)
+    mx_ref[...] = jnp.full((2, ROWS, HD), LOW, jnp.float32)
 
     def body(zt, masked):
-        q = q_ref[0]
-        m = mx_ref[...]
-        for p in range(PIECES):
-            s = score(q, k_ref, zt, p, spot("c"), masked)
-            s_ref[zt, :, p * PIECE : (p + 1) * PIECE] = s
-            m = highest(m, s)
-        mx_ref[...] = m
+        for hh, s_ref, pieces in ((0, s0_ref, PIECES), (1, s1_ref, 1)):
+            q = q_ref[hh]
+            m = mx_ref[hh]
+            for p in range(pieces):
+                s = score(q, k_ref, zt, p, spot("c"), masked)
+                s_ref[zt, :, p * PIECE : (p + 1) * PIECE] = s
+                m = highest(m, s)
+            mx_ref[hh] = m
 
     lax.fori_loop(0, spot("zh"), lambda zt, _: (body(zt, False), 0)[1], 0)
     body(spot("zh"), True)
 
 
 def attend_kernel(
-    q_ref, k0_ref, ve0_ref, s0_ref, mx0_ref, oth_ref, o_ref, k1_s, ve1_s, s_s, mx_s, acc_s, st_s, o0_s
+    q_ref, k0_ref, ve0_ref, s0_ref, s1_ref, mx0_ref, oth_ref, o_ref, k1_s, ve1_s, s_s, mx_s, acc_s, st_s, o0_s
 ):
     zh, b, c, xl = spot("zh"), spot("b"), spot("c"), spot("xl")
     lay_keys(oth_ref, k1_s, ve1_s)
@@ -129,10 +129,10 @@
             for p in range(PIECES):
                 at = slice(p * PIECE, (p + 1) * PIECE)
                 if old is not None:
-                    s_ref = s0_ref if old == 0 and a == 0 else s_s.at[a]
+                    s_ref = s0_ref if old == 0 and a == 0 else s1_ref if old == 1 and a == 0 and p == 0 else s_s.at[a]
                     w = jnp.exp2(s_ref[zt, :, at] * SCALE - top).astype(jnp.bfloat16)
                     acc = acc + dot(w, ve_ref[zt, at, :])
-                if new == 1 or new == 0 and a == 1:
+                if new is not None and (a == 1 or new == 1 and p > 0):
                     s = score(q, k_ref, zt, p, side, masked)
                     s_s[a, zt, :, at] = s
                     m = highest(m, s)
@@ -143,7 +143,7 @@
 
     def sweep(new, old, top):
         if new is not None:
-            mx_s[...] = jnp.full((ROWS, HD), LOW, jnp.float32) if new else mx0_ref[...]
+            mx_s[...] = mx0_ref[new]
         if old is not None:
             acc_s[...] = jnp.zeros((ROWS, 2 * HD), jnp.float32)
 
@@ -200,15 +200,15 @@
         turned = jnp.transpose(stats[at:end])
         tail = jnp.concatenate([turned[0:8, 0:HD], turned[0:8, HD : 2 * HD]], axis=0)
         for k in range(NQ):
-            o_ref[k * 2 + to_x, rows, :] = slots[k].astype(jnp.bfloat16)
-            o_ref[k * 2 + to_x, tails, :] = tail.astype(jnp.bfloat16)
+            o_ref[to_x * NQ + k, rows, :] = slots[k].astype(jnp.bfloat16)
+            o_ref[to_x * NQ + k, tails, :] = tail.astype(jnp.bfloat16)
 
 
 def combine_kernel(r_ref, x_ref, many_ref):
     row = iota((STAT, HD), 0)
     lanes = jnp.logical_and(row % NQ == iota((STAT, HD), 1) // GRP, row < 3 * NQ).astype(jnp.bfloat16)
     for k in range(NQ):
-        sources = [(s // 2 * NC + k % NC) * 2 + s % 2 for s in range(NS)]
+        sources = [s % 2 * NQ + s // 2 * NC + k % NC for s in range(NS)]
         first, stat = k // NC * HD, 2 * HD + k // NC * STAT
         shares = [[] for _ in range(NS)]
         for place in range(NQ):
@@ -255,8 +255,11 @@
 
 def gram_kernel(r_ref, x_ref, h_ref):
     for i in range(8):
-        part = dot(r_ref[i], x_ref[0], ATB)[0 : HD // 2] + dot(r_ref[i], x_ref[1], ATB)[HD // 2 : HD]
-        h_ref[i * 2 : (i + 1) * 2] = part.astype(jnp.bfloat16).reshape(2, GRP, 2 * HD)
+        at = i % 2 * 4 + i // 2
+        part = dot(r_ref[at], x_ref[0], ATB)[0 : HD // 2] + dot(r_ref[at], x_ref[1], ATB)[HD // 2 : HD]
+        for hh in range(2):
+            zh, yh = (i * 2 + hh) // 4, (i * 2 + hh) % 4
+            h_ref[yh * NZ + zh] = part[hh * GRP : (hh + 1) * GRP].astype(jnp.bfloat16)
 
 
 def call(kernel, name, outs, args, scratch=(), flops=0, moved=0, space=pltpu.VMEM, limit=40, kinds=()):
@@ -290,18 +293,18 @@
     with jax.named_scope("kv_gather"):
         kv_own = lax.all_to_all(own, CHIPS, 0, 0)
         kv_own, far = lax.optimization_barrier((kv_own, far))
-        kv_own = kv_own.reshape(KEYS, 2 * HD)
+        kv_own = kv_own.reshape(NY, NZ, CUT, 2 * HD)
     with jax.named_scope("kv_swap"):
         kv_oth = lax.ppermute(kv_own, "c", swap)
     f32, bf16 = jnp.float32, jnp.bfloat16
     begun = call(
         begin_kernel,
         "attend_begin",
-        [(2, ROWS, HD), (NZ, HD, TILE), (NZ, TILE, 2 * HD), (NZ, ROWS, TILE), (ROWS, HD)],
+        [(2, ROWS, HD), (NZ, HD, TILE), (NZ, TILE, 2 * HD), (NZ, ROWS, TILE), (NZ, ROWS, PIECE), (2, ROWS, HD)],
         (near, far, kv_own),
         flops=1 << 31,
-        limit=24,
-        kinds=(bf16, bf16, bf16, f32, f32),
+        limit=16,
+        kinds=(bf16, bf16, bf16, f32, f32, f32),
     )
     (part,) = call(
         attend_kernel,
@@ -318,16 +321,16 @@
             pltpu.VMEM((ROWS, HD), f32),
         ),
         flops=1 << 33,
-        limit=32,
+        limit=28,
     )
     with jax.named_scope("part_exchange"):
-        parts = lax.all_to_all(part, QUAD + ("xl",), 0, 0)
+        parts = lax.all_to_all(part, ("xl",) + QUAD, 0, 0)
     x0, x_many = call(combine_kernel, "combine", [(NQ * HD, HD), (8, NQ * HD, HD)], (parts,))
     with jax.named_scope("x_swap"):
         x1 = lax.ppermute(x0, "b", swap)
         x2 = lax.ppermute(jnp.stack([x0, x1]), "c", swap)
     with jax.named_scope("x_gather"):
-        x_all = lax.all_to_all(x_many, HEAD, 0, 0)
+        x_all = lax.all_to_all(x_many, ("zl", "g", "xl"), 0, 0)
     x, attn_out = call(
         assemble_kernel,
         "assemble",

time: 124 us -> 123 us (level)
  waiting for transfers between devices: 31.9 us -> 30.6 us
where the time goes in v7:
time: 123 us; the launch traced here: 121 us
  blocking collectives  41.7 us (34%)
  starting transfers between devices  36.9 us (30%)
  waiting for transfers between devices  30.6 us (25%)
  Pallas kernels  9.96 us (8%)
  other arithmetic  1.62 us (1%)
    all_to_all x1, blocking collectives, local(): h_parts = lax.all_to_all(gram, PAIRS, 0, 0)  28.4 us
    ppermute x1, waiting for transfers between devices, local(): far = lax.ppermute(near, 'b', swap)  18.9 us
    all_to_all x1, starting transfers between devices, local(): kv_own = lax.all_to_all(own, CHIPS, 0, 0)  16.5 us
    all_to_all x1, blocking collectives, local(): parts = lax.all_to_all(part, ('xl',) + QUAD, 0, 0)  13.3 us
    pallas_call x6, Pallas kernels, call(): pl.pallas_call(kernel, out_shape=[jax.ShapeDtypeStruct(s, kind) for s, ki...  9.96 us
    all_to_all x1, starting transfers between devices, local(): x_all = lax.all_to_all(x_many, ('zl', 'g', 'xl'), 0, 0)  4.28 us
    ppermute x1, starting transfers between devices, local(): x2 = lax.ppermute(jnp.stack([x0, x1]), 'c', swap)  3.79 us
    ppermute x1, starting transfers between devices, local(): kv_oth = lax.ppermute(kv_own, 'c', swap)  3.7 us
  transfers between devices with their start and end apart: 7, of which 6 were waited for; matrix products, arithmetic and copies ran while one was open for 1% of the time, Pallas kernels for 2%

profile of v7, /device:TPU:1, one launch (start us, length us, event | category | flops | bytes accessed | tf_op | source)
XLA Modules:
  0.0 121.5 jit_solution(9153432216332907390)
XLA Ops:
  0.6 1.9 %prep.1 = bf16[32,64,256]{2,1,0:T(8,128)(2,1)} custom-call(bf16[256,256]{1,0:T(8,128)(2,1)} %k_ref.1, bf16[256,256]{1,0:T(8,128)(2,1)} %v_ref.1), custom_call_target="tpu_custom_call" | custom-call | bytes 1048576 | tf_op jit(solution)/shard_map/prep/pallas_call | solution.py:266
  2.6 16.5 %all-to-all-start = ((bf16[32,64,256]{2,1,0:T(8,128)(2,1)}), bf16[32,64,256]{2,1,0:T(8,128)(2,1)S(1)}, u32[]{:S(2)}, u32[]{:S(2)}) async-start(bf16[32,64,256]{2,1,0:T(8,128)(2,1)} %prep.1), calls=%async_computation | async-start | bytes 2097152 | tf_op jit(solution)/shard_map/kv_gather/all_to_all | solution.py:294
  19.1 3.1 %collective-permute-start = (bf16[256,256]{1,0:T(8,128)(2,1)}, bf16[256,256]{1,0:T(8,128)(2,1)S(1)}, u32[]{:S(2)}, u32[]{:S(2)}) collective-permute-start(bf16[256,256]{1,0:T(8,128)(2,1)} %param.3), channel_id=1, source_target_pairs={{0,2},{2,0},{1,3},{3,1},{4,6},{6,4},{5,7},{7,5},{8,10},{10,8},{9,1... | collective-permute-start | bytes 393224 | tf_op jit(solution)/shard_map/q_gather/ppermute | solution.py:291
  22.2 3.1 %collective-permute-done = bf16[256,256]{1,0:T(8,128)(2,1)S(1)} collective-permute-done((bf16[256,256]{1,0:T(8,128)(2,1)}, bf16[256,256]{1,0:T(8,128)(2,1)S(1)}, u32[]{:S(2)}, u32[]{:S(2)}) %collective-permute-start) | collective-permute-done | bytes 131104 | tf_op jit(solution)/shard_map/q_gather/ppermute | solution.py:291
  25.3 0.9 pad_maximum_fusion.near_ref
  26.2 3.1 %collective-permute-start.1 = (bf16[2,256,256]{2,1,0:T(8,128)(2,1)S(1)}, bf16[2,256,256]{2,1,0:T(8,128)(2,1)S(1)}, u32[]{:S(2)}, u32[]{:S(2)}) collective-permute-start(bf16[2,256,256]{2,1,0:T(8,128)(2,1)S(1)} %pad_maximum_fusion.near_ref), channel_id=1, source_target_pairs={{0,16},{16,0},{1,17},{17,1},{2,18},{18,2},{3,19},{19,3},{4,20},{20... | collective-permute-start | bytes 786440 | tf_op jit(solution)/shard_map/q_gather/ppermute | solution.py:292
  29.4 18.9 %collective-permute-done.1.far_ref = bf16[2,256,256]{2,1,0:T(8,128)(2,1)S(1)} collective-permute-done((bf16[2,256,256]{2,1,0:T(8,128)(2,1)S(1)}, bf16[2,256,256]{2,1,0:T(8,128)(2,1)S(1)}, u32[]{:S(2)}, u32[]{:S(2)}) %collective-permute-start.1) | collective-permute-done | bytes 262176 | tf_op jit(solution)/shard_map/q_gather/ppermute | solution.py:292
  48.3 0.0 all-to-all-done
  48.3 3.7 %collective-permute-start.2 = (bf16[8,4,64,256]{3,2,1,0:T(8,128)(2,1)S(1)}, bf16[8,4,64,256]{3,2,1,0:T(8,128)(2,1)S(1)}, u32[]{:S(2)}, u32[]{:S(2)}) collective-permute-start(bf16[8,4,64,256]{3,2,1,0:T(8,128)(2,1)S(1)} %bitcast.5), channel_id=1, source_target_pairs={{0,8},{8,0},{1,9},{9,1},{2,10},{10,2},{3,11},{11,3},{4,12},{12,4},... | collective-permute-start | bytes 3145736 | tf_op jit(solution)/shard_map/kv_swap/ppermute | solution.py:298
  52.0 1.0 attend_begin.1
  53.0 1.3 %collective-permute-done.2.oth_ref = bf16[8,4,64,256]{3,2,1,0:T(8,128)(2,1)S(1)} collective-permute-done((bf16[8,4,64,256]{3,2,1,0:T(8,128)(2,1)S(1)}, bf16[8,4,64,256]{3,2,1,0:T(8,128)(2,1)S(1)}, u32[]{:S(2)}, u32[]{:S(2)}) %collective-permute-start.2) | collective-permute-done | bytes 1048608 | tf_op jit(solution)/shard_map/kv_swap/ppermute | solution.py:298
  54.3 3.6 %attend.1 = bf16[8,288,128]{2,1,0:T(8,128)(2,1)S(1)} custom-call(bf16[2,1024,128]{2,1,0:T(8,128)(2,1)S(1)} %get-tuple-element.16.q_ref, bf16[4,128,512]{2,1,0:T(8,128)(2,1)S(1)} %get-tuple-element.17.k0_ref, bf16[4,512,256]{2,1,0:T(8,128)(2,1)S(1)} %get-tuple-element.18.ve0_ref, f32[4,1024,512]{2,1,0:T(8,128)S(1)} %get-tuple-element.19.s0_ref, ...), custom_call_target="tpu_custom_call" | custom-call | flops 8589934592 | tf_op jit(solution)/shard_map/attend/pallas_call | solution.py:266
  57.9 13.3 %all_to_all.20.r_ref = bf16[8,288,128]{2,1,0:T(8,128)(2,1)S(1)} all-to-all(bf16[8,288,128]{2,1,0:T(8,128)(2,1)S(1)} %attend.1), channel_id=1, replica_groups=mesh['zh'=4,'yh'=4,'b'=2,'c'=2,'g'=2,'xl'=2,'zl'=2] {'xl','b','c'}, dimensions={0} | all-to-all | bytes 1179648 | tf_op jit(solution)/shard_map/part_exchange/all_to_all | solution.py:327
  71.2 1.4 %combine.1 = (bf16[512,128]{1,0:T(8,128)(2,1)S(1)}, bf16[8,512,128]{2,1,0:T(8,128)(2,1)}) custom-call(bf16[8,288,128]{2,1,0:T(8,128)(2,1)S(1)} %all_to_all.20.r_ref), custom_call_target="tpu_custom_call" | custom-call | tf_op jit(solution)/shard_map/combine/pallas_call | solution.py:266
  72.6 4.3 %all-to-all-start.2 = ((bf16[8,512,128]{2,1,0:T(8,128)(2,1)}), bf16[8,512,128]{2,1,0:T(8,128)(2,1)S(1)}, u32[]{:S(2)}, u32[]{:S(2)}) async-start(bf16[8,512,128]{2,1,0:T(8,128)(2,1)} %get-tuple-element.24), calls=%async_computation.2 | async-start | bytes 2097152 | tf_op jit(solution)/shard_map/x_gather/all_to_all | solution.py:333
  76.9 2.4 %collective-permute-start.3 = (bf16[512,128]{1,0:T(8,128)(2,1)S(1)}, bf16[512,128]{1,0:T(8,128)(2,1)S(1)}, u32[]{:S(2)}, u32[]{:S(2)}) collective-permute-start(bf16[512,128]{1,0:T(8,128)(2,1)S(1)} %get-tuple-element.22.x0_ref), channel_id=1, source_target_pairs={{0,16},{16,0},{1,17},{17,1},{2,18},{18,2},{3,19},{19,3},{4,20},{20... | collective-permute-start | bytes 393224 | tf_op jit(solution)/shard_map/x_swap/ppermute | solution.py:330
  79.2 3.6 %collective-permute-done.3.x1_ref = bf16[512,128]{1,0:T(8,128)(2,1)S(1)} collective-permute-done((bf16[512,128]{1,0:T(8,128)(2,1)S(1)}, bf16[512,128]{1,0:T(8,128)(2,1)S(1)}, u32[]{:S(2)}, u32[]{:S(2)}) %collective-permute-start.3) | collective-permute-done | bytes 131104 | tf_op jit(solution)/shard_map/x_swap/ppermute | solution.py:330
  82.9 3.8 %collective-permute-start.4 = (bf16[2,512,128]{2,1,0:T(8,128)(2,1)S(1)}, bf16[2,512,128]{2,1,0:T(8,128)(2,1)S(1)}, u32[]{:S(2)}, u32[]{:S(2)}) collective-permute-start(bf16[2,512,128]{2,1,0:T(8,128)(2,1)S(1)} %pad_maximum_fusion.1), channel_id=1, source_target_pairs={{0,8},{8,0},{1,9},{9,1},{2,10},{10,2},{3,11},{11,3},{4,12},{12,4},... | collective-permute-start | bytes 786440 | tf_op jit(solution)/shard_map/x_swap/ppermute | solution.py:331
  86.7 1.1 collective-permute-done.4.x2_ref
  87.8 1.4 %assemble.1 = (bf16[2,512,256]{2,1,0:T(8,128)(2,1)S(1)}, bf16[256,256]{1,0:T(8,128)(2,1)}) custom-call(bf16[512,128]{1,0:T(8,128)(2,1)S(1)} %get-tuple-element.22.x0_ref, bf16[512,128]{1,0:T(8,128)(2,1)S(1)} %collective-permute-done.3.x1_ref, bf16[2,512,128]{2,1,0:T(8,128)(2,1)S(1)} %collective-permute-done.4.x2_ref), custom_call_target="tpu_custom_call" | custom-call | flops 268435456 | bytes 1048576 | tf_op jit(solution)/shard_map/assemble/pallas_call | solution.py:266
  89.2 2.4 %all-to-all-done.2.r_ref = bf16[8,512,128]{2,1,0:T(8,128)(2,1)S(1)} async-done(((bf16[8,512,128]{2,1,0:T(8,128)(2,1)}), bf16[8,512,128]{2,1,0:T(8,128)(2,1)S(1)}, u32[]{:S(2)}, u32[]{:S(2)}) %all-to-all-start.2) | async-done | bytes 1048608 | tf_op jit(solution)/shard_map/x_gather/all_to_all | solution.py:333
  91.6 0.8 gram.1
  92.4 28.4 %all_to_all.21 = bf16[16,32,256]{2,1,0:T(8,128)(2,1)S(1)} all-to-all(bf16[16,32,256]{2,1,0:T(8,128)(2,1)S(1)} %gram.1), channel_id=1, replica_groups=mesh['zh'=4,'yh'=4,'b'=2,'c'=2,'g'=2,'xl'=2,'zl'=2] {'yh','zh'}, dimensions={0} | all-to-all | bytes 524288 | tf_op jit(solution)/shard_map/h_exchange/all_to_all | solution.py:344
  120.9 0.6 broadcast_multiply_fusion
  (2 shorter events, 0.1 us)
Async XLA Ops:
  2.6 45.8 %all-to-all-start = ((bf16[32,64,256]{2,1,0:T(8,128)(2,1)}), bf16[32,64,256]{2,1,0:T(8,128)(2,1)S(1)}, u32[]{:S(2)}, u32[]{:S(2)}) async-start(bf16[32,64,256]{2,1,0:T(8,128)(2,1)} %prep.1), calls=%async_computation | async-start | bytes 2097152 | tf_op jit(solution)/shard_map/kv_gather/all_to_all | solution.py:294
  19.1 6.2 %collective-permute-start = (bf16[256,256]{1,0:T(8,128)(2,1)}, bf16[256,256]{1,0:T(8,128)(2,1)S(1)}, u32[]{:S(2)}, u32[]{:S(2)}) collective-permute-start(bf16[256,256]{1,0:T(8,128)(2,1)} %param.3), channel_id=1, source_target_pairs={{0,2},{2,0},{1,3},{3,1},{4,6},{6,4},{5,7},{7,5},{8,10},{10,8},{9,1... | collective-permute-start | bytes 393224 | tf_op jit(solution)/shard_map/q_gather/ppermute | solution.py:291
  26.2 22.1 %collective-permute-start.1 = (bf16[2,256,256]{2,1,0:T(8,128)(2,1)S(1)}, bf16[2,256,256]{2,1,0:T(8,128)(2,1)S(1)}, u32[]{:S(2)}, u32[]{:S(2)}) collective-permute-start(bf16[2,256,256]{2,1,0:T(8,128)(2,1)S(1)} %pad_maximum_fusion.near_ref), channel_id=1, source_target_pairs={{0,16},{16,0},{1,17},{17,1},{2,18},{18,2},{3,19},{19,3},{4,20},{20... | collective-permute-start | bytes 786440 | tf_op jit(solution)/shard_map/q_gather/ppermute | solution.py:292
  48.3 6.0 %collective-permute-start.2 = (bf16[8,4,64,256]{3,2,1,0:T(8,128)(2,1)S(1)}, bf16[8,4,64,256]{3,2,1,0:T(8,128)(2,1)S(1)}, u32[]{:S(2)}, u32[]{:S(2)}) collective-permute-start(bf16[8,4,64,256]{3,2,1,0:T(8,128)(2,1)S(1)} %bitcast.5), channel_id=1, source_target_pairs={{0,8},{8,0},{1,9},{9,1},{2,10},{10,2},{3,11},{11,3},{4,12},{12,4},... | collective-permute-start | bytes 3145736 | tf_op jit(solution)/shard_map/kv_swap/ppermute | solution.py:298
  72.6 19.1 %all-to-all-start.2 = ((bf16[8,512,128]{2,1,0:T(8,128)(2,1)}), bf16[8,512,128]{2,1,0:T(8,128)(2,1)S(1)}, u32[]{:S(2)}, u32[]{:S(2)}) async-start(bf16[8,512,128]{2,1,0:T(8,128)(2,1)} %get-tuple-element.24), calls=%async_computation.2 | async-start | bytes 2097152 | tf_op jit(solution)/shard_map/x_gather/all_to_all | solution.py:333
  76.9 6.0 %collective-permute-start.3 = (bf16[512,128]{1,0:T(8,128)(2,1)S(1)}, bf16[512,128]{1,0:T(8,128)(2,1)S(1)}, u32[]{:S(2)}, u32[]{:S(2)}) collective-permute-start(bf16[512,128]{1,0:T(8,128)(2,1)S(1)} %get-tuple-element.22.x0_ref), channel_id=1, source_target_pairs={{0,16},{16,0},{1,17},{17,1},{2,18},{18,2},{3,19},{19,3},{4,20},{20... | collective-permute-start | bytes 393224 | tf_op jit(solution)/shard_map/x_swap/ppermute | solution.py:330
  82.9 4.9 %collective-permute-start.4 = (bf16[2,512,128]{2,1,0:T(8,128)(2,1)S(1)}, bf16[2,512,128]{2,1,0:T(8,128)(2,1)S(1)}, u32[]{:S(2)}, u32[]{:S(2)}) collective-permute-start(bf16[2,512,128]{2,1,0:T(8,128)(2,1)S(1)} %pad_maximum_fusion.1), channel_id=1, source_target_pairs={{0,8},{8,0},{1,9},{9,1},{2,10},{10,2},{3,11},{11,3},{4,12},{12,4},... | collective-permute-start | bytes 786440 | tf_op jit(solution)/shard_map/x_swap/ppermute | solution.py:331

commit v8 on v7

--- a/solution.py
+++ b/solution.py
@@ -259,7 +259,7 @@
         part = dot(r_ref[at], x_ref[0], ATB)[0 : HD // 2] + dot(r_ref[at], x_ref[1], ATB)[HD // 2 : HD]
         for hh in range(2):
             zh, yh = (i * 2 + hh) // 4, (i * 2 + hh) % 4
-            h_ref[yh * NZ + zh] = part[hh * GRP : (hh + 1) * GRP].astype(jnp.bfloat16)
+            h_ref[yh * NZ + zh] = (part[hh * GRP : (hh + 1) * GRP] * (2.0 / TOKENS)).astype(jnp.bfloat16)
 
 
 def call(kernel, name, outs, args, scratch=(), flops=0, moved=0, space=pltpu.VMEM, limit=40, kinds=()):
@@ -342,7 +342,7 @@
     (gram,) = call(gram_kernel, "gram", [(NZ * NY // 2, GRP, 2 * HD)], (x_all, x))
     with jax.named_scope("h_exchange"):
         h_parts = lax.all_to_all(gram, PAIRS, 0, 0)
-    hessian = jnp.sum(h_parts.astype(jnp.float32), axis=0) * (2.0 / TOKENS)
+    hessian = jnp.sum(h_parts.astype(jnp.float32), axis=0)
     return attn_out, hessian
 
 

time: 123 us -> 123 us (level)
  no operation moved by 1% of the time
where the time goes in v8:
time: 123 us; the launch traced here: 121 us
  blocking collectives  41.7 us (34%)
  starting transfers between devices  36.9 us (30%)
  waiting for transfers between devices  30.6 us (25%)
  Pallas kernels  9.96 us (8%)
  other arithmetic  1.61 us (1%)
    all_to_all x1, blocking collectives, local(): h_parts = lax.all_to_all(gram, PAIRS, 0, 0)  28.4 us
    ppermute x1, waiting for transfers between devices, local(): far = lax.ppermute(near, 'b', swap)  18.9 us
    all_to_all x1, starting transfers between devices, local(): kv_own = lax.all_to_all(own, CHIPS, 0, 0)  16.5 us
    all_to_all x1, blocking collectives, local(): parts = lax.all_to_all(part, ('xl',) + QUAD, 0, 0)  13.3 us
    pallas_call x6, Pallas kernels, call(): pl.pallas_call(kernel, out_shape=[jax.ShapeDtypeStruct(s, kind) for s, ki...  9.96 us
    all_to_all x1, starting transfers between devices, local(): x_all = lax.all_to_all(x_many, ('zl', 'g', 'xl'), 0, 0)  4.28 us
    ppermute x1, starting transfers between devices, local(): x2 = lax.ppermute(jnp.stack([x0, x1]), 'c', swap)  3.79 us
    ppermute x1, starting transfers between devices, local(): kv_oth = lax.ppermute(kv_own, 'c', swap)  3.7 us
  transfers between devices with their start and end apart: 7, of which 6 were waited for; matrix products, arithmetic and copies ran while one was open for 1% of the time, Pallas kernels for 2%

profile of v8, /device:TPU:1, one launch (start us, length us, event | category | flops | bytes accessed | tf_op | source)
XLA Modules:
  0.0 121.5 jit_solution(4114008121301900403)
XLA Ops:
  0.6 1.9 %prep.1 = bf16[32,64,256]{2,1,0:T(8,128)(2,1)} custom-call(bf16[256,256]{1,0:T(8,128)(2,1)} %k_ref.1, bf16[256,256]{1,0:T(8,128)(2,1)} %v_ref.1), custom_call_target="tpu_custom_call" | custom-call | bytes 1048576 | tf_op jit(solution)/shard_map/prep/pallas_call | solution.py:266
  2.6 16.5 %all-to-all-start = ((bf16[32,64,256]{2,1,0:T(8,128)(2,1)}), bf16[32,64,256]{2,1,0:T(8,128)(2,1)S(1)}, u32[]{:S(2)}, u32[]{:S(2)}) async-start(bf16[32,64,256]{2,1,0:T(8,128)(2,1)} %prep.1), calls=%async_computation | async-start | bytes 2097152 | tf_op jit(solution)/shard_map/kv_gather/all_to_all | solution.py:294
  19.1 3.1 %collective-permute-start = (bf16[256,256]{1,0:T(8,128)(2,1)}, bf16[256,256]{1,0:T(8,128)(2,1)S(1)}, u32[]{:S(2)}, u32[]{:S(2)}) collective-permute-start(bf16[256,256]{1,0:T(8,128)(2,1)} %param.3), channel_id=1, source_target_pairs={{0,2},{2,0},{1,3},{3,1},{4,6},{6,4},{5,7},{7,5},{8,10},{10,8},{9,1... | collective-permute-start | bytes 393224 | tf_op jit(solution)/shard_map/q_gather/ppermute | solution.py:291
  22.2 3.1 %collective-permute-done = bf16[256,256]{1,0:T(8,128)(2,1)S(1)} collective-permute-done((bf16[256,256]{1,0:T(8,128)(2,1)}, bf16[256,256]{1,0:T(8,128)(2,1)S(1)}, u32[]{:S(2)}, u32[]{:S(2)}) %collective-permute-start) | collective-permute-done | bytes 131104 | tf_op jit(solution)/shard_map/q_gather/ppermute | solution.py:291
  25.3 0.9 pad_maximum_fusion.near_ref
  26.2 3.1 %collective-permute-start.1 = (bf16[2,256,256]{2,1,0:T(8,128)(2,1)S(1)}, bf16[2,256,256]{2,1,0:T(8,128)(2,1)S(1)}, u32[]{:S(2)}, u32[]{:S(2)}) collective-permute-start(bf16[2,256,256]{2,1,0:T(8,128)(2,1)S(1)} %pad_maximum_fusion.near_ref), channel_id=1, source_target_pairs={{0,16},{16,0},{1,17},{17,1},{2,18},{18,2},{3,19},{19,3},{4,20},{20... | collective-permute-start | bytes 786440 | tf_op jit(solution)/shard_map/q_gather/ppermute | solution.py:292
  29.4 18.9 %collective-permute-done.1.far_ref = bf16[2,256,256]{2,1,0:T(8,128)(2,1)S(1)} collective-permute-done((bf16[2,256,256]{2,1,0:T(8,128)(2,1)S(1)}, bf16[2,256,256]{2,1,0:T(8,128)(2,1)S(1)}, u32[]{:S(2)}, u32[]{:S(2)}) %collective-permute-start.1) | collective-permute-done | bytes 262176 | tf_op jit(solution)/shard_map/q_gather/ppermute | solution.py:292
  48.3 0.0 all-to-all-done
  48.3 3.7 %collective-permute-start.2 = (bf16[8,4,64,256]{3,2,1,0:T(8,128)(2,1)S(1)}, bf16[8,4,64,256]{3,2,1,0:T(8,128)(2,1)S(1)}, u32[]{:S(2)}, u32[]{:S(2)}) collective-permute-start(bf16[8,4,64,256]{3,2,1,0:T(8,128)(2,1)S(1)} %bitcast.5), channel_id=1, source_target_pairs={{0,8},{8,0},{1,9},{9,1},{2,10},{10,2},{3,11},{11,3},{4,12},{12,4},... | collective-permute-start | bytes 3145736 | tf_op jit(solution)/shard_map/kv_swap/ppermute | solution.py:298
  52.0 1.0 attend_begin.1
  53.0 1.3 %collective-permute-done.2.oth_ref = bf16[8,4,64,256]{3,2,1,0:T(8,128)(2,1)S(1)} collective-permute-done((bf16[8,4,64,256]{3,2,1,0:T(8,128)(2,1)S(1)}, bf16[8,4,64,256]{3,2,1,0:T(8,128)(2,1)S(1)}, u32[]{:S(2)}, u32[]{:S(2)}) %collective-permute-start.2) | collective-permute-done | bytes 1048608 | tf_op jit(solution)/shard_map/kv_swap/ppermute | solution.py:298
  54.3 3.6 %attend.1 = bf16[8,288,128]{2,1,0:T(8,128)(2,1)S(1)} custom-call(bf16[2,1024,128]{2,1,0:T(8,128)(2,1)S(1)} %get-tuple-element.16.q_ref, bf16[4,128,512]{2,1,0:T(8,128)(2,1)S(1)} %get-tuple-element.17.k0_ref, bf16[4,512,256]{2,1,0:T(8,128)(2,1)S(1)} %get-tuple-element.18.ve0_ref, f32[4,1024,512]{2,1,0:T(8,128)S(1)} %get-tuple-element.19.s0_ref, ...), custom_call_target="tpu_custom_call" | custom-call | flops 8589934592 | tf_op jit(solution)/shard_map/attend/pallas_call | solution.py:266
  57.9 13.3 %all_to_all.20.r_ref = bf16[8,288,128]{2,1,0:T(8,128)(2,1)S(1)} all-to-all(bf16[8,288,128]{2,1,0:T(8,128)(2,1)S(1)} %attend.1), channel_id=1, replica_groups=mesh['zh'=4,'yh'=4,'b'=2,'c'=2,'g'=2,'xl'=2,'zl'=2] {'xl','b','c'}, dimensions={0} | all-to-all | bytes 1179648 | tf_op jit(solution)/shard_map/part_exchange/all_to_all | solution.py:327
  71.2 1.4 %combine.1 = (bf16[512,128]{1,0:T(8,128)(2,1)S(1)}, bf16[8,512,128]{2,1,0:T(8,128)(2,1)}) custom-call(bf16[8,288,128]{2,1,0:T(8,128)(2,1)S(1)} %all_to_all.20.r_ref), custom_call_target="tpu_custom_call" | custom-call | tf_op jit(solution)/shard_map/combine/pallas_call | solution.py:266
  72.6 4.3 %all-to-all-start.2 = ((bf16[8,512,128]{2,1,0:T(8,128)(2,1)}), bf16[8,512,128]{2,1,0:T(8,128)(2,1)S(1)}, u32[]{:S(2)}, u32[]{:S(2)}) async-start(bf16[8,512,128]{2,1,0:T(8,128)(2,1)} %get-tuple-element.24), calls=%async_computation.2 | async-start | bytes 2097152 | tf_op jit(solution)/shard_map/x_gather/all_to_all | solution.py:333
  76.9 2.4 %collective-permute-start.3 = (bf16[512,128]{1,0:T(8,128)(2,1)S(1)}, bf16[512,128]{1,0:T(8,128)(2,1)S(1)}, u32[]{:S(2)}, u32[]{:S(2)}) collective-permute-start(bf16[512,128]{1,0:T(8,128)(2,1)S(1)} %get-tuple-element.22.x0_ref), channel_id=1, source_target_pairs={{0,16},{16,0},{1,17},{17,1},{2,18},{18,2},{3,19},{19,3},{4,20},{20... | collective-permute-start | bytes 393224 | tf_op jit(solution)/shard_map/x_swap/ppermute | solution.py:330
  79.2 3.6 %collective-permute-done.3.x1_ref = bf16[512,128]{1,0:T(8,128)(2,1)S(1)} collective-permute-done((bf16[512,128]{1,0:T(8,128)(2,1)S(1)}, bf16[512,128]{1,0:T(8,128)(2,1)S(1)}, u32[]{:S(2)}, u32[]{:S(2)}) %collective-permute-start.3) | collective-permute-done | bytes 131104 | tf_op jit(solution)/shard_map/x_swap/ppermute | solution.py:330
  82.9 3.8 %collective-permute-start.4 = (bf16[2,512,128]{2,1,0:T(8,128)(2,1)S(1)}, bf16[2,512,128]{2,1,0:T(8,128)(2,1)S(1)}, u32[]{:S(2)}, u32[]{:S(2)}) collective-permute-start(bf16[2,512,128]{2,1,0:T(8,128)(2,1)S(1)} %pad_maximum_fusion.1), channel_id=1, source_target_pairs={{0,8},{8,0},{1,9},{9,1},{2,10},{10,2},{3,11},{11,3},{4,12},{12,4},... | collective-permute-start | bytes 786440 | tf_op jit(solution)/shard_map/x_swap/ppermute | solution.py:331
  86.7 1.1 collective-permute-done.4.x2_ref
  87.8 1.4 %assemble.1 = (bf16[2,512,256]{2,1,0:T(8,128)(2,1)S(1)}, bf16[256,256]{1,0:T(8,128)(2,1)}) custom-call(bf16[512,128]{1,0:T(8,128)(2,1)S(1)} %get-tuple-element.22.x0_ref, bf16[512,128]{1,0:T(8,128)(2,1)S(1)} %collective-permute-done.3.x1_ref, bf16[2,512,128]{2,1,0:T(8,128)(2,1)S(1)} %collective-permute-done.4.x2_ref), custom_call_target="tpu_custom_call" | custom-call | flops 268435456 | bytes 1048576 | tf_op jit(solution)/shard_map/assemble/pallas_call | solution.py:266
  89.2 2.4 %all-to-all-done.2.r_ref = bf16[8,512,128]{2,1,0:T(8,128)(2,1)S(1)} async-done(((bf16[8,512,128]{2,1,0:T(8,128)(2,1)}), bf16[8,512,128]{2,1,0:T(8,128)(2,1)S(1)}, u32[]{:S(2)}, u32[]{:S(2)}) %all-to-all-start.2) | async-done | bytes 1048608 | tf_op jit(solution)/shard_map/x_gather/all_to_all | solution.py:333
  91.6 0.8 gram.1
  92.4 28.4 %all_to_all.21 = bf16[16,32,256]{2,1,0:T(8,128)(2,1)S(1)} all-to-all(bf16[16,32,256]{2,1,0:T(8,128)(2,1)S(1)} %gram.1), channel_id=1, replica_groups=mesh['zh'=4,'yh'=4,'b'=2,'c'=2,'g'=2,'xl'=2,'zl'=2] {'yh','zh'}, dimensions={0} | all-to-all | bytes 524288 | tf_op jit(solution)/shard_map/h_exchange/all_to_all | solution.py:344
  120.8 0.7 convert_reduce_fusion
  (1 shorter events, 0.0 us)
Async XLA Ops:
  2.6 45.8 %all-to-all-start = ((bf16[32,64,256]{2,1,0:T(8,128)(2,1)}), bf16[32,64,256]{2,1,0:T(8,128)(2,1)S(1)}, u32[]{:S(2)}, u32[]{:S(2)}) async-start(bf16[32,64,256]{2,1,0:T(8,128)(2,1)} %prep.1), calls=%async_computation | async-start | bytes 2097152 | tf_op jit(solution)/shard_map/kv_gather/all_to_all | solution.py:294
  19.1 6.2 %collective-permute-start = (bf16[256,256]{1,0:T(8,128)(2,1)}, bf16[256,256]{1,0:T(8,128)(2,1)S(1)}, u32[]{:S(2)}, u32[]{:S(2)}) collective-permute-start(bf16[256,256]{1,0:T(8,128)(2,1)} %param.3), channel_id=1, source_target_pairs={{0,2},{2,0},{1,3},{3,1},{4,6},{6,4},{5,7},{7,5},{8,10},{10,8},{9,1... | collective-permute-start | bytes 393224 | tf_op jit(solution)/shard_map/q_gather/ppermute | solution.py:291
  26.2 22.1 %collective-permute-start.1 = (bf16[2,256,256]{2,1,0:T(8,128)(2,1)S(1)}, bf16[2,256,256]{2,1,0:T(8,128)(2,1)S(1)}, u32[]{:S(2)}, u32[]{:S(2)}) collective-permute-start(bf16[2,256,256]{2,1,0:T(8,128)(2,1)S(1)} %pad_maximum_fusion.near_ref), channel_id=1, source_target_pairs={{0,16},{16,0},{1,17},{17,1},{2,18},{18,2},{3,19},{19,3},{4,20},{20... | collective-permute-start | bytes 786440 | tf_op jit(solution)/shard_map/q_gather/ppermute | solution.py:292
  48.3 6.0 %collective-permute-start.2 = (bf16[8,4,64,256]{3,2,1,0:T(8,128)(2,1)S(1)}, bf16[8,4,64,256]{3,2,1,0:T(8,128)(2,1)S(1)}, u32[]{:S(2)}, u32[]{:S(2)}) collective-permute-start(bf16[8,4,64,256]{3,2,1,0:T(8,128)(2,1)S(1)} %bitcast.5), channel_id=1, source_target_pairs={{0,8},{8,0},{1,9},{9,1},{2,10},{10,2},{3,11},{11,3},{4,12},{12,4},... | collective-permute-start | bytes 3145736 | tf_op jit(solution)/shard_map/kv_swap/ppermute | solution.py:298
  72.6 19.1 %all-to-all-start.2 = ((bf16[8,512,128]{2,1,0:T(8,128)(2,1)}), bf16[8,512,128]{2,1,0:T(8,128)(2,1)S(1)}, u32[]{:S(2)}, u32[]{:S(2)}) async-start(bf16[8,512,128]{2,1,0:T(8,128)(2,1)} %get-tuple-element.24), calls=%async_computation.2 | async-start | bytes 2097152 | tf_op jit(solution)/shard_map/x_gather/all_to_all | solution.py:333
  76.9 6.0 %collective-permute-start.3 = (bf16[512,128]{1,0:T(8,128)(2,1)S(1)}, bf16[512,128]{1,0:T(8,128)(2,1)S(1)}, u32[]{:S(2)}, u32[]{:S(2)}) collective-permute-start(bf16[512,128]{1,0:T(8,128)(2,1)S(1)} %get-tuple-element.22.x0_ref), channel_id=1, source_target_pairs={{0,16},{16,0},{1,17},{17,1},{2,18},{18,2},{3,19},{19,3},{4,20},{20... | collective-permute-start | bytes 393224 | tf_op jit(solution)/shard_map/x_swap/ppermute | solution.py:330
  82.9 4.9 %collective-permute-start.4 = (bf16[2,512,128]{2,1,0:T(8,128)(2,1)S(1)}, bf16[2,512,128]{2,1,0:T(8,128)(2,1)S(1)}, u32[]{:S(2)}, u32[]{:S(2)}) collective-permute-start(bf16[2,512,128]{2,1,0:T(8,128)(2,1)S(1)} %pad_maximum_fusion.1), channel_id=1, source_target_pairs={{0,8},{8,0},{1,9},{9,1},{2,10},{10,2},{3,11},{11,3},{4,12},{12,4},... | collective-permute-start | bytes 786440 | tf_op jit(solution)/shard_map/x_swap/ppermute | solution.py:331

commit v9 on v8

--- a/solution.py
+++ b/solution.py
@@ -151,8 +151,9 @@
             body(zt, False, new, old, top)
             return 0
 
-        lax.fori_loop(0, zh, step, 0)
-        body(zh, True, new, old, top)
+        lax.fori_loop(0, zh + (new is None), step, 0)
+        if new is not None:
+            body(zh, True, new, old, top)
 
     def tops():
         return jnp.maximum(jnp.max(mx_s[...], axis=1, keepdims=True), FLOOR) * SCALE

time: 123 us -> 123 us (level)
  no operation moved by 1% of the time
where the time goes in v9:
time: 123 us; the launch traced here: 122 us
  blocking collectives  41.7 us (34%)
  starting transfers between devices  36.9 us (30%)
  waiting for transfers between devices  30.6 us (25%)
  Pallas kernels  10.4 us (8%)
  other arithmetic  1.61 us (1%)
    all_to_all x1, blocking collectives, local(): h_parts = lax.all_to_all(gram, PAIRS, 0, 0)  28.4 us
    ppermute x1, waiting for transfers between devices, local(): far = lax.ppermute(near, 'b', swap)  18.9 us
    all_to_all x1, starting transfers between devices, local(): kv_own = lax.all_to_all(own, CHIPS, 0, 0)  16.5 us
    all_to_all x1, blocking collectives, local(): parts = lax.all_to_all(part, ('xl',) + QUAD, 0, 0)  13.3 us
    pallas_call x6, Pallas kernels, call(): pl.pallas_call(kernel, out_shape=[jax.ShapeDtypeStruct(s, kind) for s, ki...  10.4 us
    all_to_all x1, starting transfers between devices, local(): x_all = lax.all_to_all(x_many, ('zl', 'g', 'xl'), 0, 0)  4.28 us
    ppermute x1, starting transfers between devices, local(): x2 = lax.ppermute(jnp.stack([x0, x1]), 'c', swap)  3.79 us
    ppermute x1, starting transfers between devices, local(): kv_oth = lax.ppermute(kv_own, 'c', swap)  3.7 us
  transfers between devices with their start and end apart: 7, of which 6 were waited for; matrix products, arithmetic and copies ran while one was open for 1% of the time, Pallas kernels for 2%

profile of v9, /device:TPU:1, one launch (start us, length us, event | category | flops | bytes accessed | tf_op | source)
XLA Modules:
  0.0 121.9 jit_solution(2133778268443552828)
XLA Ops:
  0.6 1.9 %prep.1 = bf16[32,64,256]{2,1,0:T(8,128)(2,1)} custom-call(bf16[256,256]{1,0:T(8,128)(2,1)} %k_ref.1, bf16[256,256]{1,0:T(8,128)(2,1)} %v_ref.1), custom_call_target="tpu_custom_call" | custom-call | bytes 1048576 | tf_op jit(solution)/shard_map/prep/pallas_call | solution.py:267
  2.6 16.5 %all-to-all-start = ((bf16[32,64,256]{2,1,0:T(8,128)(2,1)}), bf16[32,64,256]{2,1,0:T(8,128)(2,1)S(1)}, u32[]{:S(2)}, u32[]{:S(2)}) async-start(bf16[32,64,256]{2,1,0:T(8,128)(2,1)} %prep.1), calls=%async_computation | async-start | bytes 2097152 | tf_op jit(solution)/shard_map/kv_gather/all_to_all | solution.py:295
  19.1 3.1 %collective-permute-start = (bf16[256,256]{1,0:T(8,128)(2,1)}, bf16[256,256]{1,0:T(8,128)(2,1)S(1)}, u32[]{:S(2)}, u32[]{:S(2)}) collective-permute-start(bf16[256,256]{1,0:T(8,128)(2,1)} %param.3), channel_id=1, source_target_pairs={{0,2},{2,0},{1,3},{3,1},{4,6},{6,4},{5,7},{7,5},{8,10},{10,8},{9,1... | collective-permute-start | bytes 393224 | tf_op jit(solution)/shard_map/q_gather/ppermute | solution.py:292
  22.2 3.1 %collective-permute-done = bf16[256,256]{1,0:T(8,128)(2,1)S(1)} collective-permute-done((bf16[256,256]{1,0:T(8,128)(2,1)}, bf16[256,256]{1,0:T(8,128)(2,1)S(1)}, u32[]{:S(2)}, u32[]{:S(2)}) %collective-permute-start) | collective-permute-done | bytes 131104 | tf_op jit(solution)/shard_map/q_gather/ppermute | solution.py:292
  25.3 0.9 pad_maximum_fusion.near_ref
  26.2 3.1 %collective-permute-start.1 = (bf16[2,256,256]{2,1,0:T(8,128)(2,1)S(1)}, bf16[2,256,256]{2,1,0:T(8,128)(2,1)S(1)}, u32[]{:S(2)}, u32[]{:S(2)}) collective-permute-start(bf16[2,256,256]{2,1,0:T(8,128)(2,1)S(1)} %pad_maximum_fusion.near_ref), channel_id=1, source_target_pairs={{0,16},{16,0},{1,17},{17,1},{2,18},{18,2},{3,19},{19,3},{4,20},{20... | collective-permute-start | bytes 786440 | tf_op jit(solution)/shard_map/q_gather/ppermute | solution.py:293
  29.4 18.9 %collective-permute-done.1.far_ref = bf16[2,256,256]{2,1,0:T(8,128)(2,1)S(1)} collective-permute-done((bf16[2,256,256]{2,1,0:T(8,128)(2,1)S(1)}, bf16[2,256,256]{2,1,0:T(8,128)(2,1)S(1)}, u32[]{:S(2)}, u32[]{:S(2)}) %collective-permute-start.1) | collective-permute-done | bytes 262176 | tf_op jit(solution)/shard_map/q_gather/ppermute | solution.py:293
  48.3 0.0 all-to-all-done
  48.3 3.7 %collective-permute-start.2 = (bf16[8,4,64,256]{3,2,1,0:T(8,128)(2,1)S(1)}, bf16[8,4,64,256]{3,2,1,0:T(8,128)(2,1)S(1)}, u32[]{:S(2)}, u32[]{:S(2)}) collective-permute-start(bf16[8,4,64,256]{3,2,1,0:T(8,128)(2,1)S(1)} %bitcast.5), channel_id=1, source_target_pairs={{0,8},{8,0},{1,9},{9,1},{2,10},{10,2},{3,11},{11,3},{4,12},{12,4},... | collective-permute-start | bytes 3145736 | tf_op jit(solution)/shard_map/kv_swap/ppermute | solution.py:299
  52.0 1.0 attend_begin.1
  53.0 1.3 %collective-permute-done.2.oth_ref = bf16[8,4,64,256]{3,2,1,0:T(8,128)(2,1)S(1)} collective-permute-done((bf16[8,4,64,256]{3,2,1,0:T(8,128)(2,1)S(1)}, bf16[8,4,64,256]{3,2,1,0:T(8,128)(2,1)S(1)}, u32[]{:S(2)}, u32[]{:S(2)}) %collective-permute-start.2) | collective-permute-done | bytes 1048608 | tf_op jit(solution)/shard_map/kv_swap/ppermute | solution.py:299
  54.3 4.0 %attend.1 = bf16[8,288,128]{2,1,0:T(8,128)(2,1)S(1)} custom-call(bf16[2,1024,128]{2,1,0:T(8,128)(2,1)S(1)} %get-tuple-element.16.q_ref, bf16[4,128,512]{2,1,0:T(8,128)(2,1)S(1)} %get-tuple-element.17.k0_ref, bf16[4,512,256]{2,1,0:T(8,128)(2,1)S(1)} %get-tuple-element.18.ve0_ref, f32[4,1024,512]{2,1,0:T(8,128)S(1)} %get-tuple-element.19.s0_ref, ...), custom_call_target="tpu_custom_call" | custom-call | flops 8589934592 | tf_op jit(solution)/shard_map/attend/pallas_call | solution.py:267
  58.3 13.3 %all_to_all.20.r_ref = bf16[8,288,128]{2,1,0:T(8,128)(2,1)S(1)} all-to-all(bf16[8,288,128]{2,1,0:T(8,128)(2,1)S(1)} %attend.1), channel_id=1, replica_groups=mesh['zh'=4,'yh'=4,'b'=2,'c'=2,'g'=2,'xl'=2,'zl'=2] {'xl','b','c'}, dimensions={0} | all-to-all | bytes 1179648 | tf_op jit(solution)/shard_map/part_exchange/all_to_all | solution.py:328
  71.6 1.4 %combine.1 = (bf16[512,128]{1,0:T(8,128)(2,1)S(1)}, bf16[8,512,128]{2,1,0:T(8,128)(2,1)}) custom-call(bf16[8,288,128]{2,1,0:T(8,128)(2,1)S(1)} %all_to_all.20.r_ref), custom_call_target="tpu_custom_call" | custom-call | tf_op jit(solution)/shard_map/combine/pallas_call | solution.py:267
  73.0 4.3 %all-to-all-start.2 = ((bf16[8,512,128]{2,1,0:T(8,128)(2,1)}), bf16[8,512,128]{2,1,0:T(8,128)(2,1)S(1)}, u32[]{:S(2)}, u32[]{:S(2)}) async-start(bf16[8,512,128]{2,1,0:T(8,128)(2,1)} %get-tuple-element.24), calls=%async_computation.2 | async-start | bytes 2097152 | tf_op jit(solution)/shard_map/x_gather/all_to_all | solution.py:334
  77.3 2.4 %collective-permute-start.3 = (bf16[512,128]{1,0:T(8,128)(2,1)S(1)}, bf16[512,128]{1,0:T(8,128)(2,1)S(1)}, u32[]{:S(2)}, u32[]{:S(2)}) collective-permute-start(bf16[512,128]{1,0:T(8,128)(2,1)S(1)} %get-tuple-element.22.x0_ref), channel_id=1, source_target_pairs={{0,16},{16,0},{1,17},{17,1},{2,18},{18,2},{3,19},{19,3},{4,20},{20... | collective-permute-start | bytes 393224 | tf_op jit(solution)/shard_map/x_swap/ppermute | solution.py:331
  79.6 3.6 %collective-permute-done.3.x1_ref = bf16[512,128]{1,0:T(8,128)(2,1)S(1)} collective-permute-done((bf16[512,128]{1,0:T(8,128)(2,1)S(1)}, bf16[512,128]{1,0:T(8,128)(2,1)S(1)}, u32[]{:S(2)}, u32[]{:S(2)}) %collective-permute-start.3) | collective-permute-done | bytes 131104 | tf_op jit(solution)/shard_map/x_swap/ppermute | solution.py:331
  83.3 3.8 %collective-permute-start.4 = (bf16[2,512,128]{2,1,0:T(8,128)(2,1)S(1)}, bf16[2,512,128]{2,1,0:T(8,128)(2,1)S(1)}, u32[]{:S(2)}, u32[]{:S(2)}) collective-permute-start(bf16[2,512,128]{2,1,0:T(8,128)(2,1)S(1)} %pad_maximum_fusion.1), channel_id=1, source_target_pairs={{0,8},{8,0},{1,9},{9,1},{2,10},{10,2},{3,11},{11,3},{4,12},{12,4},... | collective-permute-start | bytes 786440 | tf_op jit(solution)/shard_map/x_swap/ppermute | solution.py:332
  87.1 1.1 collective-permute-done.4.x2_ref
  88.2 1.4 %assemble.1 = (bf16[2,512,256]{2,1,0:T(8,128)(2,1)S(1)}, bf16[256,256]{1,0:T(8,128)(2,1)}) custom-call(bf16[512,128]{1,0:T(8,128)(2,1)S(1)} %get-tuple-element.22.x0_ref, bf16[512,128]{1,0:T(8,128)(2,1)S(1)} %collective-permute-done.3.x1_ref, bf16[2,512,128]{2,1,0:T(8,128)(2,1)S(1)} %collective-permute-done.4.x2_ref), custom_call_target="tpu_custom_call" | custom-call | flops 268435456 | bytes 1048576 | tf_op jit(solution)/shard_map/assemble/pallas_call | solution.py:267
  89.6 2.4 %all-to-all-done.2.r_ref = bf16[8,512,128]{2,1,0:T(8,128)(2,1)S(1)} async-done(((bf16[8,512,128]{2,1,0:T(8,128)(2,1)}), bf16[8,512,128]{2,1,0:T(8,128)(2,1)S(1)}, u32[]{:S(2)}, u32[]{:S(2)}) %all-to-all-start.2) | async-done | bytes 1048608 | tf_op jit(solution)/shard_map/x_gather/all_to_all | solution.py:334
  92.0 0.8 gram.1
  92.8 28.4 %all_to_all.21 = bf16[16,32,256]{2,1,0:T(8,128)(2,1)S(1)} all-to-all(bf16[16,32,256]{2,1,0:T(8,128)(2,1)S(1)} %gram.1), channel_id=1, replica_groups=mesh['zh'=4,'yh'=4,'b'=2,'c'=2,'g'=2,'xl'=2,'zl'=2] {'yh','zh'}, dimensions={0} | all-to-all | bytes 524288 | tf_op jit(solution)/shard_map/h_exchange/all_to_all | solution.py:345
  121.2 0.7 convert_reduce_fusion
  (1 shorter events, 0.0 us)
Async XLA Ops:
  2.6 45.8 %all-to-all-start = ((bf16[32,64,256]{2,1,0:T(8,128)(2,1)}), bf16[32,64,256]{2,1,0:T(8,128)(2,1)S(1)}, u32[]{:S(2)}, u32[]{:S(2)}) async-start(bf16[32,64,256]{2,1,0:T(8,128)(2,1)} %prep.1), calls=%async_computation | async-start | bytes 2097152 | tf_op jit(solution)/shard_map/kv_gather/all_to_all | solution.py:295
  19.1 6.2 %collective-permute-start = (bf16[256,256]{1,0:T(8,128)(2,1)}, bf16[256,256]{1,0:T(8,128)(2,1)S(1)}, u32[]{:S(2)}, u32[]{:S(2)}) collective-permute-start(bf16[256,256]{1,0:T(8,128)(2,1)} %param.3), channel_id=1, source_target_pairs={{0,2},{2,0},{1,3},{3,1},{4,6},{6,4},{5,7},{7,5},{8,10},{10,8},{9,1... | collective-permute-start | bytes 393224 | tf_op jit(solution)/shard_map/q_gather/ppermute | solution.py:292
  26.2 22.1 %collective-permute-start.1 = (bf16[2,256,256]{2,1,0:T(8,128)(2,1)S(1)}, bf16[2,256,256]{2,1,0:T(8,128)(2,1)S(1)}, u32[]{:S(2)}, u32[]{:S(2)}) collective-permute-start(bf16[2,256,256]{2,1,0:T(8,128)(2,1)S(1)} %pad_maximum_fusion.near_ref), channel_id=1, source_target_pairs={{0,16},{16,0},{1,17},{17,1},{2,18},{18,2},{3,19},{19,3},{4,20},{20... | collective-permute-start | bytes 786440 | tf_op jit(solution)/shard_map/q_gather/ppermute | solution.py:293
  48.3 6.0 %collective-permute-start.2 = (bf16[8,4,64,256]{3,2,1,0:T(8,128)(2,1)S(1)}, bf16[8,4,64,256]{3,2,1,0:T(8,128)(2,1)S(1)}, u32[]{:S(2)}, u32[]{:S(2)}) collective-permute-start(bf16[8,4,64,256]{3,2,1,0:T(8,128)(2,1)S(1)} %bitcast.5), channel_id=1, source_target_pairs={{0,8},{8,0},{1,9},{9,1},{2,10},{10,2},{3,11},{11,3},{4,12},{12,4},... | collective-permute-start | bytes 3145736 | tf_op jit(solution)/shard_map/kv_swap/ppermute | solution.py:299
  73.0 19.1 %all-to-all-start.2 = ((bf16[8,512,128]{2,1,0:T(8,128)(2,1)}), bf16[8,512,128]{2,1,0:T(8,128)(2,1)S(1)}, u32[]{:S(2)}, u32[]{:S(2)}) async-start(bf16[8,512,128]{2,1,0:T(8,128)(2,1)} %get-tuple-element.24), calls=%async_computation.2 | async-start | bytes 2097152 | tf_op jit(solution)/shard_map/x_gather/all_to_all | solution.py:334
  77.3 6.0 %collective-permute-start.3 = (bf16[512,128]{1,0:T(8,128)(2,1)S(1)}, bf16[512,128]{1,0:T(8,128)(2,1)S(1)}, u32[]{:S(2)}, u32[]{:S(2)}) collective-permute-start(bf16[512,128]{1,0:T(8,128)(2,1)S(1)} %get-tuple-element.22.x0_ref), channel_id=1, source_target_pairs={{0,16},{16,0},{1,17},{17,1},{2,18},{18,2},{3,19},{19,3},{4,20},{20... | collective-permute-start | bytes 393224 | tf_op jit(solution)/shard_map/x_swap/ppermute | solution.py:331
  83.3 4.9 %collective-permute-start.4 = (bf16[2,512,128]{2,1,0:T(8,128)(2,1)S(1)}, bf16[2,512,128]{2,1,0:T(8,128)(2,1)S(1)}, u32[]{:S(2)}, u32[]{:S(2)}) collective-permute-start(bf16[2,512,128]{2,1,0:T(8,128)(2,1)S(1)} %pad_maximum_fusion.1), channel_id=1, source_target_pairs={{0,8},{8,0},{1,9},{9,1},{2,10},{10,2},{3,11},{11,3},{4,12},{12,4},... | collective-permute-start | bytes 786440 | tf_op jit(solution)/shard_map/x_swap/ppermute | solution.py:332
